TPU v7x, 768 devices: a whole 4x8x12 slice. The times are simulated.
768 devices in a mesh: grid: 96 (over y, z), mem: 8 (over x, core).
Axes of the slice: x: 4, y: 8, z: 12, core: 2. Of those that a mesh axis runs over, the one named last changes fastest.
Arguments:
- background_fields: float32 [64, 12288, 128], P('mem', 'grid'), may hold values from -12 to 12
- wind_courant: float32 [12288, 128], P('grid'), may hold values from -0.4 to 0.4
- spreading_number: float32 [12288, 128], P('grid'), may hold values from 0.05 to 0.2
- obs_col: int32 [36864], P('grid'), may hold values from 0 to 127
- obs_lev: int32 [36864], P('grid'), may hold values from 0 to 127
- obs_value: float32 [36864], P('grid'), may hold values from -48 to 48
- obs_var: float32 [36864], P('grid'), may hold values from 64 to 256
Outputs:
- analysis: bfloat16 [64, 12288, 128], P('mem', 'grid')
All inputs are finite; a program needn't handle non-finite values.
Results may differ from a plain program's by a relative error of at most 0.0055.
Values may be sent and summed in bfloat16 or wider, within the bound.
No kernel may reach another device: no remote copies, remote signals or barrier semaphores. Data moves between devices by JAX's collectives and lax.ppermute only.
A program may use at most 32 MiB of HBM per device.

v0:
```python
import jax
import jax.numpy as jnp
from jax import lax
from jax.sharding import PartitionSpec as P

NSITER = 8


def extended(block, sides, width):
    for axis, dim in sides:
        count = lax.axis_size(axis)
        forward = [(i, i + 1) for i in range(count - 1)]
        backward = [(target, source) for source, target in forward]
        low = lax.ppermute(
            lax.slice_in_dim(block, block.shape[dim] - width, None, axis=dim), axis, forward
        )
        high = lax.ppermute(lax.slice_in_dim(block, 0, width, axis=dim), axis, backward)
        block = jnp.concatenate([low, block, high], axis=dim)
    return block


def inverse_root(amat, count, iters):
    scale = jnp.sqrt(jnp.sum(amat * amat))
    eye = jnp.eye(count, dtype=jnp.float32)
    yit = amat / scale
    zit = eye
    for step in range(iters):
        tmat = (3.0 * eye - jnp.dot(zit, yit, precision=lax.Precision.HIGHEST)) / 2.0
        yit = jnp.dot(yit, tmat, precision=lax.Precision.HIGHEST)
        zit = jnp.dot(tmat, zit, precision=lax.Precision.HIGHEST)
    return zit / jnp.sqrt(scale)


def build_mix(gram, proj, count, iters):
    amat = (count - 1.0) * jnp.eye(count, dtype=jnp.float32) + gram
    root = inverse_root(amat, count, iters)
    inner = jnp.dot(root, proj, precision=lax.Precision.HIGHEST)
    wmean = jnp.dot(root, inner, precision=lax.Precision.HIGHEST)
    tfm = wmean[:, None] + jnp.sqrt(count - 1.0) * root
    blend_factors = 1.0 / count + tfm - jnp.mean(tfm, axis=0, keepdims=True)
    return blend_factors.astype(jnp.bfloat16)


def adjacent_increment(field, padded_border, wind_courant, spreading_number):
    left_box = padded_border[:, :-2, :]
    right_box = padded_border[:, 2:, :]
    vertical = jnp.pad(field, ((0, 0), (0, 0), (1, 1)))
    below_layer = vertical[:, :, :-2]
    above_layer = vertical[:, :, 2:]
    return (
        field
        + wind_courant * (left_box - right_box) / 2.0
        + spreading_number * (right_box + left_box + above_layer + below_layer - 4.0 * field)
    )


def member_path(
    background_fields, wind_courant, spreading_number, obs_col, obs_lev, obs_value, obs_var
):
    participant_piece, pillar_amount, layer_amount = background_fields.shape
    members = participant_piece * lax.axis_size("mem")
    padded_border = extended(background_fields, (("grid", 1),), 1)
    advance_model = adjacent_increment(
        background_fields, padded_border, wind_courant, spreading_number
    )
    flattened_position = obs_col * layer_amount + obs_lev
    local_predicted_observations = jnp.take(
        advance_model.reshape(participant_piece, pillar_amount * layer_amount),
        flattened_position,
        axis=1,
    )
    expected_readings = lax.all_gather(local_predicted_observations, "mem", axis=0, tiled=True)
    ybar = jnp.mean(expected_readings, axis=0)
    anomaly = expected_readings - ybar
    innov = obs_value - ybar
    weighted = anomaly / obs_var
    gram_part = jnp.dot(weighted, anomaly.T, precision=lax.Precision.HIGHEST)
    proj_part = jnp.dot(weighted, innov, precision=lax.Precision.HIGHEST)
    gram, proj = lax.psum((gram_part, proj_part), "grid")
    blend_factors = build_mix(gram, proj, members, NSITER)
    return (advance_model.astype(jnp.bfloat16), blend_factors)


def on_device(
    background_fields, wind_courant, spreading_number, obs_col, obs_lev, obs_value, obs_var
):
    participant_piece, pillar_amount, layer_amount = background_fields.shape
    participant_fields, blend_factors = member_path(
        background_fields, wind_courant, spreading_number, obs_col, obs_lev, obs_value, obs_var
    )
    first_own = lax.axis_index("mem") * participant_piece
    piece = lax.all_gather(participant_fields, "mem", axis=0, tiled=True)
    rows = piece.shape[0]
    block = lax.dynamic_slice(blend_factors, (0, first_own), (rows, participant_piece))
    flat_piece = piece.reshape(rows, pillar_amount * layer_amount)
    total = jnp.dot(block.T, flat_piece, preferred_element_type=jnp.float32)
    analysis = total.astype(jnp.bfloat16).reshape(participant_piece, pillar_amount, layer_amount)
    return analysis


def solution(mesh):
    in_specs = (
        P("mem", "grid", None),
        P("grid", None),
        P("grid", None),
        P("grid"),
        P("grid"),
        P("grid"),
        P("grid"),
    )
    out_specs = P("mem", "grid", None)
    return jax.shard_map(
        on_device, mesh=mesh, in_specs=in_specs, out_specs=out_specs, check_vma=False
    )
```

profile of v0, /device:TPU:1, one launch (start us, length us, event | category | flops | bytes accessed | tf_op | source)
XLA Modules:
  0.0 507.8 jit_solution(2684081028645218687)
XLA Ops:
  6.5 0.8 fusion.45
  7.3 4.8 collective-permute-start
  12.1 1.3 collective-permute-start.1
  13.4 0.7 compare_and_fusion
  14.2 3.0 collective-permute-done.1
  17.1 3.2 fusion.43
  20.3 4.6 copy.10
  24.9 4.5 gather_fusion
  29.6 20.1 %all_gather.6 = f32[64,384]{1,0:T(8,128)S(1)} all-gather(f32[8,384]{1,0:T(8,128)S(1)} %copy.11), channel_id=1, replica_groups=mesh['grid'=96,'mem'=8] {'mem'}, dimensions={0}, use_global_device_ids=true | all-gather | bytes 110592 | tf_op jit(solution)/shard_map/all_gather | solution.py:72
  49.7 0.2 fusion.18
  50.0 0.2 convolution_bitcast_fusion.2
  50.2 335.5 %all-reduce.1 = (f32[64,64]{1,0:T(8,128)S(1)}, f32[64]{0:T(128)S(1)}) all-reduce(f32[64,64]{1,0:T(8,128)S(1)} %fusion.18, f32[64]{0:T(128)S(1)} %convolution_bitcast_fusion.2), channel_id=1, replica_groups=mesh['grid'=96,'mem'=8] {'grid'}, use_global_device_ids=true, to_apply=%region_1.2 | all-reduce | flops 4160 | bytes 33280 | tf_op jit(solution)/shard_map/psum | solution.py:79
  385.7 0.6 multiply_reduce_fusion
  387.2 0.2 fusion.26
  387.5 0.2 fusion.11
  387.7 0.2 fusion.47
  388.0 0.2 fusion.10
  388.2 0.2 fusion.49
  388.4 0.2 fusion.48
  388.6 0.2 fusion.9
  388.8 0.2 fusion.51
  388.9 0.2 fusion.50
  389.1 0.2 fusion.8
  389.6 0.2 fusion.7
  389.8 0.2 fusion.55
  390.0 0.2 fusion.54
  390.1 0.2 fusion.6
  390.6 0.2 fusion.5
  390.8 0.2 convolution_divide_fusion
  391.6 105.8 %all-gather.2.cloned.1.call-done = bf16[64,128,128]{2,1,0:T(8,128)(2,1)} async-done(((bf16[8,128,128]{2,1,0:T(8,128)(2,1)}), bf16[64,128,128]{2,1,0:T(8,128)(2,1)}) %all-gather.2.cloned.1.call-update) | async-done | bytes 2097168 | tf_op jit(solution)/shard_map/all_gather | solution.py:92
  497.4 2.8 fusion.2
  500.2 0.7 copy.12
  (25 shorter events, 1.9 us)
Async XLA Ops:
  6.5 490.9 %all-gather.2.cloned.1.call-start = ((), (), s32[]{:S(2)}) async-start(), calls=%async_computation | async-start | bytes 2359296 | tf_op jit(solution)/shard_map/all_gather | solution.py:92
  7.3 6.8 %collective-permute-start = (f32[8,1,128]{2,1,0:T(1,128)S(1)}, f32[8,1,128]{2,1,0:T(1,128)S(1)}, u32[]{:S(2)}, u32[]{:S(2)}) collective-permute-start(f32[8,1,128]{2,1,0:T(1,128)S(1)} %get-tuple-element.13), channel_id=1, source_target_pairs={{0,8},{8,16},{16,24},{24,32},{32,40},{40,48},{48,56},{56,64},{64,7... | collective-permute-start | bytes 12296 | tf_op jit(solution)/shard_map/ppermute | solution.py:14
  12.1 5.0 collective-permute-start.1
  20.3 29.4 %copy-start = (f32[384]{0:T(512)S(1)}, f32[384]{0:T(512)}, u32[]{:S(2)}) copy-start(f32[384]{0:T(512)} %param.12) | copy-start | bytes 4612
  20.3 29.4 %copy-start.1 = (f32[384]{0:T(512)S(1)}, f32[384]{0:T(512)}, u32[]{:S(2)}) copy-start(f32[384]{0:T(512)} %param.13) | copy-start | bytes 4612
Sparse Core Ops, SparseCore 0:
  388.7 108.6 all-gather.1
where the time goes:
time: 508 us
  blocking collectives  356 us (70%)
  waiting for transfers between devices  109 us (21%)
  between operations  14.4 us (3%)
  local copies, waits for them, and re-layouts  10.8 us (2%)
  matrix products  7.31 us (1%)
  starting transfers between devices  6.11 us (1%)
    psum x1, blocking collectives, member_path(): gram, proj = lax.psum((gram_part, proj_part), 'grid')  336 us
    all_gather x1, waiting for transfers between devices, on_device(): piece = lax.all_gather(participant_fields, 'mem', axis=0, tiled=True)  106 us
    all_gather x1, blocking collectives, member_path(): lax.all_gather(local_predicted_observations, 'mem', axis=0, tiled=True)  20.1 us
  transfers between devices with their start and end apart: 3, of which 2 were waited for; matrix products, arithmetic and copies ran while one was open for 1% of the time, Pallas kernels for 0%

commit v1 on v0

--- a/solution.py
+++ b/solution.py
@@ -1,9 +1,10 @@
 import jax
 import jax.numpy as jnp
 from jax import lax
-from jax.sharding import PartitionSpec as P
+from jax.sharding import Mesh, PartitionSpec as P
 
 NSITER = 8
+ROWS = 8
 
 
 def extended(block, sides, width):
@@ -54,12 +55,32 @@
     )
 
 
+def exchange_sum(part, axis):
+    copies = jnp.broadcast_to(part[None], (lax.axis_size(axis),) + part.shape)
+    return jnp.sum(lax.all_to_all(copies, axis, 0, 0), axis=0)
+
+
+def summed(gram_part, proj_part, axis):
+    half = gram_part.shape[0] // 2
+    packed = jnp.concatenate(
+        [
+            jnp.concatenate([gram_part[:half], gram_part[half:]], axis=1),
+            jnp.pad(proj_part[None], ((0, 7), (0, half * 2))),
+        ],
+        axis=0,
+    )
+    for part in ("row", "col"):
+        packed = exchange_sum(packed, part)
+    gram = jnp.concatenate([packed[:half, : 2 * half], packed[:half, 2 * half :]], axis=0)
+    return gram, packed[half, : 2 * half]
+
+
 def member_path(
     background_fields, wind_courant, spreading_number, obs_col, obs_lev, obs_value, obs_var
 ):
     participant_piece, pillar_amount, layer_amount = background_fields.shape
     members = participant_piece * lax.axis_size("mem")
-    padded_border = extended(background_fields, (("grid", 1),), 1)
+    padded_border = extended(background_fields, ((("row", "col"), 1),), 1)
     advance_model = adjacent_increment(
         background_fields, padded_border, wind_courant, spreading_number
     )
@@ -69,14 +90,18 @@
         flattened_position,
         axis=1,
     )
-    expected_readings = lax.all_gather(local_predicted_observations, "mem", axis=0, tiled=True)
+    count = lax.axis_size("mem")
+    copies = jnp.broadcast_to(
+        local_predicted_observations[None], (count,) + local_predicted_observations.shape
+    )
+    expected_readings = lax.all_to_all(copies, "mem", 0, 0).reshape(members, -1)
     ybar = jnp.mean(expected_readings, axis=0)
     anomaly = expected_readings - ybar
     innov = obs_value - ybar
     weighted = anomaly / obs_var
     gram_part = jnp.dot(weighted, anomaly.T, precision=lax.Precision.HIGHEST)
     proj_part = jnp.dot(weighted, innov, precision=lax.Precision.HIGHEST)
-    gram, proj = lax.psum((gram_part, proj_part), "grid")
+    gram, proj = summed(gram_part, proj_part, "grid")
     blend_factors = build_mix(gram, proj, members, NSITER)
     return (advance_model.astype(jnp.bfloat16), blend_factors)
 
@@ -99,16 +124,19 @@
 
 
 def solution(mesh):
+    grid, mem = mesh.shape["grid"], mesh.shape["mem"]
+    fine = Mesh(mesh.devices.reshape(ROWS, grid // ROWS, mem), ("row", "col", "mem"))
+    blocks = ("row", "col")
     in_specs = (
-        P("mem", "grid", None),
-        P("grid", None),
-        P("grid", None),
-        P("grid"),
-        P("grid"),
-        P("grid"),
-        P("grid"),
+        P("mem", blocks, None),
+        P(blocks, None),
+        P(blocks, None),
+        P(blocks),
+        P(blocks),
+        P(blocks),
+        P(blocks),
     )
-    out_specs = P("mem", "grid", None)
+    out_specs = P("mem", blocks, None)
     return jax.shard_map(
-        on_device, mesh=mesh, in_specs=in_specs, out_specs=out_specs, check_vma=False
+        on_device, mesh=fine, in_specs=in_specs, out_specs=out_specs, check_vma=False
     )

time: 508 us -> 116 us (0.23)
  blocking collectives: 356 us -> 33.3 us
  waiting for transfers between devices: 109 us -> 30.4 us
  starting transfers between devices: 6.11 us -> 13.3 us
    psum x1 -> x0, blocking collectives: 336 us -> none  [member_path(): gram, proj = lax.psum((gram_part, proj_part), 'grid')]
    all_gather x1, waiting for transfers between devices: 106 us -> 15.8 us  [on_device(): piece = lax.all_gather(participant_fields, 'mem', axis=0, tiled=True)]
    all_to_all x0 -> x2, blocking collectives: none -> 33.3 us  [the longest x1 18.4 us: exchange_sum(): return jnp.sum(lax.all_to_all(copies, axis, 0, 0), axis=0)]
    all_gather x1 -> x0, blocking collectives: 20.1 us -> none  [member_path(): lax.all_gather(local_predicted_observations, 'mem', axis=0, tiled=True)]
    all_to_all x0 -> x1, waiting for transfers between devices: none -> 10.9 us  [exchange_sum(): return jnp.sum(lax.all_to_all(copies, axis, 0, 0), axis=0)]
    all_to_all x0 -> x1, starting transfers between devices: none -> 7.15 us  [exchange_sum(): return jnp.sum(lax.all_to_all(copies, axis, 0, 0), axis=0)]
  transfers between devices with their start and end apart: 3 -> 4, of which waited for: 2 -> 3; matrix products, arithmetic and copies ran while one was open for 1% -> 5% of each run, Pallas kernels for 0% -> 0%
where the time goes in v1:
time: 116 us; the launch traced here: 115 us
  blocking collectives  33.3 us (29%)
  waiting for transfers between devices  30.4 us (26%)
  between operations  14.4 us (12%)
  starting transfers between devices  13.3 us (11%)
  local copies, waits for them, and re-layouts  11.6 us (10%)
  matrix products  7.32 us (6%)
  other arithmetic  4.95 us (4%)
    all_to_all x1, blocking collectives, exchange_sum(): return jnp.sum(lax.all_to_all(copies, axis, 0, 0), axis=0)  18.4 us
    all_gather x1, waiting for transfers between devices, on_device(): piece = lax.all_gather(participant_fields, 'mem', axis=0, tiled=True)  15.8 us
    all_to_all x1, blocking collectives, member_path(): expected_readings = lax.all_to_all(copies, 'mem', 0, 0).reshape(members, -1)  14.9 us
    all_to_all x1, waiting for transfers between devices, exchange_sum(): return jnp.sum(lax.all_to_all(copies, axis, 0, 0), axis=0)  10.9 us
    all_to_all x1, starting transfers between devices, exchange_sum(): return jnp.sum(lax.all_to_all(copies, axis, 0, 0), axis=0)  7.15 us
    ppermute x1, starting transfers between devices, extended(): lax.ppermute(lax.slice_in_dim(block, block.shape[dim] - width, None, axis...  4.81 us
    add x1, local copies, waits for them, and re-layouts, adjacent_increment(): field + wind_courant * (left_box - right_box) / 2.0  4.57 us
    gather x1, local copies, waits for them, and re-layouts, member_path(): jnp.take(advance_model.reshape(participant_piece, pillar_amount * layer_a...  4.5 us
  transfers between devices with their start and end apart: 4, of which 3 were waited for; matrix products, arithmetic and copies ran while one was open for 5% of the time, Pallas kernels for 0%

profile of v1, /device:TPU:1, one launch (start us, length us, event | category | flops | bytes accessed | tf_op | source)
XLA Modules:
  0.0 115.3 jit_solution(16044305040106654325)
XLA Ops:
  6.5 0.8 fusion.52
  7.3 4.8 %collective-permute-start = (f32[8,1,128]{2,1,0:T(1,128)S(1)}, f32[8,1,128]{2,1,0:T(1,128)S(1)}, u32[]{:S(2)}, u32[]{:S(2)}) collective-permute-start(f32[8,1,128]{2,1,0:T(1,128)S(1)} %get-tuple-element.11), channel_id=1, source_target_pairs={{0,8},{8,16},{16,24},{24,32},{32,40},{40,48},{48,56},{56,64},{64,7... | collective-permute-start | bytes 12296 | tf_op jit(solution)/shard_map/ppermute | solution.py:15
  12.1 1.3 %collective-permute-start.1 = (f32[8,1,128]{2,1,0:T(1,128)S(1)}, f32[8,1,128]{2,1,0:T(1,128)S(1)}, u32[]{:S(2)}, u32[]{:S(2)}) collective-permute-start(f32[8,1,128]{2,1,0:T(1,128)S(1)} %get-tuple-element.12), channel_id=1, source_target_pairs={{8,0},{16,8},{24,16},{32,24},{40,32},{48,40},{56,48},{64,56},{72,6... | collective-permute-start | bytes 12296 | tf_op jit(solution)/shard_map/ppermute | solution.py:18
  13.4 0.7 compare_and_fusion
  14.2 3.0 %collective-permute-done.1 = f32[8,1,128]{2,1,0:T(1,128)S(1)} collective-permute-done((f32[8,1,128]{2,1,0:T(1,128)S(1)}, f32[8,1,128]{2,1,0:T(1,128)S(1)}, u32[]{:S(2)}, u32[]{:S(2)}) %collective-permute-start.1) | collective-permute-done | bytes 4128 | tf_op jit(solution)/shard_map/ppermute | solution.py:18
  17.1 3.2 %fusion.50 = (bf16[8,128,128]{2,1,0:T(8,128)(2,1)}, f32[8,128,128]{2,1,0:T(8,128)S(1)}) fusion(f32[8,128,128]{2,1,0:T(8,128)} %param.7, f32[128,128]{1,0:T(8,128)} %param.9, f32[8,1,128]{2,1,0:T(1,128)S(1)} %collective-permute-done.1, f32[8,1,128]{2,1,0:T(1,128)S(1)} %collective-permute-done, f32[128,128]{1,0:T(8,128)} %param.8), kind=kLoop, calls=%fused_computation.76 | loop fusion | flops 1835008 | bytes 1449984 | tf_op jit(solution)/shard_map/convert_element_type | solution.py:106
  20.3 4.6 %copy.14 = f32[8,128,128]{0,2,1:T(8,128)} copy(f32[8,128,128]{2,1,0:T(8,128)S(1)} %get-tuple-element.10) | data formatting | bytes 1048576 | tf_op jit(solution)/shard_map/add | solution.py:52
  24.9 4.5 %gather_fusion = f32[384,8]{1,0:T(8,128)S(1)} fusion(f32[8,16384]{0,1:T(8,128)} %bitcast.78, s32[1024]{0:T(1024)S(1)} %pad_clamp_fusion), kind=kCustom, calls=%fused_computation | custom fusion | bytes 26112 | tf_op jit(solution)/shard_map/jit(_take)/gather | solution.py:88
  29.6 14.9 %all_to_all.15 = f32[8,8,384]{2,1,0:T(8,128)S(1)} all-to-all(f32[8,8,384]{2,1,0:T(8,128)S(1)} %broadcast_in_dim.23), channel_id=1, replica_groups=mesh['row'=8,'col'=12,'mem'=8] {'mem'}, dimensions={0} | all-to-all | bytes 196608 | tf_op jit(solution)/shard_map/all_to_all | solution.py:97
  44.5 0.2 fusion.19
  44.8 0.2 fusion.24
  45.1 18.4 %all_to_all.16 = f32[8,40,128]{2,1,0:T(8,128)S(1)} all-to-all(f32[8,40,128]{2,1,0:T(8,128)S(1)} %broadcast_in_dim.44), channel_id=1, replica_groups=mesh['row'=8,'col'=12,'mem'=8] {'row'}, dimensions={0} | all-to-all | bytes 327680 | tf_op jit(solution)/shard_map/all_to_all | solution.py:60
  63.6 0.8 broadcast_in_dim.45
  64.4 7.1 %all-to-all-start.2 = ((f32[12,40,128]{2,1,0:T(8,128)}), f32[12,40,128]{2,1,0:T(8,128)S(1)}, u32[]{:S(2)}, u32[]{:S(2)}) async-start(f32[12,40,128]{2,1,0:T(8,128)} %broadcast_in_dim.45), calls=%async_computation.2 | async-start | bytes 491520 | tf_op jit(solution)/shard_map/all_to_all | solution.py:60
  71.6 0.7 all-gather.2.cloned.1.call-update
  72.2 10.9 %all-to-all-done.2 = f32[12,40,128]{2,1,0:T(8,128)S(1)} async-done(((f32[12,40,128]{2,1,0:T(8,128)}), f32[12,40,128]{2,1,0:T(8,128)S(1)}, u32[]{:S(2)}, u32[]{:S(2)}) %all-to-all-start.2) | async-done | bytes 245792 | tf_op jit(solution)/shard_map/all_to_all | solution.py:60
  83.3 0.6 multiply_reduce_fusion
  84.7 0.2 fusion.37
  85.1 0.2 fusion.11
  85.2 0.2 fusion.56
  85.4 0.2 fusion.55
  85.6 0.2 fusion.10
  86.1 0.2 fusion.9
  86.6 0.2 fusion.8
  87.0 0.2 fusion.61
  87.1 0.2 fusion.7
  87.6 0.2 fusion.6
  88.2 0.2 fusion.5
  88.3 0.2 convolution_divide_fusion
  89.1 15.8 %all-gather.2.cloned.1.call-done = bf16[64,128,128]{2,1,0:T(8,128)(2,1)} async-done(((bf16[8,128,128]{2,1,0:T(8,128)(2,1)}), bf16[64,128,128]{2,1,0:T(8,128)(2,1)}) %all-gather.2.cloned.1.call-update) | async-done | bytes 2097168 | tf_op jit(solution)/shard_map/all_gather | solution.py:117
  104.9 2.8 %fusion.2 = bf16[8,128,128]{2,0,1:T(8,128)(2,1)S(1)} fusion(bf16[8,8,128,128]{3,2,1,0:T(8,128)(2,1)} %bitcast.79, f32[64,64]{0,1:T(8,128)S(1)} %get-tuple-element.6, s32[]{:T(128)S(6)} %select_n.18, f32[8]{0:T(128)S(1)} %dynamic-slice), kind=kOutput, calls=%fused_computation.6 | convolution fusion | flops 16909824 | bytes 2363908 | tf_op jit(solution)/shard_map/dot_general | solution.py:121
  107.7 0.7 copy.16
  (35 shorter events, 2.8 us)
Async XLA Ops:
  7.3 6.8 %collective-permute-start = (f32[8,1,128]{2,1,0:T(1,128)S(1)}, f32[8,1,128]{2,1,0:T(1,128)S(1)}, u32[]{:S(2)}, u32[]{:S(2)}) collective-permute-start(f32[8,1,128]{2,1,0:T(1,128)S(1)} %get-tuple-element.11), channel_id=1, source_target_pairs={{0,8},{8,16},{16,24},{24,32},{32,40},{40,48},{48,56},{56,64},{64,7... | collective-permute-start | bytes 12296 | tf_op jit(solution)/shard_map/ppermute | solution.py:15
  12.1 5.0 %collective-permute-start.1 = (f32[8,1,128]{2,1,0:T(1,128)S(1)}, f32[8,1,128]{2,1,0:T(1,128)S(1)}, u32[]{:S(2)}, u32[]{:S(2)}) collective-permute-start(f32[8,1,128]{2,1,0:T(1,128)S(1)} %get-tuple-element.12), channel_id=1, source_target_pairs={{8,0},{16,8},{24,16},{32,24},{40,32},{48,40},{56,48},{64,56},{72,6... | collective-permute-start | bytes 12296 | tf_op jit(solution)/shard_map/ppermute | solution.py:18
  20.3 24.2 %copy-start = (f32[384]{0:T(512)S(1)}, f32[384]{0:T(512)}, u32[]{:S(2)}) copy-start(f32[384]{0:T(512)} %param.12) | copy-start | bytes 4612
  20.3 24.2 %copy-start.1 = (f32[384]{0:T(512)S(1)}, f32[384]{0:T(512)}, u32[]{:S(2)}) copy-start(f32[384]{0:T(512)} %param.13) | copy-start | bytes 4612
  64.4 18.8 %all-to-all-start.2 = ((f32[12,40,128]{2,1,0:T(8,128)}), f32[12,40,128]{2,1,0:T(8,128)S(1)}, u32[]{:S(2)}, u32[]{:S(2)}) async-start(f32[12,40,128]{2,1,0:T(8,128)} %broadcast_in_dim.45), calls=%async_computation.2 | async-start | bytes 491520 | tf_op jit(solution)/shard_map/all_to_all | solution.py:60
  71.5 33.4 %all-gather.2.cloned.1.call-start = ((), (), s32[]{:S(2)}) async-start(), calls=%async_computation.3 | async-start | bytes 2359296 | tf_op jit(solution)/shard_map/all_gather | solution.py:117
Sparse Core Ops, SparseCore 0:
  74.8 30.0 all-gather.1

commit v2 on v1

v2 whole, which is shorter than its diff:
```python
import functools

import jax
import jax.numpy as jnp
from jax import lax
from jax.experimental import pallas as pl
from jax.experimental.pallas import tpu as pltpu
from jax.sharding import Mesh, PartitionSpec as P

NSITER = 8
ROWS = 8
LANES = 128
GROUP = 8
EXACT = lax.Precision.HIGHEST
VMEM = pl.BlockSpec(memory_space=pltpu.VMEM)


def lane_index(rows):
    return lax.broadcasted_iota(jnp.int32, (rows, LANES), 1)


def neighbours(block, axis):
    count = lax.axis_size(axis)
    forward = [(i, i + 1) for i in range(count - 1)]
    backward = [(target, source) for source, target in forward]
    last = block.shape[1] - 1
    low = lax.ppermute(block[:, last:, :], axis, forward)
    high = lax.ppermute(block[:, :1, :], axis, backward)
    return low[:, 0], high[:, 0]


def forecast_kernel(columns, field, low, high, courant, spreading, col, lev, fields, readings, cells):
    members, layers = low.shape
    lane = lax.broadcasted_iota(jnp.int32, (members, layers), 1)

    def column(i):
        return field[pl.ds(i, members, stride=columns), :]

    def advance(i, left, centre, right):
        below = jnp.where(lane == 0, 0.0, pltpu.roll(centre, 1, 1))
        above = jnp.where(lane == layers - 1, 0.0, pltpu.roll(centre, layers - 1, 1))
        wind = courant[pl.ds(i, 1), :]
        spread = spreading[pl.ds(i, 1), :]
        value = (
            centre
            + wind * (left - right) * 0.5
            + spread * (right + left + above + below - 4.0 * centre)
        )
        cells[i * members : (i + 1) * members, :] = value
        fields[:, i * layers : (i + 1) * layers] = value.astype(jnp.bfloat16)

    left, centre = low[...], column(0)
    for i in range(columns):
        right = column(i + 1) if i + 1 < columns else high[...]
        advance(i, left, centre, right)
        left, centre = centre, right

    observations = col.shape[1]
    level = lax.broadcasted_iota(jnp.int32, (layers, observations), 0)
    chosen = jnp.where(level == lev[...], 1.0, 0.0).astype(jnp.bfloat16)
    where_col = jnp.broadcast_to(col[...], (members, observations))
    step = 16
    total = jnp.zeros((members, observations), jnp.float32)
    for base in range(0, columns, step):
        rest = cells[base * members : (base + step) * members, :]
        picked = None
        for _ in range(3):
            part = rest.astype(jnp.bfloat16)
            rest = rest - part.astype(jnp.float32)
            term = jnp.dot(part, chosen, preferred_element_type=jnp.float32)
            picked = term if picked is None else picked + term
        for i in range(step):
            row = picked[i * members : (i + 1) * members, :]
            total = total + jnp.where(where_col == base + i, row, 0.0)
    readings[...] = total


def forecast(field, low, high, courant, spreading, col, lev):
    members, columns, layers = field.shape
    observations = col.shape[0]
    return pl.pallas_call(
        functools.partial(forecast_kernel, columns),
        out_shape=(
            jax.ShapeDtypeStruct((members, columns * layers), jnp.bfloat16),
            jax.ShapeDtypeStruct((members, observations), jnp.float32),
        ),
        in_specs=[VMEM] * 7,
        out_specs=(VMEM, VMEM),
        scratch_shapes=[pltpu.VMEM((members * columns, layers), jnp.float32)],
        compiler_params=pltpu.CompilerParams(vmem_limit_bytes=16 * 2**20),
        name="forecast",
    )(
        field.reshape(members * columns, layers),
        low,
        high,
        courant,
        spreading,
        col.reshape(1, observations),
        lev.reshape(1, observations),
    )


def pack(upper, proj_row):
    lane = lane_index(GROUP)
    row = [upper[GROUP * r : GROUP * (r + 1), :] for r in range(8)]
    roll = lambda r, shift: pltpu.roll(row[r], shift, 1)
    first = jnp.where(lane < 64, row[0], roll(1, 64))
    second = jnp.where(lane < 16, roll(7, 80), row[2])
    second = jnp.where(lane >= 64, roll(3, 48), second)
    second = jnp.where(lane >= 112, roll(6, 64), second)
    third = jnp.where(lane < 32, roll(5, 96), row[4])
    third = jnp.where(lane >= 64, pltpu.roll(proj_row, 64, 1), third)
    return first, second, third


def unpack(first, second, third):
    lane = lane_index(GROUP)
    roll = lambda part, shift: pltpu.roll(part, shift, 1)
    rows = [
        first,
        roll(first, 64),
        second,
        roll(second, 80),
        third,
        roll(third, 32),
        roll(second, 64),
        roll(second, 48),
    ]
    keep = [
        jnp.where((lane >= 16 * (r // 2)) & (lane < 64), part, 0.0) for r, part in enumerate(rows)
    ]
    upper = jnp.concatenate(keep, axis=0)
    return upper, roll(third, 64)[:1, :]


def gram_kernel(members, readings, value, var, copies):
    hx = readings[...]
    ybar = jnp.sum(hx, axis=0, keepdims=True) * (1.0 / members)
    anomaly = hx - ybar
    innov = value[...] - ybar
    weighted = anomaly / var[...]
    pad = jnp.zeros((LANES - members, hx.shape[1]), jnp.float32)
    weighted = jnp.concatenate([weighted, pad], axis=0)
    nt = (((1,), (1,)), ((), ()))
    gram = lax.dot_general(
        anomaly, weighted, nt, precision=EXACT, preferred_element_type=jnp.float32
    )
    rows = jnp.where(
        lax.broadcasted_iota(jnp.int32, (GROUP, hx.shape[1]), 0) == 0,
        jnp.broadcast_to(innov, (GROUP, hx.shape[1])),
        0.0,
    )
    proj = lax.dot_general(
        rows, weighted, nt, precision=EXACT, preferred_element_type=jnp.float32
    )
    for s, part in enumerate(pack(gram, proj)):
        for r in range(copies.shape[0]):
            copies[r, GROUP * s : GROUP * (s + 1), :] = part


def gram_parts(readings, value, var, count):
    members, observations = readings.shape
    return pl.pallas_call(
        functools.partial(gram_kernel, members),
        out_shape=jax.ShapeDtypeStruct((count, 3 * GROUP, LANES), jnp.float32),
        in_specs=[VMEM] * 3,
        out_specs=VMEM,
        name="gram",
    )(readings, value.reshape(1, observations), var.reshape(1, observations))


def sum_kernel(parts, copies):
    total = parts[0]
    for r in range(1, parts.shape[0]):
        total = total + parts[r]
    for r in range(copies.shape[0]):
        copies[r] = total


def sum_copies(parts, count):
    return pl.pallas_call(
        sum_kernel,
        out_shape=jax.ShapeDtypeStruct((count,) + parts.shape[1:], jnp.float32),
        in_specs=[VMEM],
        out_specs=VMEM,
        name="row_sum",
    )(parts)


def analysis_kernel(members, iters, own, parts, fields, out, held, mixed, cells, sem):
    fetch = pltpu.make_async_copy(fields, held, sem)
    fetch.start()

    total = parts[0]
    for r in range(1, parts.shape[0]):
        total = total + parts[r]
    upper, proj = unpack(*[total[GROUP * s : GROUP * (s + 1), :] for s in range(3)])
    square = jnp.concatenate(
        [upper, jnp.zeros((LANES - members, LANES), jnp.float32)], axis=0
    )
    turned = square.T
    row = lax.broadcasted_iota(jnp.int32, (LANES, LANES), 0)
    lane = lane_index(LANES)
    gram = jnp.where(lane // 16 >= row // 16, square, turned)[:members, :members]
    row, lane = row[:members, :members], lane[:members, :members]
    eye = jnp.where(row == lane, 1.0, 0.0)
    proj = proj[:, :members]

    dot = lambda a, b: jnp.dot(a, b, precision=EXACT, preferred_element_type=jnp.float32)
    amat = (members - 1.0) * eye + gram
    scale = jnp.sqrt(jnp.sum(amat * amat, keepdims=True))
    yit = amat / scale
    zit = eye
    for step in range(iters):
        if step == 0:
            tmat = (3.0 * eye - yit) * 0.5
        else:
            tmat = (3.0 * eye - dot(zit, yit)) * 0.5
        if step + 1 < iters:
            yit = dot(yit, tmat)
        zit = tmat if step == 0 else dot(tmat, zit)
    root = zit / jnp.sqrt(scale)
    turned = root.T
    wmean = dot(dot(proj, turned), turned)
    tfm = wmean + jnp.sqrt(jnp.float32(members - 1.0)) * turned
    centre = jnp.sum(tfm, axis=1, keepdims=True) * (1.0 / members)
    mixed[...] = 1.0 / members + tfm - centre

    count, columns, layers = out.shape
    mine = mixed[pl.ds(pl.multiple_of(own[0] * count, count), count), :].astype(jnp.bfloat16)
    fetch.wait()
    step = 16
    for base in range(0, columns, step):
        block = jnp.dot(
            mine,
            held[:, base * layers : (base + step) * layers],
            preferred_element_type=jnp.float32,
        )
        for i in range(step):
            cells[pl.ds(base + i, count, stride=columns), :] = block[
                :, i * layers : (i + 1) * layers
            ]
    out[...] = cells[...].astype(jnp.bfloat16).reshape(out.shape)


def analysis(own, parts, fields, shape):
    members = fields.shape[0]
    count, columns, layers = shape
    return pl.pallas_call(
        functools.partial(analysis_kernel, members, NSITER),
        out_shape=jax.ShapeDtypeStruct(shape, jnp.bfloat16),
        in_specs=[
            pl.BlockSpec(memory_space=pltpu.SMEM),
            VMEM,
            pl.BlockSpec(memory_space=pl.ANY),
        ],
        out_specs=VMEM,
        scratch_shapes=[
            pltpu.VMEM(fields.shape, jnp.bfloat16),
            pltpu.VMEM((members, members), jnp.float32),
            pltpu.VMEM((count * columns, layers), jnp.float32),
            pltpu.SemaphoreType.DMA,
        ],
        compiler_params=pltpu.CompilerParams(vmem_limit_bytes=60 * 2**20),
        name="analysis",
    )(own, parts, fields)


def on_device(
    background_fields, wind_courant, spreading_number, obs_col, obs_lev, obs_value, obs_var
):
    own = background_fields.shape[0]
    low, high = neighbours(background_fields, ("row", "col"))
    fields, hx = forecast(
        background_fields, low, high, wind_courant, spreading_number, obs_col, obs_lev
    )
    everyone = lax.all_gather(fields, "mem", axis=0, tiled=True)
    mems, cols, rows = (lax.axis_size(a) for a in ("mem", "col", "row"))
    copies = jnp.broadcast_to(hx[None], (mems,) + hx.shape)
    readings = lax.all_to_all(copies, "mem", 0, 0).reshape(mems * own, hx.shape[1])
    parts = gram_parts(readings, obs_value, obs_var, rows)
    parts = lax.all_to_all(parts, "row", 0, 0)
    parts = sum_copies(parts, cols)
    parts = lax.all_to_all(parts, "col", 0, 0)
    index = lax.axis_index("mem").astype(jnp.int32).reshape(1)
    return analysis(index, parts, everyone, background_fields.shape)


def solution(mesh):
    grid, mem = mesh.shape["grid"], mesh.shape["mem"]
    fine = Mesh(mesh.devices.reshape(ROWS, grid // ROWS, mem), ("row", "col", "mem"))
    blocks = ("row", "col")
    in_specs = (
        P("mem", blocks, None),
        P(blocks, None),
        P(blocks, None),
        P(blocks),
        P(blocks),
        P(blocks),
        P(blocks),
    )
    out_specs = P("mem", blocks, None)
    return jax.shard_map(
        on_device, mesh=fine, in_specs=in_specs, out_specs=out_specs, check_vma=False
    )
```

time: 116 us -> 92.4 us (0.80)
  the two profiles are of different devices: /device:TPU:1 before, /device:TPU:2 now
where the time goes in v2:
time: 92.4 us; the launch traced here: 91.6 us
  starting transfers between devices  22.4 us (24%)
  blocking collectives  19 us (21%)
  waiting for transfers between devices  17 us (18%)
  between operations  13.4 us (15%)
  Pallas kernels  10.5 us (11%)
  local copies, waits for them, and re-layouts  9.28 us (10%)
    all_to_all x1, blocking collectives, on_device(): parts = lax.all_to_all(parts, 'row', 0, 0)  19 us
    all_to_all x1, waiting for transfers between devices, on_device(): parts = lax.all_to_all(parts, 'col', 0, 0)  11.9 us
    all_to_all x1, starting transfers between devices, on_device(): lax.all_to_all(copies, 'mem', 0, 0).reshape(mems * own, hx.shape[1])  9.47 us
    all_to_all x1, starting transfers between devices, on_device(): parts = lax.all_to_all(parts, 'col', 0, 0)  7.36 us
    pallas_call x1, Pallas kernels, analysis(): pl.pallas_call(functools.partial(analysis_kernel, members, NSITER), out_s...  5.57 us
    ppermute x1, starting transfers between devices, neighbours(): low = lax.ppermute(block[:, last:, :], axis, forward)  4.26 us
    unnamed x10, local copies, waits for them, and re-layouts  4 us
    ppermute x1, waiting for transfers between devices, neighbours(): high = lax.ppermute(block[:, :1, :], axis, backward)  3.19 us
  transfers between devices with their start and end apart: 5, of which 3 were waited for; matrix products, arithmetic and copies ran while one was open for 5% of the time, Pallas kernels for 4%

profile of v2, /device:TPU:2, one launch (start us, length us, event | category | flops | bytes accessed | tf_op | source)
XLA Modules:
  0.0 91.6 jit_solution(7142480415189138287)
XLA Ops:
  6.5 0.0 all-gather.2.cloned.1.call-start
  6.5 0.8 fusion
  7.3 4.3 %collective-permute-start = (f32[8,1,128]{2,0,1:T(8,128)S(1)}, f32[8,1,128]{2,0,1:T(8,128)S(1)}, u32[]{:S(2)}, u32[]{:S(2)}) collective-permute-start(f32[8,1,128]{2,0,1:T(8,128)S(1)} %bitcast.12), channel_id=1, source_target_pairs={{0,8},{8,16},{16,24},{24,32},{32,40},{40,48},{48,56},{56,64},{64,7... | collective-permute-start | bytes 12296 | tf_op jit(solution)/shard_map/ppermute | solution.py:27
  11.6 1.3 %collective-permute-start.1 = (f32[8,1,128]{2,0,1:T(8,128)S(1)}, f32[8,1,128]{2,0,1:T(8,128)S(1)}, u32[]{:S(2)}, u32[]{:S(2)}) collective-permute-start(f32[8,1,128]{2,0,1:T(8,128)S(1)} %bitcast.11), channel_id=1, source_target_pairs={{8,0},{16,8},{24,16},{32,24},{40,32},{48,40},{56,48},{64,56},{72,6... | collective-permute-start | bytes 12296 | tf_op jit(solution)/shard_map/ppermute | solution.py:28
  12.9 0.7 reshape.24.col
  13.6 0.7 reshape.25.lev
  14.3 0.0 collective-permute-done
  14.3 3.2 %collective-permute-done.1 = f32[8,1,128]{2,0,1:T(8,128)S(1)} collective-permute-done((f32[8,1,128]{2,0,1:T(8,128)S(1)}, f32[8,1,128]{2,0,1:T(8,128)S(1)}, u32[]{:S(2)}, u32[]{:S(2)}) %collective-permute-start.1) | collective-permute-done | bytes 4128 | tf_op jit(solution)/shard_map/ppermute | solution.py:28
  17.5 0.0 copy-start
  17.5 1.0 %copy-done = f32[8,128,128]{2,1,0:T(8,128)S(1)} copy-done((f32[8,128,128]{2,1,0:T(8,128)S(1)}, f32[8,128,128]{2,1,0:T(8,128)}, u32[]{:S(2)}) %copy-start) | copy-done | bytes 524312
  18.5 0.0 copy-start.1
  18.5 0.8 copy-done.1
  19.3 0.0 copy-start.2
  19.3 0.8 copy-done.2
  20.2 1.4 %forecast.1 = (bf16[8,16384]{1,0:T(8,128)(2,1)}, f32[8,384]{1,0:T(8,128)S(1)}) custom-call(f32[1024,128]{1,0:T(8,128)S(1)} %bitcast.7, f32[8,128]{1,0:T(8,128)S(1)} %bitcast.8, f32[8,128]{1,0:T(8,128)S(1)} %bitcast.9, f32[128,128]{1,0:T(8,128)S(1)} %copy-done.1, f32[128,128]{1,0:T(8,128)S(1)} %copy-done.2, s32[1,384]{1,0:T(1,128)S(1)} %reshape.24.col, ...), custom_call_target="tpu_custom_call" | custom-call | tf_op jit(solution)/shard_map/forecast/pallas_call | solution.py:81
  21.6 0.0 all-gather.2.cloned.1.call-update
  21.6 0.6 broadcast_in_dim.2
  22.3 9.5 %all-to-all-start = ((f32[8,8,384]{2,1,0:T(8,128)}), f32[8,8,384]{2,1,0:T(8,128)S(1)}, u32[]{:S(2)}, u32[]{:S(2)}) async-start(f32[8,8,384]{2,1,0:T(8,128)} %broadcast_in_dim.2), calls=%async_computation | async-start | bytes 196608 | tf_op jit(solution)/shard_map/all_to_all | solution.py:280
  31.7 1.2 %reshape.27.value = f32[1,384]{1,0:T(1,128)} reshape(f32[384]{0:T(512)} %param.12) | data formatting | bytes 3072 | tf_op jit(solution)/shard_map/reshape | solution.py:169
  33.0 1.3 %reshape.28.var = f32[1,384]{1,0:T(1,128)} reshape(f32[384]{0:T(512)} %param.13) | data formatting | bytes 3072 | tf_op jit(solution)/shard_map/reshape | solution.py:169
  34.2 1.9 %all-to-all-done = f32[8,8,384]{2,1,0:T(8,128)S(1)} async-done(((f32[8,8,384]{2,1,0:T(8,128)}), f32[8,8,384]{2,1,0:T(8,128)S(1)}, u32[]{:S(2)}, u32[]{:S(2)}) %all-to-all-start) | async-done | bytes 98336 | tf_op jit(solution)/shard_map/all_to_all | solution.py:280
  36.1 0.0 copy-start.4
  36.1 0.6 copy-done.4
  36.7 2.0 %gram.1 = f32[8,24,128]{2,1,0:T(8,128)} custom-call(f32[64,384]{1,0:T(8,128)} %bitcast.10, f32[1,384]{1,0:T(1,128)} %reshape.27.value, f32[1,384]{1,0:T(1,128)} %reshape.28.var), custom_call_target="tpu_custom_call" | custom-call | tf_op jit(solution)/shard_map/gram/pallas_call | solution.py:163
  38.7 19.0 %all_to_all.15.parts = f32[8,24,128]{2,1,0:T(8,128)} all-to-all(f32[8,24,128]{2,1,0:T(8,128)} %gram.1), channel_id=1, replica_groups=mesh['row'=8,'col'=12,'mem'=8] {'row'}, dimensions={0} | all-to-all | bytes 196608 | tf_op jit(solution)/shard_map/all_to_all | solution.py:282
  57.7 1.6 %row_sum.1 = f32[12,24,128]{2,1,0:T(8,128)} custom-call(f32[8,24,128]{2,1,0:T(8,128)} %all_to_all.15.parts), custom_call_target="tpu_custom_call" | custom-call | tf_op jit(solution)/shard_map/row_sum/pallas_call | solution.py:181
  59.3 7.4 %all-to-all-start.2 = ((f32[12,24,128]{2,1,0:T(8,128)}), f32[12,24,128]{2,1,0:T(8,128)S(1)}, u32[]{:S(2)}, u32[]{:S(2)}) async-start(f32[12,24,128]{2,1,0:T(8,128)} %row_sum.1), calls=%async_computation.2 | async-start | bytes 294912 | tf_op jit(solution)/shard_map/all_to_all | solution.py:284
  66.6 11.9 %all-to-all-done.2.parts = f32[12,24,128]{2,1,0:T(8,128)S(1)} async-done(((f32[12,24,128]{2,1,0:T(8,128)}), f32[12,24,128]{2,1,0:T(8,128)S(1)}, u32[]{:S(2)}, u32[]{:S(2)}) %all-to-all-start.2) | async-done | bytes 147488 | tf_op jit(solution)/shard_map/all_to_all | solution.py:284
  78.5 0.0 copy-start.3
  78.5 0.0 all-gather.2.cloned.1.call-done.fields
  78.5 0.7 copy-done.3
  79.2 5.6 %analysis.1 = bf16[8,128,128]{2,1,0:T(8,128)(2,1)} custom-call(s32[1]{0:T(128)} %bitcast.own, f32[12,24,128]{2,1,0:T(8,128)} %copy-done.3, bf16[64,16384]{1,0:T(8,128)(2,1)} %all-gather.2.cloned.1.call-done.fields), custom_call_target="tpu_custom_call" | custom-call | tf_op jit(solution)/shard_map/analysis/pallas_call | solution.py:249
Async XLA Ops:
  6.5 72.0 %all-gather.2.cloned.1.call-start = ((), (), s32[]{:S(2)}) async-start(), calls=%async_computation.3 | async-start | bytes 2359296 | tf_op jit(solution)/shard_map/all_gather | solution.py:277
  7.3 6.9 %collective-permute-start = (f32[8,1,128]{2,0,1:T(8,128)S(1)}, f32[8,1,128]{2,0,1:T(8,128)S(1)}, u32[]{:S(2)}, u32[]{:S(2)}) collective-permute-start(f32[8,1,128]{2,0,1:T(8,128)S(1)} %bitcast.12), channel_id=1, source_target_pairs={{0,8},{8,16},{16,24},{24,32},{32,40},{40,48},{48,56},{56,64},{64,7... | collective-permute-start | bytes 12296 | tf_op jit(solution)/shard_map/ppermute | solution.py:27
  11.6 5.9 %collective-permute-start.1 = (f32[8,1,128]{2,0,1:T(8,128)S(1)}, f32[8,1,128]{2,0,1:T(8,128)S(1)}, u32[]{:S(2)}, u32[]{:S(2)}) collective-permute-start(f32[8,1,128]{2,0,1:T(8,128)S(1)} %bitcast.11), channel_id=1, source_target_pairs={{8,0},{16,8},{24,16},{32,24},{40,32},{48,40},{56,48},{64,56},{72,6... | collective-permute-start | bytes 12296 | tf_op jit(solution)/shard_map/ppermute | solution.py:28
  17.5 1.0 %copy-start = (f32[8,128,128]{2,1,0:T(8,128)S(1)}, f32[8,128,128]{2,1,0:T(8,128)}, u32[]{:S(2)}) copy-start(f32[8,128,128]{2,1,0:T(8,128)} %param.7) | copy-start | bytes 1572868
  18.5 0.8 copy-start.1
  19.3 0.8 copy-start.2
  22.3 13.8 %all-to-all-start = ((f32[8,8,384]{2,1,0:T(8,128)}), f32[8,8,384]{2,1,0:T(8,128)S(1)}, u32[]{:S(2)}, u32[]{:S(2)}) async-start(f32[8,8,384]{2,1,0:T(8,128)} %broadcast_in_dim.2), calls=%async_computation | async-start | bytes 196608 | tf_op jit(solution)/shard_map/all_to_all | solution.py:280
  36.1 0.6 copy-start.4
  59.3 19.3 %all-to-all-start.2 = ((f32[12,24,128]{2,1,0:T(8,128)}), f32[12,24,128]{2,1,0:T(8,128)S(1)}, u32[]{:S(2)}, u32[]{:S(2)}) async-start(f32[12,24,128]{2,1,0:T(8,128)} %row_sum.1), calls=%async_computation.2 | async-start | bytes 294912 | tf_op jit(solution)/shard_map/all_to_all | solution.py:284
  78.5 0.7 copy-start.3
Sparse Core Ops, SparseCore 0:
  21.7 39.3 all-gather.1

commit v3 on v2

v3 whole, which is shorter than its diff:
```python
import functools

import jax
import jax.numpy as jnp
from jax import lax
from jax.experimental import pallas as pl
from jax.experimental.pallas import tpu as pltpu
from jax.sharding import Mesh, PartitionSpec as P

NSITER = 8
ROWS = 8
LANES = 128
GROUP = 8
ORDER = (0, 2, 6, 4, 1, 3, 7, 5)
EXACT = lax.Precision.HIGHEST
VMEM = pl.BlockSpec(memory_space=pltpu.VMEM)
SMALL = pltpu.CompilerParams(vmem_limit_bytes=16 * 2**20)


def lane_index(rows):
    return lax.broadcasted_iota(jnp.int32, (rows, LANES), 1)


def neighbours(block, axis):
    count = lax.axis_size(axis)
    forward = [(i, i + 1) for i in range(count - 1)]
    backward = [(target, source) for source, target in forward]
    last = block.shape[1] - 1
    low = lax.ppermute(block[:, last:, :], axis, forward)
    high = lax.ppermute(block[:, :1, :], axis, backward)
    return low[:, 0], high[:, 0]


def chosen_levels(lev, layers):
    level = lax.broadcasted_iota(jnp.int32, (layers, lev.shape[0]), 0)
    return jnp.where(level == lev[...].reshape(1, -1), 1.0, 0.0).astype(jnp.bfloat16)


def at_levels(values, chosen):
    rest, picked = values, None
    for _ in range(3):
        part = rest.astype(jnp.bfloat16)
        rest = rest - part.astype(jnp.float32)
        term = jnp.dot(part, chosen, preferred_element_type=jnp.float32)
        picked = term if picked is None else picked + term
    return picked


def inner_kernel(
    columns, field_hbm, courant_hbm, spreading_hbm, col, lev, fields, readings, edges,
    field, courant, spreading, cells, sems,
):
    sources = ((field_hbm, field), (courant_hbm, courant), (spreading_hbm, spreading))
    fetches = [pltpu.make_async_copy(s, d, sems.at[i]) for i, (s, d) in enumerate(sources)]
    for fetch in fetches:
        fetch.start()
    members = fields.shape[0]
    layers = field.shape[1]
    observations = col.shape[0]
    lane = lax.broadcasted_iota(jnp.int32, (members, layers), 1)
    chosen = chosen_levels(lev, layers)
    where_col = jnp.broadcast_to(col[...].reshape(1, -1), (members, observations))
    for fetch in fetches:
        fetch.wait()

    def column(i):
        if i < 0 or i >= columns:
            return jnp.zeros((members, layers), jnp.float32)
        return field[pl.ds(i, members, stride=columns), :]

    left, centre = column(-1), column(0)
    for i in range(columns):
        right = column(i + 1)
        below = jnp.where(lane == 0, 0.0, pltpu.roll(centre, 1, 1))
        above = jnp.where(lane == layers - 1, 0.0, pltpu.roll(centre, layers - 1, 1))
        value = (
            centre
            + courant[pl.ds(i, 1), :] * (left - right) * 0.5
            + spreading[pl.ds(i, 1), :] * (right + left + above + below - 4.0 * centre)
        )
        cells[i * members : (i + 1) * members, :] = value
        fields[:, i * layers : (i + 1) * layers] = value.astype(jnp.bfloat16)
        left, centre = centre, right

    last = columns - 1
    spread = lambda row: jnp.broadcast_to(row, (members, layers))
    edges[0] = cells[:members, :]
    edges[1] = cells[last * members :, :]
    edges[2] = spread(spreading[:1, :] + courant[:1, :] * 0.5)
    edges[3] = spread(spreading[last:, :] - courant[last:, :] * 0.5)

    step = 16
    total = jnp.zeros((members, observations), jnp.float32)
    for base in range(0, columns, step):
        picked = at_levels(cells[base * members : (base + step) * members, :], chosen)
        for i in range(step):
            if 0 < base + i < last:
                row = picked[i * members : (i + 1) * members, :]
                total = total + jnp.where(where_col == base + i, row, 0.0)
    readings[...] = total


def inner_forecast(field, courant, spreading, col, lev):
    members, columns, layers = field.shape
    observations = col.shape[0]
    anywhere = pl.BlockSpec(memory_space=pltpu.HBM)
    return pl.pallas_call(
        functools.partial(inner_kernel, columns),
        out_shape=(
            jax.ShapeDtypeStruct((members, columns * layers), jnp.bfloat16),
            jax.ShapeDtypeStruct((members, observations), jnp.float32),
            jax.ShapeDtypeStruct((4, members, layers), jnp.float32),
        ),
        in_specs=[anywhere] * 3 + [VMEM] * 2,
        out_specs=(VMEM, VMEM, VMEM),
        scratch_shapes=[
            pltpu.VMEM((members * columns, layers), jnp.float32),
            pltpu.VMEM((columns, layers), jnp.float32),
            pltpu.VMEM((columns, layers), jnp.float32),
            pltpu.VMEM((members * columns, layers), jnp.float32),
            pltpu.SemaphoreType.DMA((3,)),
        ],
        compiler_params=SMALL,
        cost_estimate=pl.CostEstimate(
            flops=6 * members * columns * layers * observations,
            bytes_accessed=4 * members * columns * layers,
            transcendentals=0,
        ),
        name="inner_forecast",
    )(field.reshape(members * columns, layers), courant, spreading, col, lev)


def edge_kernel(columns, edges, low, high, readings, col, lev, fields_in, fields, copies):
    del fields_in
    members, layers = low.shape
    observations = col.shape[0]
    first = edges[0] + edges[2] * low[...]
    last = edges[1] + edges[3] * high[...]
    fields[:, :layers] = first.astype(jnp.bfloat16)
    fields[:, (columns - 1) * layers :] = last.astype(jnp.bfloat16)
    picked = at_levels(jnp.concatenate([first, last], axis=0), chosen_levels(lev, layers))
    where_col = jnp.broadcast_to(col[...].reshape(1, -1), (members, observations))
    total = jnp.where(where_col == 0, picked[:members, :], readings[...])
    total = jnp.where(where_col == columns - 1, picked[members:, :], total)
    for r in range(copies.shape[0]):
        copies[r] = total


def edge_forecast(columns, edges, low, high, readings, col, lev, fields, count):
    return pl.pallas_call(
        functools.partial(edge_kernel, columns),
        out_shape=(
            jax.ShapeDtypeStruct(fields.shape, fields.dtype),
            jax.ShapeDtypeStruct((count,) + readings.shape, jnp.float32),
        ),
        in_specs=[VMEM] * 7,
        out_specs=(VMEM, VMEM),
        input_output_aliases={6: 0},
        compiler_params=SMALL,
        name="edge_forecast",
    )(edges, low, high, readings, col, lev, fields)


def pack(upper, proj_row):
    lane = lane_index(GROUP)
    row = [upper[GROUP * r : GROUP * (r + 1), :] for r in range(8)]
    roll = lambda r, shift: pltpu.roll(row[r], shift, 1)
    first = jnp.where(lane < 64, row[0], roll(1, 64))
    second = jnp.where(lane < 16, roll(7, 80), row[2])
    second = jnp.where(lane >= 64, roll(3, 48), second)
    second = jnp.where(lane >= 112, roll(6, 64), second)
    third = jnp.where(lane < 32, roll(5, 96), row[4])
    third = jnp.where(lane >= 64, pltpu.roll(proj_row, 64, 1), third)
    return first, second, third


def unpack(first, second, third):
    lane = lane_index(GROUP)
    roll = lambda part, shift: pltpu.roll(part, shift, 1)
    rows = [
        first,
        roll(first, 64),
        second,
        roll(second, 80),
        third,
        roll(third, 32),
        roll(second, 64),
        roll(second, 48),
    ]
    keep = [
        jnp.where((lane >= 16 * (r // 2)) & (lane < 64), part, 0.0) for r, part in enumerate(rows)
    ]
    upper = jnp.concatenate(keep, axis=0)
    return upper, roll(third, 64)[:1, :]


def gram_kernel(me, readings, value, var, copies):
    hx = jnp.concatenate([readings[me[0] ^ code] for code in ORDER], axis=0)
    members = hx.shape[0]
    ybar = jnp.sum(hx, axis=0, keepdims=True) * (1.0 / members)
    anomaly = hx - ybar
    innov = value[...].reshape(1, -1) - ybar
    weighted = anomaly / var[...].reshape(1, -1)
    pad = jnp.zeros((LANES - members, hx.shape[1]), jnp.float32)
    weighted = jnp.concatenate([weighted, pad], axis=0)
    nt = (((1,), (1,)), ((), ()))
    gram = lax.dot_general(
        anomaly, weighted, nt, precision=EXACT, preferred_element_type=jnp.float32
    )
    rows = jnp.where(
        lax.broadcasted_iota(jnp.int32, (GROUP, hx.shape[1]), 0) == 0,
        jnp.broadcast_to(innov, (GROUP, hx.shape[1])),
        0.0,
    )
    proj = lax.dot_general(
        rows, weighted, nt, precision=EXACT, preferred_element_type=jnp.float32
    )
    for s, part in enumerate(pack(gram, proj)):
        for r in range(copies.shape[0]):
            copies[r, GROUP * s : GROUP * (s + 1), :] = part


def gram_parts(me, readings, value, var, count):
    return pl.pallas_call(
        gram_kernel,
        out_shape=jax.ShapeDtypeStruct((count, 3 * GROUP, LANES), jnp.float32),
        in_specs=[pl.BlockSpec(memory_space=pltpu.SMEM)] + [VMEM] * 3,
        out_specs=VMEM,
        compiler_params=SMALL,
        name="gram",
    )(me, readings, value, var)


def sum_kernel(parts, copies):
    total = parts[0]
    for r in range(1, parts.shape[0]):
        total = total + parts[r]
    for r in range(copies.shape[0]):
        copies[r] = total


def sum_copies(parts, count):
    return pl.pallas_call(
        sum_kernel,
        out_shape=jax.ShapeDtypeStruct((count,) + parts.shape[1:], jnp.float32),
        in_specs=[VMEM],
        out_specs=VMEM,
        compiler_params=SMALL,
        name="row_sum",
    )(parts)


def analysis_kernel(members, iters, parts, *refs):
    *fields, out, cells = refs
    total = parts[0]
    for r in range(1, parts.shape[0]):
        total = total + parts[r]
    upper, proj = unpack(*[total[GROUP * s : GROUP * (s + 1), :] for s in range(3)])
    square = jnp.concatenate(
        [upper, jnp.zeros((LANES - members, LANES), jnp.float32)], axis=0
    )
    turned = square.T
    row = lax.broadcasted_iota(jnp.int32, (LANES, LANES), 0)
    lane = lane_index(LANES)
    gram = jnp.where(lane // 16 >= row // 16, square, turned)[:members, :members]
    row, lane = row[:members, :members], lane[:members, :members]
    eye = jnp.where(row == lane, 1.0, 0.0)
    proj = proj[:, :members]

    dot = lambda a, b: jnp.dot(a, b, precision=EXACT, preferred_element_type=jnp.float32)
    amat = (members - 1.0) * eye + gram
    scale = jnp.sqrt(jnp.sum(amat * amat, keepdims=True))
    yit = amat / scale
    zit = eye
    for step in range(iters):
        if step == 0:
            tmat = (3.0 * eye - yit) * 0.5
        else:
            tmat = (3.0 * eye - dot(zit, yit)) * 0.5
        if step + 1 < iters:
            yit = dot(yit, tmat)
        zit = tmat if step == 0 else dot(tmat, zit)
    root = zit / jnp.sqrt(scale)
    turned = root.T
    wmean = dot(dot(proj, turned), turned)
    tfm = wmean + jnp.sqrt(jnp.float32(members - 1.0)) * turned
    centre = jnp.sum(tfm, axis=1, keepdims=True) * (1.0 / members)
    mixed = 1.0 / members + tfm - centre

    count, columns, layers = out.shape
    mine = mixed[:count, :].astype(jnp.bfloat16)
    step = 16
    for base in range(0, columns, step):
        held = [part[:, base * layers : (base + step) * layers] for part in fields]
        block = jnp.dot(
            mine, jnp.concatenate(held, axis=0), preferred_element_type=jnp.float32
        )
        for i in range(step):
            cells[pl.ds(base + i, count, stride=columns), :] = block[
                :, i * layers : (i + 1) * layers
            ]
    out[...] = cells[...].astype(jnp.bfloat16).reshape(out.shape)


def analysis(parts, fields, shape):
    members = sum(part.shape[0] for part in fields)
    count, columns, layers = shape
    return pl.pallas_call(
        functools.partial(analysis_kernel, members, NSITER),
        out_shape=jax.ShapeDtypeStruct(shape, jnp.bfloat16),
        in_specs=[VMEM] * (1 + len(fields)),
        out_specs=VMEM,
        scratch_shapes=[pltpu.VMEM((count * columns, layers), jnp.float32)],
        compiler_params=SMALL,
        name="analysis",
    )(parts, *fields)


def swapped(block, code):
    return lax.ppermute(block, "mem", [(i, i ^ code) for i in range(lax.axis_size("mem"))])


def on_device(
    background_fields, wind_courant, spreading_number, obs_col, obs_lev, obs_value, obs_var
):
    columns = background_fields.shape[1]
    mems, cols, rows = (lax.axis_size(a) for a in ("mem", "col", "row"))
    low, high = neighbours(background_fields, ("row", "col"))
    fields, hx, edges = inner_forecast(
        background_fields, wind_courant, spreading_number, obs_col, obs_lev
    )
    fields, copies = edge_forecast(
        columns, edges, low, high, hx, obs_col, obs_lev, fields, mems
    )
    readings = lax.all_to_all(copies, "mem", 0, 0)
    me = lax.axis_index("mem").astype(jnp.int32).reshape(1)
    near = [swapped(fields, code) for code in (2, 6)]
    parts = gram_parts(me, readings, obs_value, obs_var, rows)
    fields_later, _ = lax.optimization_barrier((fields, parts))
    far = swapped(fields_later, 4)
    other = swapped(fields_later, 1)
    parts = lax.all_to_all(parts, "row", 0, 0)
    parts = sum_copies(parts, cols)
    near[0], near[1], _ = lax.optimization_barrier((*near, parts))
    other_near = [swapped(block, 1) for block in near]
    other_far = swapped(far, 1)
    parts = lax.all_to_all(parts, "col", 0, 0)
    held = (fields, *near, far, other, *other_near, other_far)
    return analysis(parts, held, background_fields.shape)


def solution(mesh):
    grid, mem = mesh.shape["grid"], mesh.shape["mem"]
    fine = Mesh(mesh.devices.reshape(ROWS, grid // ROWS, mem), ("row", "col", "mem"))
    blocks = ("row", "col")
    in_specs = (
        P("mem", blocks, None),
        P(blocks, None),
        P(blocks, None),
        P(blocks),
        P(blocks),
        P(blocks),
        P(blocks),
    )
    out_specs = P("mem", blocks, None)
    return jax.shard_map(
        on_device, mesh=fine, in_specs=in_specs, out_specs=out_specs, check_vma=False
    )
```

time: 92.4 us -> 74.1 us (0.80)
  the two profiles are of different devices: /device:TPU:2 before, /device:TPU:8 now
where the time goes in v3:
time: 74.1 us; the launch traced here: 73.3 us
  starting transfers between devices  52.1 us (70%)
  waiting for transfers between devices  8.94 us (12%)
  Pallas kernels  8.45 us (11%)
  local copies, waits for them, and re-layouts  3.52 us (5%)
    ppermute x7, starting transfers between devices, swapped(): lax.ppermute(block, 'mem', [(i, i ^ code) for i in range(lax.axis_size('m...  19.1 us
    ppermute x1, starting transfers between devices, neighbours(): high = lax.ppermute(block[:, :1, :], axis, backward)  12.1 us
    all_to_all x1, starting transfers between devices, on_device(): parts = lax.all_to_all(parts, 'row', 0, 0)  7.66 us
    all_to_all x1, waiting for transfers between devices, on_device(): readings = lax.all_to_all(copies, 'mem', 0, 0)  5.78 us
    all_to_all x1, starting transfers between devices, on_device(): parts = lax.all_to_all(parts, 'col', 0, 0)  4.73 us
    pallas_call x1, Pallas kernels, analysis(): pl.pallas_call(functools.partial(analysis_kernel, members, NSITER), out_s...  4.66 us
    all_to_all x1, starting transfers between devices, on_device(): readings = lax.all_to_all(copies, 'mem', 0, 0)  4.3 us
    ppermute x1, starting transfers between devices, neighbours(): low = lax.ppermute(block[:, last:, :], axis, forward)  4.27 us
  transfers between devices with their start and end apart: 12, of which 3 were waited for; matrix products, arithmetic and copies ran while one was open for 0% of the time, Pallas kernels for 3%

profile of v3, /device:TPU:8, one launch (start us, length us, event | category | flops | bytes accessed | tf_op | source)
XLA Modules:
  0.0 73.3 jit_solution(3085965168352156067)
XLA Ops:
  0.0 0.8 %fusion = (f32[8,1,128]{2,1,0:T(1,128)S(1)}, f32[8,1,128]{2,1,0:T(1,128)S(1)}) fusion(f32[8,128,128]{2,1,0:T(8,128)} %param.7), kind=kLoop, calls=%fused_computation | loop fusion | bytes 16384 | tf_op jit(solution)/shard_map/slice | solution.py:30
  0.8 4.3 %collective-permute-start = (f32[8,1,128]{2,0,1:T(8,128)S(1)}, f32[8,1,128]{2,0,1:T(8,128)S(1)}, u32[]{:S(2)}, u32[]{:S(2)}) collective-permute-start(f32[8,1,128]{2,0,1:T(8,128)S(1)} %bitcast.10), channel_id=1, source_target_pairs={{0,8},{8,16},{16,24},{24,32},{32,40},{40,48},{48,56},{56,64},{64,7... | collective-permute-start | bytes 12296 | tf_op jit(solution)/shard_map/ppermute | solution.py:29
  5.1 0.0 copy-start.1
  5.1 0.0 copy-start
  5.1 12.1 %collective-permute-start.1 = (f32[8,1,128]{2,0,1:T(8,128)S(1)}, f32[8,1,128]{2,0,1:T(8,128)S(1)}, u32[]{:S(2)}, u32[]{:S(2)}) collective-permute-start(f32[8,1,128]{2,0,1:T(8,128)S(1)} %bitcast.9), channel_id=1, source_target_pairs={{8,0},{16,8},{24,16},{32,24},{40,32},{48,40},{56,48},{64,56},{72,6... | collective-permute-start | bytes 12296 | tf_op jit(solution)/shard_map/ppermute | solution.py:30
  17.2 0.0 copy-start.4
  17.2 1.0 %copy-done.4 = f32[8,128,128]{2,1,0:T(8,128)S(1)} copy-done((f32[8,128,128]{2,1,0:T(8,128)S(1)}, f32[8,128,128]{2,1,0:T(8,128)}, u32[]{:S(2)}) %copy-start.4) | copy-done | bytes 524312
  18.3 0.8 %copy-done.5 = f32[128,128]{1,0:T(8,128)S(1)} copy-done((f32[128,128]{1,0:T(8,128)S(1)}, f32[128,128]{1,0:T(8,128)}, u32[]{:S(2)}) %copy-start.5) | copy-done | bytes 65560
  19.1 0.8 %copy-done.6 = f32[128,128]{1,0:T(8,128)S(1)} copy-done((f32[128,128]{1,0:T(8,128)S(1)}, f32[128,128]{1,0:T(8,128)}, u32[]{:S(2)}) %copy-start.6) | copy-done | bytes 65560
  19.9 1.2 %inner_forecast.1 = (bf16[8,16384]{1,0:T(8,128)(2,1)S(1)}, f32[8,384]{1,0:T(8,128)S(1)}, f32[4,8,128]{2,1,0:T(8,128)S(1)}) custom-call(f32[1024,128]{1,0:T(8,128)S(1)} %bitcast.8, f32[128,128]{1,0:T(8,128)S(1)} %copy-done.5, f32[128,128]{1,0:T(8,128)S(1)} %copy-done.6, s32[384]{0:T(512)S(1)} %copy-done, s32[384]{0:T(512)S(1)} %copy-done.1), custom_call_target="tpu_custom_call" | custom-call | flops 301989888 | bytes 524288 | tf_op jit(solution)/shard_map/inner_forecast/pallas_call | solution.py:107
  21.2 0.0 collective-permute-done
  21.2 0.0 collective-permute-done.1
  21.2 0.8 %edge_forecast.1 = (bf16[8,16384]{1,0:T(8,128)(2,1)S(1)}, f32[8,8,384]{2,1,0:T(8,128)}) custom-call(f32[4,8,128]{2,1,0:T(8,128)S(1)} %get-tuple-element.13.edges, f32[8,128]{1,0:T(8,128)S(1)} %bitcast.6, f32[8,128]{1,0:T(8,128)S(1)} %bitcast.7, f32[8,384]{1,0:T(8,128)S(1)} %get-tuple-element.14.readings, ...), custom_call_target="tpu_custom_call", output_to_operand_aliasing={{0}: (6, {})} | custom-call | tf_op jit(solution)/shard_map/edge_forecast/pallas_call | solution.py:150
  22.0 4.3 %all-to-all-start = ((f32[8,8,384]{2,1,0:T(8,128)}), f32[8,8,384]{2,1,0:T(8,128)S(1)}, u32[]{:S(2)}, u32[]{:S(2)}) async-start(f32[8,8,384]{2,1,0:T(8,128)} %get-tuple-element.16), calls=%async_computation | async-start | bytes 196608 | tf_op jit(solution)/shard_map/all_to_all | solution.py:335
  26.3 0.0 copy-start.2
  26.3 5.8 %all-to-all-done.readings = f32[8,8,384]{2,1,0:T(8,128)S(1)} async-done(((f32[8,8,384]{2,1,0:T(8,128)}), f32[8,8,384]{2,1,0:T(8,128)S(1)}, u32[]{:S(2)}, u32[]{:S(2)}) %all-to-all-start) | async-done | bytes 98336 | tf_op jit(solution)/shard_map/all_to_all | solution.py:335
  32.1 1.1 %gram.1 = f32[8,24,128]{2,1,0:T(8,128)} custom-call(s32[1]{0:T(128)} %bitcast.me, f32[8,8,384]{2,1,0:T(8,128)S(1)} %all-to-all-done.readings, f32[384]{0:T(512)S(1)} %copy-done.2, f32[384]{0:T(512)S(1)} %copy-done.3), custom_call_target="tpu_custom_call" | custom-call | tf_op jit(solution)/shard_map/gram/pallas_call | solution.py:224
  33.2 7.7 %all-to-all-start.1 = ((f32[8,24,128]{2,1,0:T(8,128)}), f32[8,24,128]{2,1,0:T(8,128)S(1)}, u32[]{:S(2)}, u32[]{:S(2)}) async-start(f32[8,24,128]{2,1,0:T(8,128)} %gram.1), calls=%async_computation.1 | async-start | bytes 196608 | tf_op jit(solution)/shard_map/all_to_all | solution.py:342
  40.9 3.1 %collective-permute-start.3 = (bf16[8,16384]{1,0:T(8,128)(2,1)S(1)}, bf16[8,16384]{1,0:T(8,128)(2,1)S(1)}, u32[]{:S(2)}, u32[]{:S(2)}) collective-permute-start(bf16[8,16384]{1,0:T(8,128)(2,1)S(1)} %get-tuple-element.20.refs_0_), channel_id=1, source_target_pairs={{0,6},{1,7},{2,4},{3,5},{4,2},{5,3},{6,0},{7,1},{8,14},{9,15},{10,... | collective-permute-start | bytes 786440 | tf_op jit(solution)/shard_map/ppermute | solution.py:320
  43.9 1.9 %collective-permute-start.2 = (bf16[8,16384]{1,0:T(8,128)(2,1)S(1)}, bf16[8,16384]{1,0:T(8,128)(2,1)S(1)}, u32[]{:S(2)}, u32[]{:S(2)}) collective-permute-start(bf16[8,16384]{1,0:T(8,128)(2,1)S(1)} %get-tuple-element.20.refs_0_), channel_id=1, source_target_pairs={{0,2},{1,3},{2,0},{3,1},{4,6},{5,7},{6,4},{7,5},{8,10},{9,11},{10,... | collective-permute-start | bytes 786440 | tf_op jit(solution)/shard_map/ppermute | solution.py:320
  45.9 5.4 %collective-permute-start.4 = (bf16[8,16384]{1,0:T(8,128)(2,1)S(1)}, bf16[8,16384]{1,0:T(8,128)(2,1)S(1)}, u32[]{:S(2)}, u32[]{:S(2)}) collective-permute-start(bf16[8,16384]{1,0:T(8,128)(2,1)S(1)} %get-tuple-element.20.refs_0_), channel_id=1, source_target_pairs={{0,4},{1,5},{2,6},{3,7},{4,0},{5,1},{6,2},{7,3},{8,12},{9,13},{10,... | collective-permute-start | bytes 786440 | tf_op jit(solution)/shard_map/ppermute | solution.py:320
  51.3 0.0 all-to-all-done.1.parts
  51.3 0.7 row_sum.1
  52.0 4.7 %all-to-all-start.2 = ((f32[12,24,128]{2,1,0:T(8,128)}), f32[12,24,128]{2,1,0:T(8,128)S(1)}, u32[]{:S(2)}, u32[]{:S(2)}) async-start(f32[12,24,128]{2,1,0:T(8,128)} %row_sum.1), calls=%async_computation.2 | async-start | bytes 294912 | tf_op jit(solution)/shard_map/all_to_all | solution.py:347
  56.7 1.9 %collective-permute-start.5 = (bf16[8,16384]{1,0:T(8,128)(2,1)S(1)}, bf16[8,16384]{1,0:T(8,128)(2,1)S(1)}, u32[]{:S(2)}, u32[]{:S(2)}) collective-permute-start(bf16[8,16384]{1,0:T(8,128)(2,1)S(1)} %get-tuple-element.20.refs_0_), channel_id=1, source_target_pairs={{0,1},{1,0},{2,3},{3,2},{4,5},{5,4},{6,7},{7,6},{8,9},{9,8},{10,11... | collective-permute-start | bytes 786440 | tf_op jit(solution)/shard_map/ppermute | solution.py:320
  58.7 2.4 %collective-permute-start.6 = (bf16[8,16384]{1,0:T(8,128)(2,1)S(1)}, bf16[8,16384]{1,0:T(8,128)(2,1)S(1)}, u32[]{:S(2)}, u32[]{:S(2)}) collective-permute-start(bf16[8,16384]{1,0:T(8,128)(2,1)S(1)} %collective-permute-done.2.refs_1_), channel_id=1, source_target_pairs={{0,1},{1,0},{2,3},{3,2},{4,5},{5,4},{6,7},{7,6},{8,9},{9,8},{10,11... | collective-permute-start | bytes 786440 | tf_op jit(solution)/shard_map/ppermute | solution.py:320
  61.1 1.9 %collective-permute-start.7 = (bf16[8,16384]{1,0:T(8,128)(2,1)S(1)}, bf16[8,16384]{1,0:T(8,128)(2,1)S(1)}, u32[]{:S(2)}, u32[]{:S(2)}) collective-permute-start(bf16[8,16384]{1,0:T(8,128)(2,1)S(1)} %collective-permute-done.3.refs_2_), channel_id=1, source_target_pairs={{0,1},{1,0},{2,3},{3,2},{4,5},{5,4},{6,7},{7,6},{8,9},{9,8},{10,11... | collective-permute-start | bytes 786440 | tf_op jit(solution)/shard_map/ppermute | solution.py:320
  63.0 2.4 %collective-permute-start.8 = (bf16[8,16384]{1,0:T(8,128)(2,1)S(1)}, bf16[8,16384]{1,0:T(8,128)(2,1)S(1)}, u32[]{:S(2)}, u32[]{:S(2)}) collective-permute-start(bf16[8,16384]{1,0:T(8,128)(2,1)S(1)} %collective-permute-done.4.refs_3_), channel_id=1, source_target_pairs={{0,1},{1,0},{2,3},{3,2},{4,5},{5,4},{6,7},{7,6},{8,9},{9,8},{10,11... | collective-permute-start | bytes 786440 | tf_op jit(solution)/shard_map/ppermute | solution.py:320
  65.5 0.0 collective-permute-done.7.refs_6_
  65.5 1.1 %collective-permute-done.8.refs_7_ = bf16[8,16384]{1,0:T(8,128)(2,1)S(1)} collective-permute-done((bf16[8,16384]{1,0:T(8,128)(2,1)S(1)}, bf16[8,16384]{1,0:T(8,128)(2,1)S(1)}, u32[]{:S(2)}, u32[]{:S(2)}) %collective-permute-start.8) | collective-permute-done | bytes 262176 | tf_op jit(solution)/shard_map/ppermute | solution.py:320
  66.6 2.0 %all-to-all-done.2.parts = f32[12,24,128]{2,1,0:T(8,128)S(1)} async-done(((f32[12,24,128]{2,1,0:T(8,128)}), f32[12,24,128]{2,1,0:T(8,128)S(1)}, u32[]{:S(2)}, u32[]{:S(2)}) %all-to-all-start.2) | async-done | bytes 147488 | tf_op jit(solution)/shard_map/all_to_all | solution.py:347
  68.6 4.7 %analysis.1 = bf16[8,128,128]{2,1,0:T(8,128)(2,1)} custom-call(f32[12,24,128]{2,1,0:T(8,128)S(1)} %all-to-all-done.2.parts, bf16[8,16384]{1,0:T(8,128)(2,1)S(1)} %get-tuple-element.20.refs_0_, bf16[8,16384]{1,0:T(8,128)(2,1)S(1)} %collective-permute-done.2.refs_1_, bf16[8,16384]{1,0:T(8,128)(2,1)S(1)} %collective-permute-done.3.refs_2_, ...), custom_call_target="tpu_custom_call" | custom-call | tf_op jit(solution)/shard_map/analysis/pallas_call | solution.py:308
  (12 shorter events, 0.0 us)
Async XLA Ops:
  0.8 20.4 %collective-permute-start = (f32[8,1,128]{2,0,1:T(8,128)S(1)}, f32[8,1,128]{2,0,1:T(8,128)S(1)}, u32[]{:S(2)}, u32[]{:S(2)}) collective-permute-start(f32[8,1,128]{2,0,1:T(8,128)S(1)} %bitcast.10), channel_id=1, source_target_pairs={{0,8},{8,16},{16,24},{24,32},{32,40},{40,48},{48,56},{56,64},{64,7... | collective-permute-start | bytes 12296 | tf_op jit(solution)/shard_map/ppermute | solution.py:29
  5.1 12.1 %copy-start.1 = (s32[384]{0:T(512)S(1)}, s32[384]{0:T(512)}, u32[]{:S(2)}) copy-start(s32[384]{0:T(512)} %lev.3) | copy-start | bytes 4612
  5.1 12.1 %copy-start = (s32[384]{0:T(512)S(1)}, s32[384]{0:T(512)}, u32[]{:S(2)}) copy-start(s32[384]{0:T(512)} %col.3) | copy-start | bytes 4612
  5.1 16.1 %collective-permute-start.1 = (f32[8,1,128]{2,0,1:T(8,128)S(1)}, f32[8,1,128]{2,0,1:T(8,128)S(1)}, u32[]{:S(2)}, u32[]{:S(2)}) collective-permute-start(f32[8,1,128]{2,0,1:T(8,128)S(1)} %bitcast.9), channel_id=1, source_target_pairs={{8,0},{16,8},{24,16},{32,24},{40,32},{48,40},{56,48},{64,56},{72,6... | collective-permute-start | bytes 12296 | tf_op jit(solution)/shard_map/ppermute | solution.py:30
  17.2 1.0 %copy-start.4 = (f32[8,128,128]{2,1,0:T(8,128)S(1)}, f32[8,128,128]{2,1,0:T(8,128)}, u32[]{:S(2)}) copy-start(f32[8,128,128]{2,1,0:T(8,128)} %param.7) | copy-start | bytes 1572868
  18.3 0.8 %copy-start.5 = (f32[128,128]{1,0:T(8,128)S(1)}, f32[128,128]{1,0:T(8,128)}, u32[]{:S(2)}) copy-start(f32[128,128]{1,0:T(8,128)} %courant_hbm.1) | copy-start | bytes 196612
  19.1 0.8 %copy-start.6 = (f32[128,128]{1,0:T(8,128)S(1)}, f32[128,128]{1,0:T(8,128)}, u32[]{:S(2)}) copy-start(f32[128,128]{1,0:T(8,128)} %spreading_hbm.1) | copy-start | bytes 196612
  22.0 10.1 %all-to-all-start = ((f32[8,8,384]{2,1,0:T(8,128)}), f32[8,8,384]{2,1,0:T(8,128)S(1)}, u32[]{:S(2)}, u32[]{:S(2)}) async-start(f32[8,8,384]{2,1,0:T(8,128)} %get-tuple-element.16), calls=%async_computation | async-start | bytes 196608 | tf_op jit(solution)/shard_map/all_to_all | solution.py:335
  26.3 5.8 %copy-start.3 = (f32[384]{0:T(512)S(1)}, f32[384]{0:T(512)}, u32[]{:S(2)}) copy-start(f32[384]{0:T(512)} %var.1) | copy-start | bytes 4612
  26.3 5.8 %copy-start.2 = (f32[384]{0:T(512)S(1)}, f32[384]{0:T(512)}, u32[]{:S(2)}) copy-start(f32[384]{0:T(512)} %value.1) | copy-start | bytes 4612
  33.2 18.1 %all-to-all-start.1 = ((f32[8,24,128]{2,1,0:T(8,128)}), f32[8,24,128]{2,1,0:T(8,128)S(1)}, u32[]{:S(2)}, u32[]{:S(2)}) async-start(f32[8,24,128]{2,1,0:T(8,128)} %gram.1), calls=%async_computation.1 | async-start | bytes 196608 | tf_op jit(solution)/shard_map/all_to_all | solution.py:342
  40.9 17.8 %collective-permute-start.3 = (bf16[8,16384]{1,0:T(8,128)(2,1)S(1)}, bf16[8,16384]{1,0:T(8,128)(2,1)S(1)}, u32[]{:S(2)}, u32[]{:S(2)}) collective-permute-start(bf16[8,16384]{1,0:T(8,128)(2,1)S(1)} %get-tuple-element.20.refs_0_), channel_id=1, source_target_pairs={{0,6},{1,7},{2,4},{3,5},{4,2},{5,3},{6,0},{7,1},{8,14},{9,15},{10,... | collective-permute-start | bytes 786440 | tf_op jit(solution)/shard_map/ppermute | solution.py:320
  43.9 14.7 %collective-permute-start.2 = (bf16[8,16384]{1,0:T(8,128)(2,1)S(1)}, bf16[8,16384]{1,0:T(8,128)(2,1)S(1)}, u32[]{:S(2)}, u32[]{:S(2)}) collective-permute-start(bf16[8,16384]{1,0:T(8,128)(2,1)S(1)} %get-tuple-element.20.refs_0_), channel_id=1, source_target_pairs={{0,2},{1,3},{2,0},{3,1},{4,6},{5,7},{6,4},{7,5},{8,10},{9,11},{10,... | collective-permute-start | bytes 786440 | tf_op jit(solution)/shard_map/ppermute | solution.py:320
  45.9 17.2 %collective-permute-start.4 = (bf16[8,16384]{1,0:T(8,128)(2,1)S(1)}, bf16[8,16384]{1,0:T(8,128)(2,1)S(1)}, u32[]{:S(2)}, u32[]{:S(2)}) collective-permute-start(bf16[8,16384]{1,0:T(8,128)(2,1)S(1)} %get-tuple-element.20.refs_0_), channel_id=1, source_target_pairs={{0,4},{1,5},{2,6},{3,7},{4,0},{5,1},{6,2},{7,3},{8,12},{9,13},{10,... | collective-permute-start | bytes 786440 | tf_op jit(solution)/shard_map/ppermute | solution.py:320
  52.0 16.6 %all-to-all-start.2 = ((f32[12,24,128]{2,1,0:T(8,128)}), f32[12,24,128]{2,1,0:T(8,128)S(1)}, u32[]{:S(2)}, u32[]{:S(2)}) async-start(f32[12,24,128]{2,1,0:T(8,128)} %row_sum.1), calls=%async_computation.2 | async-start | bytes 294912 | tf_op jit(solution)/shard_map/all_to_all | solution.py:347
  56.7 8.7 %collective-permute-start.5 = (bf16[8,16384]{1,0:T(8,128)(2,1)S(1)}, bf16[8,16384]{1,0:T(8,128)(2,1)S(1)}, u32[]{:S(2)}, u32[]{:S(2)}) collective-permute-start(bf16[8,16384]{1,0:T(8,128)(2,1)S(1)} %get-tuple-element.20.refs_0_), channel_id=1, source_target_pairs={{0,1},{1,0},{2,3},{3,2},{4,5},{5,4},{6,7},{7,6},{8,9},{9,8},{10,11... | collective-permute-start | bytes 786440 | tf_op jit(solution)/shard_map/ppermute | solution.py:320
  58.7 6.8 %collective-permute-start.6 = (bf16[8,16384]{1,0:T(8,128)(2,1)S(1)}, bf16[8,16384]{1,0:T(8,128)(2,1)S(1)}, u32[]{:S(2)}, u32[]{:S(2)}) collective-permute-start(bf16[8,16384]{1,0:T(8,128)(2,1)S(1)} %collective-permute-done.2.refs_1_), channel_id=1, source_target_pairs={{0,1},{1,0},{2,3},{3,2},{4,5},{5,4},{6,7},{7,6},{8,9},{9,8},{10,11... | collective-permute-start | bytes 786440 | tf_op jit(solution)/shard_map/ppermute | solution.py:320
  61.1 4.4 %collective-permute-start.7 = (bf16[8,16384]{1,0:T(8,128)(2,1)S(1)}, bf16[8,16384]{1,0:T(8,128)(2,1)S(1)}, u32[]{:S(2)}, u32[]{:S(2)}) collective-permute-start(bf16[8,16384]{1,0:T(8,128)(2,1)S(1)} %collective-permute-done.3.refs_2_), channel_id=1, source_target_pairs={{0,1},{1,0},{2,3},{3,2},{4,5},{5,4},{6,7},{7,6},{8,9},{9,8},{10,11... | collective-permute-start | bytes 786440 | tf_op jit(solution)/shard_map/ppermute | solution.py:320
  63.0 3.6 %collective-permute-start.8 = (bf16[8,16384]{1,0:T(8,128)(2,1)S(1)}, bf16[8,16384]{1,0:T(8,128)(2,1)S(1)}, u32[]{:S(2)}, u32[]{:S(2)}) collective-permute-start(bf16[8,16384]{1,0:T(8,128)(2,1)S(1)} %collective-permute-done.4.refs_3_), channel_id=1, source_target_pairs={{0,1},{1,0},{2,3},{3,2},{4,5},{5,4},{6,7},{7,6},{8,9},{9,8},{10,11... | collective-permute-start | bytes 786440 | tf_op jit(solution)/shard_map/ppermute | solution.py:320

commit v4 on v3

--- a/solution.py
+++ b/solution.py
@@ -334,18 +334,19 @@
     )
     readings = lax.all_to_all(copies, "mem", 0, 0)
     me = lax.axis_index("mem").astype(jnp.int32).reshape(1)
-    near = [swapped(fields, code) for code in (2, 6)]
+    beside = swapped(fields, 2)
     parts = gram_parts(me, readings, obs_value, obs_var, rows)
     fields_later, _ = lax.optimization_barrier((fields, parts))
-    far = swapped(fields_later, 4)
-    other = swapped(fields_later, 1)
+    beside, _ = lax.optimization_barrier((beside, parts))
+    pair = jnp.concatenate([fields, beside], axis=0)
+    pair_other = swapped(pair, 1)
+    far = [swapped(block, 6) for block in (fields_later, beside)]
     parts = lax.all_to_all(parts, "row", 0, 0)
     parts = sum_copies(parts, cols)
-    near[0], near[1], _ = lax.optimization_barrier((*near, parts))
-    other_near = [swapped(block, 1) for block in near]
-    other_far = swapped(far, 1)
+    far[0], far[1], _ = lax.optimization_barrier((*far, parts))
+    others = [swapped(block, 1) for block in far]
     parts = lax.all_to_all(parts, "col", 0, 0)
-    held = (fields, *near, far, other, *other_near, other_far)
+    held = (pair, *far, pair_other, *others)
     return analysis(parts, held, background_fields.shape)
 
 

time: 74.1 us -> 74.1 us (level)
  waiting for transfers between devices: 8.94 us -> 10.8 us
  starting transfers between devices: 52.1 us -> 50.3 us
    all_to_all x1, waiting for transfers between devices: 2.03 us -> 7.37 us  [on_device(): parts = lax.all_to_all(parts, 'col', 0, 0)]
    all_to_all x1, waiting for transfers between devices: 5.78 us -> 1.82 us  [on_device(): readings = lax.all_to_all(copies, 'mem', 0, 0)]
    ppermute x7 -> x6, starting transfers between devices: 19.1 us -> 17.2 us  [swapped(): lax.ppermute(block, 'mem', [(i, i ^ code) for i in range(lax.axis_size('m...]
    ppermute x7 -> x6, waiting for transfers between devices: 1.12 us -> 1.61 us  [swapped(): lax.ppermute(block, 'mem', [(i, i ^ code) for i in range(lax.axis_size('m...]
    unnamed x14 -> x15, local copies, waits for them, and re-layouts: 2.74 us -> 2.76 us
  transfers between devices with their start and end apart: 12 -> 11, of which waited for: 3 -> 3; matrix products, arithmetic and copies ran while one was open for 0% -> 0% of each run, Pallas kernels for 3% -> 4%
where the time goes in v4:
time: 74.1 us; the launch traced here: 73.3 us
  starting transfers between devices  50.3 us (68%)
  waiting for transfers between devices  10.8 us (15%)
  Pallas kernels  8.46 us (11%)
  local copies, waits for them, and re-layouts  3.56 us (5%)
    ppermute x6, starting transfers between devices, swapped(): lax.ppermute(block, 'mem', [(i, i ^ code) for i in range(lax.axis_size('m...  17.2 us
    ppermute x1, starting transfers between devices, neighbours(): high = lax.ppermute(block[:, :1, :], axis, backward)  12.1 us
    all_to_all x1, starting transfers between devices, on_device(): parts = lax.all_to_all(parts, 'row', 0, 0)  7.66 us
    all_to_all x1, waiting for transfers between devices, on_device(): parts = lax.all_to_all(parts, 'col', 0, 0)  7.37 us
    all_to_all x1, starting transfers between devices, on_device(): parts = lax.all_to_all(parts, 'col', 0, 0)  4.72 us
    pallas_call x1, Pallas kernels, analysis(): pl.pallas_call(functools.partial(analysis_kernel, members, NSITER), out_s...  4.66 us
    all_to_all x1, starting transfers between devices, on_device(): readings = lax.all_to_all(copies, 'mem', 0, 0)  4.3 us
    ppermute x1, starting transfers between devices, neighbours(): low = lax.ppermute(block[:, last:, :], axis, forward)  4.27 us
  transfers between devices with their start and end apart: 11, of which 3 were waited for; matrix products, arithmetic and copies ran while one was open for 0% of the time, Pallas kernels for 4%

profile of v4, /device:TPU:8, one launch (start us, length us, event | category | flops | bytes accessed | tf_op | source)
XLA Modules:
  0.0 73.3 jit_solution(7979476947773341293)
XLA Ops:
  0.0 0.8 %fusion = (f32[8,1,128]{2,1,0:T(1,128)S(1)}, f32[8,1,128]{2,1,0:T(1,128)S(1)}) fusion(f32[8,128,128]{2,1,0:T(8,128)} %param.7), kind=kLoop, calls=%fused_computation.2 | loop fusion | bytes 16384 | tf_op jit(solution)/shard_map/slice | solution.py:30
  0.8 4.3 %collective-permute-start = (f32[8,1,128]{2,0,1:T(8,128)S(1)}, f32[8,1,128]{2,0,1:T(8,128)S(1)}, u32[]{:S(2)}, u32[]{:S(2)}) collective-permute-start(f32[8,1,128]{2,0,1:T(8,128)S(1)} %bitcast.10), channel_id=1, source_target_pairs={{0,8},{8,16},{16,24},{24,32},{32,40},{40,48},{48,56},{56,64},{64,7... | collective-permute-start | bytes 12296 | tf_op jit(solution)/shard_map/ppermute | solution.py:29
  5.1 0.0 copy-start.1
  5.1 0.0 copy-start
  5.1 12.1 %collective-permute-start.1 = (f32[8,1,128]{2,0,1:T(8,128)S(1)}, f32[8,1,128]{2,0,1:T(8,128)S(1)}, u32[]{:S(2)}, u32[]{:S(2)}) collective-permute-start(f32[8,1,128]{2,0,1:T(8,128)S(1)} %bitcast.9), channel_id=1, source_target_pairs={{8,0},{16,8},{24,16},{32,24},{40,32},{48,40},{56,48},{64,56},{72,6... | collective-permute-start | bytes 12296 | tf_op jit(solution)/shard_map/ppermute | solution.py:30
  17.2 0.0 copy-start.4
  17.2 1.0 %copy-done.4 = f32[8,128,128]{2,1,0:T(8,128)S(1)} copy-done((f32[8,128,128]{2,1,0:T(8,128)S(1)}, f32[8,128,128]{2,1,0:T(8,128)}, u32[]{:S(2)}) %copy-start.4) | copy-done | bytes 524312
  18.3 0.8 %copy-done.5 = f32[128,128]{1,0:T(8,128)S(1)} copy-done((f32[128,128]{1,0:T(8,128)S(1)}, f32[128,128]{1,0:T(8,128)}, u32[]{:S(2)}) %copy-start.5) | copy-done | bytes 65560
  19.1 0.8 %copy-done.6 = f32[128,128]{1,0:T(8,128)S(1)} copy-done((f32[128,128]{1,0:T(8,128)S(1)}, f32[128,128]{1,0:T(8,128)}, u32[]{:S(2)}) %copy-start.6) | copy-done | bytes 65560
  19.9 1.2 %inner_forecast.1 = (bf16[8,16384]{1,0:T(8,128)(2,1)S(1)}, f32[8,384]{1,0:T(8,128)S(1)}, f32[4,8,128]{2,1,0:T(8,128)S(1)}) custom-call(f32[1024,128]{1,0:T(8,128)S(1)} %bitcast.8, f32[128,128]{1,0:T(8,128)S(1)} %copy-done.5, f32[128,128]{1,0:T(8,128)S(1)} %copy-done.6, s32[384]{0:T(512)S(1)} %copy-done, s32[384]{0:T(512)S(1)} %copy-done.1), custom_call_target="tpu_custom_call" | custom-call | flops 301989888 | bytes 524288 | tf_op jit(solution)/shard_map/inner_forecast/pallas_call | solution.py:107
  21.2 0.0 collective-permute-done.1
  21.2 0.8 %edge_forecast.1 = (bf16[8,16384]{1,0:T(8,128)(2,1)S(1)}, f32[8,8,384]{2,1,0:T(8,128)}) custom-call(f32[4,8,128]{2,1,0:T(8,128)S(1)} %get-tuple-element.14.edges, f32[8,128]{1,0:T(8,128)S(1)} %bitcast.6, f32[8,128]{1,0:T(8,128)S(1)} %bitcast.7, f32[8,384]{1,0:T(8,128)S(1)} %get-tuple-element.15.readings, ...), custom_call_target="tpu_custom_call", output_to_operand_aliasing={{0}: (6, {})} | custom-call | tf_op jit(solution)/shard_map/edge_forecast/pallas_call | solution.py:150
  22.0 4.3 %all-to-all-start = ((f32[8,8,384]{2,1,0:T(8,128)}), f32[8,8,384]{2,1,0:T(8,128)S(1)}, u32[]{:S(2)}, u32[]{:S(2)}) async-start(f32[8,8,384]{2,1,0:T(8,128)} %get-tuple-element.17), calls=%async_computation | async-start | bytes 196608 | tf_op jit(solution)/shard_map/all_to_all | solution.py:335
  26.3 3.9 %collective-permute-start.2 = (bf16[8,16384]{1,0:T(8,128)(2,1)S(1)}, bf16[8,16384]{1,0:T(8,128)(2,1)S(1)}, u32[]{:S(2)}, u32[]{:S(2)}) collective-permute-start(bf16[8,16384]{1,0:T(8,128)(2,1)S(1)} %get-tuple-element.20), channel_id=1, source_target_pairs={{0,2},{1,3},{2,0},{3,1},{4,6},{5,7},{6,4},{7,5},{8,10},{9,11},{10,... | collective-permute-start | bytes 786440 | tf_op jit(solution)/shard_map/ppermute | solution.py:320
  30.3 0.0 copy-start.2
  30.3 0.0 copy-start.3
  30.3 1.8 %all-to-all-done.readings = f32[8,8,384]{2,1,0:T(8,128)S(1)} async-done(((f32[8,8,384]{2,1,0:T(8,128)}), f32[8,8,384]{2,1,0:T(8,128)S(1)}, u32[]{:S(2)}, u32[]{:S(2)}) %all-to-all-start) | async-done | bytes 98336 | tf_op jit(solution)/shard_map/all_to_all | solution.py:335
  32.1 1.1 %gram.1 = f32[8,24,128]{2,1,0:T(8,128)} custom-call(s32[1]{0:T(128)} %bitcast.me, f32[8,8,384]{2,1,0:T(8,128)S(1)} %all-to-all-done.readings, f32[384]{0:T(512)S(1)} %copy-done.2, f32[384]{0:T(512)S(1)} %copy-done.3), custom_call_target="tpu_custom_call" | custom-call | tf_op jit(solution)/shard_map/gram/pallas_call | solution.py:224
  33.2 7.7 %all-to-all-start.1 = ((f32[8,24,128]{2,1,0:T(8,128)}), f32[8,24,128]{2,1,0:T(8,128)S(1)}, u32[]{:S(2)}, u32[]{:S(2)}) async-start(f32[8,24,128]{2,1,0:T(8,128)} %gram.1), calls=%async_computation.1 | async-start | bytes 196608 | tf_op jit(solution)/shard_map/all_to_all | solution.py:344
  40.9 3.1 %collective-permute-start.3 = (bf16[8,16384]{1,0:T(8,128)(2,1)S(1)}, bf16[8,16384]{1,0:T(8,128)(2,1)S(1)}, u32[]{:S(2)}, u32[]{:S(2)}) collective-permute-start(bf16[8,16384]{1,0:T(8,128)(2,1)S(1)} %get-tuple-element.20), channel_id=1, source_target_pairs={{0,6},{1,7},{2,4},{3,5},{4,2},{5,3},{6,0},{7,1},{8,14},{9,15},{10,... | collective-permute-start | bytes 786440 | tf_op jit(solution)/shard_map/ppermute | solution.py:320
  43.9 0.0 collective-permute-done.2
  43.9 4.0 %collective-permute-start.4 = (bf16[8,16384]{1,0:T(8,128)(2,1)S(1)}, bf16[8,16384]{1,0:T(8,128)(2,1)S(1)}, u32[]{:S(2)}, u32[]{:S(2)}) collective-permute-start(bf16[8,16384]{1,0:T(8,128)(2,1)S(1)} %collective-permute-done.2), channel_id=1, source_target_pairs={{0,6},{1,7},{2,4},{3,5},{4,2},{5,3},{6,0},{7,1},{8,14},{9,15},{10,... | collective-permute-start | bytes 786440 | tf_op jit(solution)/shard_map/ppermute | solution.py:320
  48.0 1.9 %collective-permute-start.5 = (bf16[16,16384]{1,0:T(8,128)(2,1)S(1)}, bf16[16,16384]{1,0:T(8,128)(2,1)S(1)}, u32[]{:S(2)}, u32[]{:S(2)}) collective-permute-start(bf16[16,16384]{1,0:T(8,128)(2,1)S(1)} %constant_dynamic-update-slice_fusion.refs_0_), channel_id=1, source_target_pairs={{0,1},{1,0},{2,3},{3,2},{4,5},{5,4},{6,7},{7,6},{8,9},{9,8},{10,11... | collective-permute-start | bytes 1572872 | tf_op jit(solution)/shard_map/ppermute | solution.py:320
  49.9 0.0 all-to-all-done.1.parts
  49.9 0.7 row_sum.1
  50.6 4.7 %all-to-all-start.2 = ((f32[12,24,128]{2,1,0:T(8,128)}), f32[12,24,128]{2,1,0:T(8,128)S(1)}, u32[]{:S(2)}, u32[]{:S(2)}) async-start(f32[12,24,128]{2,1,0:T(8,128)} %row_sum.1), calls=%async_computation.2 | async-start | bytes 294912 | tf_op jit(solution)/shard_map/all_to_all | solution.py:348
  55.3 1.6 %collective-permute-done.4.refs_2_ = bf16[8,16384]{1,0:T(8,128)(2,1)S(1)} collective-permute-done((bf16[8,16384]{1,0:T(8,128)(2,1)S(1)}, bf16[8,16384]{1,0:T(8,128)(2,1)S(1)}, u32[]{:S(2)}, u32[]{:S(2)}) %collective-permute-start.4) | collective-permute-done | bytes 262176 | tf_op jit(solution)/shard_map/ppermute | solution.py:320
  56.9 1.9 %collective-permute-start.6 = (bf16[8,16384]{1,0:T(8,128)(2,1)S(1)}, bf16[8,16384]{1,0:T(8,128)(2,1)S(1)}, u32[]{:S(2)}, u32[]{:S(2)}) collective-permute-start(bf16[8,16384]{1,0:T(8,128)(2,1)S(1)} %collective-permute-done.3.refs_1_), channel_id=1, source_target_pairs={{0,1},{1,0},{2,3},{3,2},{4,5},{5,4},{6,7},{7,6},{8,9},{9,8},{10,11... | collective-permute-start | bytes 786440 | tf_op jit(solution)/shard_map/ppermute | solution.py:320
  58.8 2.4 %collective-permute-start.7 = (bf16[8,16384]{1,0:T(8,128)(2,1)S(1)}, bf16[8,16384]{1,0:T(8,128)(2,1)S(1)}, u32[]{:S(2)}, u32[]{:S(2)}) collective-permute-start(bf16[8,16384]{1,0:T(8,128)(2,1)S(1)} %collective-permute-done.4.refs_2_), channel_id=1, source_target_pairs={{0,1},{1,0},{2,3},{3,2},{4,5},{5,4},{6,7},{7,6},{8,9},{9,8},{10,11... | collective-permute-start | bytes 786440 | tf_op jit(solution)/shard_map/ppermute | solution.py:320
  61.2 7.4 %all-to-all-done.2.parts = f32[12,24,128]{2,1,0:T(8,128)S(1)} async-done(((f32[12,24,128]{2,1,0:T(8,128)}), f32[12,24,128]{2,1,0:T(8,128)S(1)}, u32[]{:S(2)}, u32[]{:S(2)}) %all-to-all-start.2) | async-done | bytes 147488 | tf_op jit(solution)/shard_map/all_to_all | solution.py:348
  68.6 0.0 collective-permute-done.6.refs_4_
  68.6 4.7 %analysis.1 = bf16[8,128,128]{2,1,0:T(8,128)(2,1)} custom-call(f32[12,24,128]{2,1,0:T(8,128)S(1)} %all-to-all-done.2.parts, bf16[16,16384]{1,0:T(8,128)(2,1)S(1)} %constant_dynamic-update-slice_fusion.refs_0_, bf16[8,16384]{1,0:T(8,128)(2,1)S(1)} %collective-permute-done.3.refs_1_, bf16[8,16384]{1,0:T(8,128)(2,1)S(1)} %collective-permute-done.4.refs_2_, ...), custom_call_target="tpu_custom_call" | custom-call | tf_op jit(solution)/shard_map/analysis/pallas_call | solution.py:308
  (12 shorter events, 0.1 us)
Async XLA Ops:
  0.8 20.4 %collective-permute-start = (f32[8,1,128]{2,0,1:T(8,128)S(1)}, f32[8,1,128]{2,0,1:T(8,128)S(1)}, u32[]{:S(2)}, u32[]{:S(2)}) collective-permute-start(f32[8,1,128]{2,0,1:T(8,128)S(1)} %bitcast.10), channel_id=1, source_target_pairs={{0,8},{8,16},{16,24},{24,32},{32,40},{40,48},{48,56},{56,64},{64,7... | collective-permute-start | bytes 12296 | tf_op jit(solution)/shard_map/ppermute | solution.py:29
  5.1 12.1 %copy-start.1 = (s32[384]{0:T(512)S(1)}, s32[384]{0:T(512)}, u32[]{:S(2)}) copy-start(s32[384]{0:T(512)} %lev.3) | copy-start | bytes 4612
  5.1 12.1 %copy-start = (s32[384]{0:T(512)S(1)}, s32[384]{0:T(512)}, u32[]{:S(2)}) copy-start(s32[384]{0:T(512)} %col.3) | copy-start | bytes 4612
  5.1 16.1 %collective-permute-start.1 = (f32[8,1,128]{2,0,1:T(8,128)S(1)}, f32[8,1,128]{2,0,1:T(8,128)S(1)}, u32[]{:S(2)}, u32[]{:S(2)}) collective-permute-start(f32[8,1,128]{2,0,1:T(8,128)S(1)} %bitcast.9), channel_id=1, source_target_pairs={{8,0},{16,8},{24,16},{32,24},{40,32},{48,40},{56,48},{64,56},{72,6... | collective-permute-start | bytes 12296 | tf_op jit(solution)/shard_map/ppermute | solution.py:30
  17.2 1.0 %copy-start.4 = (f32[8,128,128]{2,1,0:T(8,128)S(1)}, f32[8,128,128]{2,1,0:T(8,128)}, u32[]{:S(2)}) copy-start(f32[8,128,128]{2,1,0:T(8,128)} %param.7) | copy-start | bytes 1572868
  18.3 0.8 %copy-start.5 = (f32[128,128]{1,0:T(8,128)S(1)}, f32[128,128]{1,0:T(8,128)}, u32[]{:S(2)}) copy-start(f32[128,128]{1,0:T(8,128)} %courant_hbm.1) | copy-start | bytes 196612
  19.1 0.8 %copy-start.6 = (f32[128,128]{1,0:T(8,128)S(1)}, f32[128,128]{1,0:T(8,128)}, u32[]{:S(2)}) copy-start(f32[128,128]{1,0:T(8,128)} %spreading_hbm.1) | copy-start | bytes 196612
  22.0 10.1 %all-to-all-start = ((f32[8,8,384]{2,1,0:T(8,128)}), f32[8,8,384]{2,1,0:T(8,128)S(1)}, u32[]{:S(2)}, u32[]{:S(2)}) async-start(f32[8,8,384]{2,1,0:T(8,128)} %get-tuple-element.17), calls=%async_computation | async-start | bytes 196608 | tf_op jit(solution)/shard_map/all_to_all | solution.py:335
  26.3 17.6 %collective-permute-start.2 = (bf16[8,16384]{1,0:T(8,128)(2,1)S(1)}, bf16[8,16384]{1,0:T(8,128)(2,1)S(1)}, u32[]{:S(2)}, u32[]{:S(2)}) collective-permute-start(bf16[8,16384]{1,0:T(8,128)(2,1)S(1)} %get-tuple-element.20), channel_id=1, source_target_pairs={{0,2},{1,3},{2,0},{3,1},{4,6},{5,7},{6,4},{7,5},{8,10},{9,11},{10,... | collective-permute-start | bytes 786440 | tf_op jit(solution)/shard_map/ppermute | solution.py:320
  30.3 1.9 %copy-start.2 = (f32[384]{0:T(512)S(1)}, f32[384]{0:T(512)}, u32[]{:S(2)}) copy-start(f32[384]{0:T(512)} %value.1) | copy-start | bytes 4612
  30.3 1.9 %copy-start.3 = (f32[384]{0:T(512)S(1)}, f32[384]{0:T(512)}, u32[]{:S(2)}) copy-start(f32[384]{0:T(512)} %var.1) | copy-start | bytes 4612
  33.2 16.7 %all-to-all-start.1 = ((f32[8,24,128]{2,1,0:T(8,128)}), f32[8,24,128]{2,1,0:T(8,128)S(1)}, u32[]{:S(2)}, u32[]{:S(2)}) async-start(f32[8,24,128]{2,1,0:T(8,128)} %gram.1), calls=%async_computation.1 | async-start | bytes 196608 | tf_op jit(solution)/shard_map/all_to_all | solution.py:344
  40.9 14.4 %collective-permute-start.3 = (bf16[8,16384]{1,0:T(8,128)(2,1)S(1)}, bf16[8,16384]{1,0:T(8,128)(2,1)S(1)}, u32[]{:S(2)}, u32[]{:S(2)}) collective-permute-start(bf16[8,16384]{1,0:T(8,128)(2,1)S(1)} %get-tuple-element.20), channel_id=1, source_target_pairs={{0,6},{1,7},{2,4},{3,5},{4,2},{5,3},{6,0},{7,1},{8,14},{9,15},{10,... | collective-permute-start | bytes 786440 | tf_op jit(solution)/shard_map/ppermute | solution.py:320
  43.9 13.0 %collective-permute-start.4 = (bf16[8,16384]{1,0:T(8,128)(2,1)S(1)}, bf16[8,16384]{1,0:T(8,128)(2,1)S(1)}, u32[]{:S(2)}, u32[]{:S(2)}) collective-permute-start(bf16[8,16384]{1,0:T(8,128)(2,1)S(1)} %collective-permute-done.2), channel_id=1, source_target_pairs={{0,6},{1,7},{2,4},{3,5},{4,2},{5,3},{6,0},{7,1},{8,14},{9,15},{10,... | collective-permute-start | bytes 786440 | tf_op jit(solution)/shard_map/ppermute | solution.py:320
  48.0 20.7 %collective-permute-start.5 = (bf16[16,16384]{1,0:T(8,128)(2,1)S(1)}, bf16[16,16384]{1,0:T(8,128)(2,1)S(1)}, u32[]{:S(2)}, u32[]{:S(2)}) collective-permute-start(bf16[16,16384]{1,0:T(8,128)(2,1)S(1)} %constant_dynamic-update-slice_fusion.refs_0_), channel_id=1, source_target_pairs={{0,1},{1,0},{2,3},{3,2},{4,5},{5,4},{6,7},{7,6},{8,9},{9,8},{10,11... | collective-permute-start | bytes 1572872 | tf_op jit(solution)/shard_map/ppermute | solution.py:320
  50.6 18.0 %all-to-all-start.2 = ((f32[12,24,128]{2,1,0:T(8,128)}), f32[12,24,128]{2,1,0:T(8,128)S(1)}, u32[]{:S(2)}, u32[]{:S(2)}) async-start(f32[12,24,128]{2,1,0:T(8,128)} %row_sum.1), calls=%async_computation.2 | async-start | bytes 294912 | tf_op jit(solution)/shard_map/all_to_all | solution.py:348
  56.9 11.7 %collective-permute-start.6 = (bf16[8,16384]{1,0:T(8,128)(2,1)S(1)}, bf16[8,16384]{1,0:T(8,128)(2,1)S(1)}, u32[]{:S(2)}, u32[]{:S(2)}) collective-permute-start(bf16[8,16384]{1,0:T(8,128)(2,1)S(1)} %collective-permute-done.3.refs_1_), channel_id=1, source_target_pairs={{0,1},{1,0},{2,3},{3,2},{4,5},{5,4},{6,7},{7,6},{8,9},{9,8},{10,11... | collective-permute-start | bytes 786440 | tf_op jit(solution)/shard_map/ppermute | solution.py:320
  58.8 9.8 %collective-permute-start.7 = (bf16[8,16384]{1,0:T(8,128)(2,1)S(1)}, bf16[8,16384]{1,0:T(8,128)(2,1)S(1)}, u32[]{:S(2)}, u32[]{:S(2)}) collective-permute-start(bf16[8,16384]{1,0:T(8,128)(2,1)S(1)} %collective-permute-done.4.refs_2_), channel_id=1, source_target_pairs={{0,1},{1,0},{2,3},{3,2},{4,5},{5,4},{6,7},{7,6},{8,9},{9,8},{10,11... | collective-permute-start | bytes 786440 | tf_op jit(solution)/shard_map/ppermute | solution.py:320

commit v5 on v4

--- a/solution.py
+++ b/solution.py
@@ -235,14 +235,17 @@
     total = parts[0]
     for r in range(1, parts.shape[0]):
         total = total + parts[r]
+    rows = total.shape[0]
+    spare = jnp.zeros((copies.shape[1] - rows, total.shape[1]), jnp.float32)
     for r in range(copies.shape[0]):
-        copies[r] = total
+        copies[r, :rows] = total
+        copies[r, rows:] = spare
 
 
 def sum_copies(parts, count):
     return pl.pallas_call(
         sum_kernel,
-        out_shape=jax.ShapeDtypeStruct((count,) + parts.shape[1:], jnp.float32),
+        out_shape=jax.ShapeDtypeStruct((count, 40, LANES), jnp.float32),
         in_specs=[VMEM],
         out_specs=VMEM,
         compiler_params=SMALL,
@@ -335,17 +338,17 @@
     readings = lax.all_to_all(copies, "mem", 0, 0)
     me = lax.axis_index("mem").astype(jnp.int32).reshape(1)
     beside = swapped(fields, 2)
-    parts = gram_parts(me, readings, obs_value, obs_var, rows)
+    parts = gram_parts(me, readings, obs_value, obs_var, cols)
     fields_later, _ = lax.optimization_barrier((fields, parts))
     beside, _ = lax.optimization_barrier((beside, parts))
     pair = jnp.concatenate([fields, beside], axis=0)
     pair_other = swapped(pair, 1)
     far = [swapped(block, 6) for block in (fields_later, beside)]
-    parts = lax.all_to_all(parts, "row", 0, 0)
-    parts = sum_copies(parts, cols)
+    parts = lax.all_to_all(parts, "col", 0, 0)
+    parts = sum_copies(parts, rows)
     far[0], far[1], _ = lax.optimization_barrier((*far, parts))
     others = [swapped(block, 1) for block in far]
-    parts = lax.all_to_all(parts, "col", 0, 0)
+    parts = lax.all_to_all(parts, "row", 0, 0)
     held = (pair, *far, pair_other, *others)
     return analysis(parts, held, background_fields.shape)
 

time: 74.1 us -> 72.5 us (0.978)
  the two profiles are of different devices: /device:TPU:8 before, /device:TPU:2 now
where the time goes in v5:
time: 72.5 us; the launch traced here: 71.7 us
  starting transfers between devices  46.7 us (64%)
  waiting for transfers between devices  12.8 us (18%)
  Pallas kernels  8.48 us (12%)
  local copies, waits for them, and re-layouts  3.56 us (5%)
    ppermute x6, starting transfers between devices, swapped(): lax.ppermute(block, 'mem', [(i, i ^ code) for i in range(lax.axis_size('m...  14.1 us
    all_to_all x1, starting transfers between devices, on_device(): parts = lax.all_to_all(parts, 'col', 0, 0)  10.4 us
    all_to_all x1, starting transfers between devices, on_device(): readings = lax.all_to_all(copies, 'mem', 0, 0)  9.47 us
    all_to_all x1, starting transfers between devices, on_device(): parts = lax.all_to_all(parts, 'row', 0, 0)  7.1 us
    all_to_all x1, waiting for transfers between devices, on_device(): parts = lax.all_to_all(parts, 'row', 0, 0)  5.07 us
    all_to_all x1, waiting for transfers between devices, on_device(): parts = lax.all_to_all(parts, 'col', 0, 0)  4.87 us
    pallas_call x1, Pallas kernels, analysis(): pl.pallas_call(functools.partial(analysis_kernel, members, NSITER), out_s...  4.66 us
    ppermute x1, starting transfers between devices, neighbours(): low = lax.ppermute(block[:, last:, :], axis, forward)  4.26 us
  transfers between devices with their start and end apart: 11, of which 4 were waited for; matrix products, arithmetic and copies ran while one was open for 0% of the time, Pallas kernels for 4%

profile of v5, /device:TPU:2, one launch (start us, length us, event | category | flops | bytes accessed | tf_op | source)
XLA Modules:
  0.0 71.7 jit_solution(902381559150251605)
XLA Ops:
  0.0 0.8 %fusion = (f32[8,1,128]{2,1,0:T(1,128)S(1)}, f32[8,1,128]{2,1,0:T(1,128)S(1)}) fusion(f32[8,128,128]{2,1,0:T(8,128)} %param.7), kind=kLoop, calls=%fused_computation.2 | loop fusion | bytes 16384 | tf_op jit(solution)/shard_map/slice | solution.py:30
  0.8 4.3 %collective-permute-start = (f32[8,1,128]{2,0,1:T(8,128)S(1)}, f32[8,1,128]{2,0,1:T(8,128)S(1)}, u32[]{:S(2)}, u32[]{:S(2)}) collective-permute-start(f32[8,1,128]{2,0,1:T(8,128)S(1)} %bitcast.10), channel_id=1, source_target_pairs={{0,8},{8,16},{16,24},{24,32},{32,40},{40,48},{48,56},{56,64},{64,7... | collective-permute-start | bytes 12296 | tf_op jit(solution)/shard_map/ppermute | solution.py:29
  5.1 0.0 copy-start.1
  5.1 0.0 copy-start
  5.1 1.3 %collective-permute-start.1 = (f32[8,1,128]{2,0,1:T(8,128)S(1)}, f32[8,1,128]{2,0,1:T(8,128)S(1)}, u32[]{:S(2)}, u32[]{:S(2)}) collective-permute-start(f32[8,1,128]{2,0,1:T(8,128)S(1)} %bitcast.9), channel_id=1, source_target_pairs={{8,0},{16,8},{24,16},{32,24},{40,32},{48,40},{56,48},{64,56},{72,6... | collective-permute-start | bytes 12296 | tf_op jit(solution)/shard_map/ppermute | solution.py:30
  6.4 0.0 copy-start.4
  6.4 1.0 %copy-done.4 = f32[8,128,128]{2,1,0:T(8,128)S(1)} copy-done((f32[8,128,128]{2,1,0:T(8,128)S(1)}, f32[8,128,128]{2,1,0:T(8,128)}, u32[]{:S(2)}) %copy-start.4) | copy-done | bytes 524312
  7.4 0.8 %copy-done.5 = f32[128,128]{1,0:T(8,128)S(1)} copy-done((f32[128,128]{1,0:T(8,128)S(1)}, f32[128,128]{1,0:T(8,128)}, u32[]{:S(2)}) %copy-start.5) | copy-done | bytes 65560
  8.3 0.8 %copy-done.6 = f32[128,128]{1,0:T(8,128)S(1)} copy-done((f32[128,128]{1,0:T(8,128)S(1)}, f32[128,128]{1,0:T(8,128)}, u32[]{:S(2)}) %copy-start.6) | copy-done | bytes 65560
  9.1 1.2 %inner_forecast.1 = (bf16[8,16384]{1,0:T(8,128)(2,1)S(1)}, f32[8,384]{1,0:T(8,128)S(1)}, f32[4,8,128]{2,1,0:T(8,128)S(1)}) custom-call(f32[1024,128]{1,0:T(8,128)S(1)} %bitcast.8, f32[128,128]{1,0:T(8,128)S(1)} %copy-done.5, f32[128,128]{1,0:T(8,128)S(1)} %copy-done.6, s32[384]{0:T(512)S(1)} %copy-done, s32[384]{0:T(512)S(1)} %copy-done.1), custom_call_target="tpu_custom_call" | custom-call | flops 301989888 | bytes 524288 | tf_op jit(solution)/shard_map/inner_forecast/pallas_call | solution.py:107
  10.4 0.0 collective-permute-done
  10.4 0.6 collective-permute-done.1
  10.9 0.8 %edge_forecast.1 = (bf16[8,16384]{1,0:T(8,128)(2,1)S(1)}, f32[8,8,384]{2,1,0:T(8,128)}) custom-call(f32[4,8,128]{2,1,0:T(8,128)S(1)} %get-tuple-element.14.edges, f32[8,128]{1,0:T(8,128)S(1)} %bitcast.6, f32[8,128]{1,0:T(8,128)S(1)} %bitcast.7, f32[8,384]{1,0:T(8,128)S(1)} %get-tuple-element.15.readings, ...), custom_call_target="tpu_custom_call", output_to_operand_aliasing={{0}: (6, {})} | custom-call | tf_op jit(solution)/shard_map/edge_forecast/pallas_call | solution.py:150
  11.8 9.5 %all-to-all-start = ((f32[8,8,384]{2,1,0:T(8,128)}), f32[8,8,384]{2,1,0:T(8,128)S(1)}, u32[]{:S(2)}, u32[]{:S(2)}) async-start(f32[8,8,384]{2,1,0:T(8,128)} %get-tuple-element.17), calls=%async_computation | async-start | bytes 196608 | tf_op jit(solution)/shard_map/all_to_all | solution.py:338
  21.2 2.0 %collective-permute-start.2 = (bf16[8,16384]{1,0:T(8,128)(2,1)S(1)}, bf16[8,16384]{1,0:T(8,128)(2,1)S(1)}, u32[]{:S(2)}, u32[]{:S(2)}) collective-permute-start(bf16[8,16384]{1,0:T(8,128)(2,1)S(1)} %get-tuple-element.20), channel_id=1, source_target_pairs={{0,2},{1,3},{2,0},{3,1},{4,6},{5,7},{6,4},{7,5},{8,10},{9,11},{10,... | collective-permute-start | bytes 786440 | tf_op jit(solution)/shard_map/ppermute | solution.py:323
  23.3 0.0 copy-start.2
  23.3 0.0 copy-start.3
  23.3 2.3 %all-to-all-done.readings = f32[8,8,384]{2,1,0:T(8,128)S(1)} async-done(((f32[8,8,384]{2,1,0:T(8,128)}), f32[8,8,384]{2,1,0:T(8,128)S(1)}, u32[]{:S(2)}, u32[]{:S(2)}) %all-to-all-start) | async-done | bytes 98336 | tf_op jit(solution)/shard_map/all_to_all | solution.py:338
  25.6 1.1 %gram.1 = f32[12,24,128]{2,1,0:T(8,128)} custom-call(s32[1]{0:T(128)} %bitcast.me, f32[8,8,384]{2,1,0:T(8,128)S(1)} %all-to-all-done.readings, f32[384]{0:T(512)S(1)} %copy-done.2, f32[384]{0:T(512)S(1)} %copy-done.3), custom_call_target="tpu_custom_call" | custom-call | tf_op jit(solution)/shard_map/gram/pallas_call | solution.py:224
  26.7 10.4 %all-to-all-start.1 = ((f32[12,24,128]{2,1,0:T(8,128)}), f32[12,24,128]{2,1,0:T(8,128)S(1)}, u32[]{:S(2)}, u32[]{:S(2)}) async-start(f32[12,24,128]{2,1,0:T(8,128)} %gram.1), calls=%async_computation.1 | async-start | bytes 294912 | tf_op jit(solution)/shard_map/all_to_all | solution.py:347
  37.1 2.8 %collective-permute-start.3 = (bf16[8,16384]{1,0:T(8,128)(2,1)S(1)}, bf16[8,16384]{1,0:T(8,128)(2,1)S(1)}, u32[]{:S(2)}, u32[]{:S(2)}) collective-permute-start(bf16[8,16384]{1,0:T(8,128)(2,1)S(1)} %get-tuple-element.20), channel_id=1, source_target_pairs={{0,6},{1,7},{2,4},{3,5},{4,2},{5,3},{6,0},{7,1},{8,14},{9,15},{10,... | collective-permute-start | bytes 786440 | tf_op jit(solution)/shard_map/ppermute | solution.py:323
  40.0 3.0 %collective-permute-start.4 = (bf16[8,16384]{1,0:T(8,128)(2,1)S(1)}, bf16[8,16384]{1,0:T(8,128)(2,1)S(1)}, u32[]{:S(2)}, u32[]{:S(2)}) collective-permute-start(bf16[8,16384]{1,0:T(8,128)(2,1)S(1)} %collective-permute-done.2), channel_id=1, source_target_pairs={{0,6},{1,7},{2,4},{3,5},{4,2},{5,3},{6,0},{7,1},{8,14},{9,15},{10,... | collective-permute-start | bytes 786440 | tf_op jit(solution)/shard_map/ppermute | solution.py:323
  43.0 1.9 %collective-permute-start.5 = (bf16[16,16384]{1,0:T(8,128)(2,1)S(1)}, bf16[16,16384]{1,0:T(8,128)(2,1)S(1)}, u32[]{:S(2)}, u32[]{:S(2)}) collective-permute-start(bf16[16,16384]{1,0:T(8,128)(2,1)S(1)} %constant_dynamic-update-slice_fusion.refs_0_), channel_id=1, source_target_pairs={{0,1},{1,0},{2,3},{3,2},{4,5},{5,4},{6,7},{7,6},{8,9},{9,8},{10,11... | collective-permute-start | bytes 1572872 | tf_op jit(solution)/shard_map/ppermute | solution.py:323
  45.0 4.9 %all-to-all-done.1.parts = f32[12,24,128]{2,1,0:T(8,128)S(1)} async-done(((f32[12,24,128]{2,1,0:T(8,128)}), f32[12,24,128]{2,1,0:T(8,128)S(1)}, u32[]{:S(2)}, u32[]{:S(2)}) %all-to-all-start.1) | async-done | bytes 147488 | tf_op jit(solution)/shard_map/all_to_all | solution.py:347
  49.8 0.7 row_sum.1
  50.5 7.1 %all-to-all-start.2 = ((f32[8,40,128]{2,1,0:T(8,128)}), f32[8,40,128]{2,1,0:T(8,128)S(1)}, u32[]{:S(2)}, u32[]{:S(2)}) async-start(f32[8,40,128]{2,1,0:T(8,128)} %row_sum.1), calls=%async_computation.2 | async-start | bytes 327680 | tf_op jit(solution)/shard_map/all_to_all | solution.py:351
  57.6 0.0 collective-permute-done.3.refs_1_
  57.6 1.9 %collective-permute-start.6 = (bf16[8,16384]{1,0:T(8,128)(2,1)S(1)}, bf16[8,16384]{1,0:T(8,128)(2,1)S(1)}, u32[]{:S(2)}, u32[]{:S(2)}) collective-permute-start(bf16[8,16384]{1,0:T(8,128)(2,1)S(1)} %collective-permute-done.3.refs_1_), channel_id=1, source_target_pairs={{0,1},{1,0},{2,3},{3,2},{4,5},{5,4},{6,7},{7,6},{8,9},{9,8},{10,11... | collective-permute-start | bytes 786440 | tf_op jit(solution)/shard_map/ppermute | solution.py:323
  59.6 2.4 %collective-permute-start.7 = (bf16[8,16384]{1,0:T(8,128)(2,1)S(1)}, bf16[8,16384]{1,0:T(8,128)(2,1)S(1)}, u32[]{:S(2)}, u32[]{:S(2)}) collective-permute-start(bf16[8,16384]{1,0:T(8,128)(2,1)S(1)} %collective-permute-done.4.refs_2_), channel_id=1, source_target_pairs={{0,1},{1,0},{2,3},{3,2},{4,5},{5,4},{6,7},{7,6},{8,9},{9,8},{10,11... | collective-permute-start | bytes 786440 | tf_op jit(solution)/shard_map/ppermute | solution.py:323
  62.0 5.1 %all-to-all-done.2.parts = f32[8,40,128]{2,1,0:T(8,128)S(1)} async-done(((f32[8,40,128]{2,1,0:T(8,128)}), f32[8,40,128]{2,1,0:T(8,128)S(1)}, u32[]{:S(2)}, u32[]{:S(2)}) %all-to-all-start.2) | async-done | bytes 163872 | tf_op jit(solution)/shard_map/all_to_all | solution.py:351
  67.1 0.0 collective-permute-done.6.refs_4_
  67.1 4.7 %analysis.1 = bf16[8,128,128]{2,1,0:T(8,128)(2,1)} custom-call(f32[8,40,128]{2,1,0:T(8,128)S(1)} %all-to-all-done.2.parts, bf16[16,16384]{1,0:T(8,128)(2,1)S(1)} %constant_dynamic-update-slice_fusion.refs_0_, bf16[8,16384]{1,0:T(8,128)(2,1)S(1)} %collective-permute-done.3.refs_1_, bf16[8,16384]{1,0:T(8,128)(2,1)S(1)} %collective-permute-done.4.refs_2_, ...), custom_call_target="tpu_custom_call" | custom-call | tf_op jit(solution)/shard_map/analysis/pallas_call | solution.py:311
  (12 shorter events, 0.1 us)
Async XLA Ops:
  0.8 9.6 %collective-permute-start = (f32[8,1,128]{2,0,1:T(8,128)S(1)}, f32[8,1,128]{2,0,1:T(8,128)S(1)}, u32[]{:S(2)}, u32[]{:S(2)}) collective-permute-start(f32[8,1,128]{2,0,1:T(8,128)S(1)} %bitcast.10), channel_id=1, source_target_pairs={{0,8},{8,16},{16,24},{24,32},{32,40},{40,48},{48,56},{56,64},{64,7... | collective-permute-start | bytes 12296 | tf_op jit(solution)/shard_map/ppermute | solution.py:29
  5.1 1.3 %copy-start.1 = (s32[384]{0:T(512)S(1)}, s32[384]{0:T(512)}, u32[]{:S(2)}) copy-start(s32[384]{0:T(512)} %lev.3) | copy-start | bytes 4612
  5.1 1.3 %copy-start = (s32[384]{0:T(512)S(1)}, s32[384]{0:T(512)}, u32[]{:S(2)}) copy-start(s32[384]{0:T(512)} %col.3) | copy-start | bytes 4612
  5.1 5.9 %collective-permute-start.1 = (f32[8,1,128]{2,0,1:T(8,128)S(1)}, f32[8,1,128]{2,0,1:T(8,128)S(1)}, u32[]{:S(2)}, u32[]{:S(2)}) collective-permute-start(f32[8,1,128]{2,0,1:T(8,128)S(1)} %bitcast.9), channel_id=1, source_target_pairs={{8,0},{16,8},{24,16},{32,24},{40,32},{48,40},{56,48},{64,56},{72,6... | collective-permute-start | bytes 12296 | tf_op jit(solution)/shard_map/ppermute | solution.py:30
  6.4 1.0 %copy-start.4 = (f32[8,128,128]{2,1,0:T(8,128)S(1)}, f32[8,128,128]{2,1,0:T(8,128)}, u32[]{:S(2)}) copy-start(f32[8,128,128]{2,1,0:T(8,128)} %param.7) | copy-start | bytes 1572868
  7.4 0.8 %copy-start.5 = (f32[128,128]{1,0:T(8,128)S(1)}, f32[128,128]{1,0:T(8,128)}, u32[]{:S(2)}) copy-start(f32[128,128]{1,0:T(8,128)} %courant_hbm.1) | copy-start | bytes 196612
  8.3 0.8 %copy-start.6 = (f32[128,128]{1,0:T(8,128)S(1)}, f32[128,128]{1,0:T(8,128)}, u32[]{:S(2)}) copy-start(f32[128,128]{1,0:T(8,128)} %spreading_hbm.1) | copy-start | bytes 196612
  11.8 13.8 %all-to-all-start = ((f32[8,8,384]{2,1,0:T(8,128)}), f32[8,8,384]{2,1,0:T(8,128)S(1)}, u32[]{:S(2)}, u32[]{:S(2)}) async-start(f32[8,8,384]{2,1,0:T(8,128)} %get-tuple-element.17), calls=%async_computation | async-start | bytes 196608 | tf_op jit(solution)/shard_map/all_to_all | solution.py:338
  21.2 18.7 %collective-permute-start.2 = (bf16[8,16384]{1,0:T(8,128)(2,1)S(1)}, bf16[8,16384]{1,0:T(8,128)(2,1)S(1)}, u32[]{:S(2)}, u32[]{:S(2)}) collective-permute-start(bf16[8,16384]{1,0:T(8,128)(2,1)S(1)} %get-tuple-element.20), channel_id=1, source_target_pairs={{0,2},{1,3},{2,0},{3,1},{4,6},{5,7},{6,4},{7,5},{8,10},{9,11},{10,... | collective-permute-start | bytes 786440 | tf_op jit(solution)/shard_map/ppermute | solution.py:323
  23.3 2.3 %copy-start.2 = (f32[384]{0:T(512)S(1)}, f32[384]{0:T(512)}, u32[]{:S(2)}) copy-start(f32[384]{0:T(512)} %value.1) | copy-start | bytes 4612
  23.3 2.3 %copy-start.3 = (f32[384]{0:T(512)S(1)}, f32[384]{0:T(512)}, u32[]{:S(2)}) copy-start(f32[384]{0:T(512)} %var.1) | copy-start | bytes 4612
  26.7 23.2 %all-to-all-start.1 = ((f32[12,24,128]{2,1,0:T(8,128)}), f32[12,24,128]{2,1,0:T(8,128)S(1)}, u32[]{:S(2)}, u32[]{:S(2)}) async-start(f32[12,24,128]{2,1,0:T(8,128)} %gram.1), calls=%async_computation.1 | async-start | bytes 294912 | tf_op jit(solution)/shard_map/all_to_all | solution.py:347
  37.1 20.5 %collective-permute-start.3 = (bf16[8,16384]{1,0:T(8,128)(2,1)S(1)}, bf16[8,16384]{1,0:T(8,128)(2,1)S(1)}, u32[]{:S(2)}, u32[]{:S(2)}) collective-permute-start(bf16[8,16384]{1,0:T(8,128)(2,1)S(1)} %get-tuple-element.20), channel_id=1, source_target_pairs={{0,6},{1,7},{2,4},{3,5},{4,2},{5,3},{6,0},{7,1},{8,14},{9,15},{10,... | collective-permute-start | bytes 786440 | tf_op jit(solution)/shard_map/ppermute | solution.py:323
  40.0 17.7 %collective-permute-start.4 = (bf16[8,16384]{1,0:T(8,128)(2,1)S(1)}, bf16[8,16384]{1,0:T(8,128)(2,1)S(1)}, u32[]{:S(2)}, u32[]{:S(2)}) collective-permute-start(bf16[8,16384]{1,0:T(8,128)(2,1)S(1)} %collective-permute-done.2), channel_id=1, source_target_pairs={{0,6},{1,7},{2,4},{3,5},{4,2},{5,3},{6,0},{7,1},{8,14},{9,15},{10,... | collective-permute-start | bytes 786440 | tf_op jit(solution)/shard_map/ppermute | solution.py:323
  43.0 24.0 %collective-permute-start.5 = (bf16[16,16384]{1,0:T(8,128)(2,1)S(1)}, bf16[16,16384]{1,0:T(8,128)(2,1)S(1)}, u32[]{:S(2)}, u32[]{:S(2)}) collective-permute-start(bf16[16,16384]{1,0:T(8,128)(2,1)S(1)} %constant_dynamic-update-slice_fusion.refs_0_), channel_id=1, source_target_pairs={{0,1},{1,0},{2,3},{3,2},{4,5},{5,4},{6,7},{7,6},{8,9},{9,8},{10,11... | collective-permute-start | bytes 1572872 | tf_op jit(solution)/shard_map/ppermute | solution.py:323
  50.5 16.5 %all-to-all-start.2 = ((f32[8,40,128]{2,1,0:T(8,128)}), f32[8,40,128]{2,1,0:T(8,128)S(1)}, u32[]{:S(2)}, u32[]{:S(2)}) async-start(f32[8,40,128]{2,1,0:T(8,128)} %row_sum.1), calls=%async_computation.2 | async-start | bytes 327680 | tf_op jit(solution)/shard_map/all_to_all | solution.py:351
  57.6 9.4 %collective-permute-start.6 = (bf16[8,16384]{1,0:T(8,128)(2,1)S(1)}, bf16[8,16384]{1,0:T(8,128)(2,1)S(1)}, u32[]{:S(2)}, u32[]{:S(2)}) collective-permute-start(bf16[8,16384]{1,0:T(8,128)(2,1)S(1)} %collective-permute-done.3.refs_1_), channel_id=1, source_target_pairs={{0,1},{1,0},{2,3},{3,2},{4,5},{5,4},{6,7},{7,6},{8,9},{9,8},{10,11... | collective-permute-start | bytes 786440 | tf_op jit(solution)/shard_map/ppermute | solution.py:323
  59.6 7.5 %collective-permute-start.7 = (bf16[8,16384]{1,0:T(8,128)(2,1)S(1)}, bf16[8,16384]{1,0:T(8,128)(2,1)S(1)}, u32[]{:S(2)}, u32[]{:S(2)}) collective-permute-start(bf16[8,16384]{1,0:T(8,128)(2,1)S(1)} %collective-permute-done.4.refs_2_), channel_id=1, source_target_pairs={{0,1},{1,0},{2,3},{3,2},{4,5},{5,4},{6,7},{7,6},{8,9},{9,8},{10,11... | collective-permute-start | bytes 786440 | tf_op jit(solution)/shard_map/ppermute | solution.py:323

commit v6 on v5

--- a/solution.py
+++ b/solution.py
@@ -47,21 +47,14 @@
 
 
 def inner_kernel(
-    columns, field_hbm, courant_hbm, spreading_hbm, col, lev, fields, readings, edges,
-    field, courant, spreading, cells, sems,
+    columns, field, leftward, rightward, col, lev, fields, readings, edges, cells
 ):
-    sources = ((field_hbm, field), (courant_hbm, courant), (spreading_hbm, spreading))
-    fetches = [pltpu.make_async_copy(s, d, sems.at[i]) for i, (s, d) in enumerate(sources)]
-    for fetch in fetches:
-        fetch.start()
     members = fields.shape[0]
     layers = field.shape[1]
     observations = col.shape[0]
     lane = lax.broadcasted_iota(jnp.int32, (members, layers), 1)
     chosen = chosen_levels(lev, layers)
     where_col = jnp.broadcast_to(col[...].reshape(1, -1), (members, observations))
-    for fetch in fetches:
-        fetch.wait()
 
     def column(i):
         if i < 0 or i >= columns:
@@ -73,10 +66,12 @@
         right = column(i + 1)
         below = jnp.where(lane == 0, 0.0, pltpu.roll(centre, 1, 1))
         above = jnp.where(lane == layers - 1, 0.0, pltpu.roll(centre, layers - 1, 1))
+        from_left, from_right = leftward[pl.ds(i, 1), :], rightward[pl.ds(i, 1), :]
         value = (
             centre
-            + courant[pl.ds(i, 1), :] * (left - right) * 0.5
-            + spreading[pl.ds(i, 1), :] * (right + left + above + below - 4.0 * centre)
+            + from_left * left
+            + from_right * right
+            + 0.5 * (from_left + from_right) * (above + below - 4.0 * centre)
         )
         cells[i * members : (i + 1) * members, :] = value
         fields[:, i * layers : (i + 1) * layers] = value.astype(jnp.bfloat16)
@@ -86,8 +81,8 @@
     spread = lambda row: jnp.broadcast_to(row, (members, layers))
     edges[0] = cells[:members, :]
     edges[1] = cells[last * members :, :]
-    edges[2] = spread(spreading[:1, :] + courant[:1, :] * 0.5)
-    edges[3] = spread(spreading[last:, :] - courant[last:, :] * 0.5)
+    edges[2] = spread(leftward[:1, :])
+    edges[3] = spread(rightward[last:, :])
 
     step = 16
     total = jnp.zeros((members, observations), jnp.float32)
@@ -100,10 +95,9 @@
     readings[...] = total
 
 
-def inner_forecast(field, courant, spreading, col, lev):
+def inner_forecast(field, leftward, rightward, col, lev):
     members, columns, layers = field.shape
     observations = col.shape[0]
-    anywhere = pl.BlockSpec(memory_space=pltpu.HBM)
     return pl.pallas_call(
         functools.partial(inner_kernel, columns),
         out_shape=(
@@ -111,14 +105,10 @@
             jax.ShapeDtypeStruct((members, observations), jnp.float32),
             jax.ShapeDtypeStruct((4, members, layers), jnp.float32),
         ),
-        in_specs=[anywhere] * 3 + [VMEM] * 2,
+        in_specs=[VMEM] * 5,
         out_specs=(VMEM, VMEM, VMEM),
         scratch_shapes=[
             pltpu.VMEM((members * columns, layers), jnp.float32),
-            pltpu.VMEM((columns, layers), jnp.float32),
-            pltpu.VMEM((columns, layers), jnp.float32),
-            pltpu.VMEM((members * columns, layers), jnp.float32),
-            pltpu.SemaphoreType.DMA((3,)),
         ],
         compiler_params=SMALL,
         cost_estimate=pl.CostEstimate(
@@ -127,7 +117,7 @@
             transcendentals=0,
         ),
         name="inner_forecast",
-    )(field.reshape(members * columns, layers), courant, spreading, col, lev)
+    )(field.reshape(members * columns, layers), leftward, rightward, col, lev)
 
 
 def edge_kernel(columns, edges, low, high, readings, col, lev, fields_in, fields, copies):
@@ -253,8 +243,7 @@
     )(parts)
 
 
-def analysis_kernel(members, iters, parts, *refs):
-    *fields, out, cells = refs
+def mix_kernel(members, iters, count, parts, mix):
     total = parts[0]
     for r in range(1, parts.shape[0]):
         total = total + parts[r]
@@ -290,8 +279,13 @@
     centre = jnp.sum(tfm, axis=1, keepdims=True) * (1.0 / members)
     mixed = 1.0 / members + tfm - centre
 
+    mix[...] = mixed[:count, :].astype(jnp.bfloat16)
+
+
+def analysis_kernel(mix, *refs):
+    *fields, out, cells = refs
     count, columns, layers = out.shape
-    mine = mixed[:count, :].astype(jnp.bfloat16)
+    mine = mix[...]
     step = 16
     for base in range(0, columns, step):
         held = [part[:, base * layers : (base + step) * layers] for part in fields]
@@ -308,15 +302,23 @@
 def analysis(parts, fields, shape):
     members = sum(part.shape[0] for part in fields)
     count, columns, layers = shape
-    return pl.pallas_call(
-        functools.partial(analysis_kernel, members, NSITER),
+    mix = pl.pallas_call(
+        functools.partial(mix_kernel, members, NSITER, count),
+        out_shape=jax.ShapeDtypeStruct((count, members), jnp.bfloat16),
+        in_specs=[VMEM],
+        out_specs=VMEM,
+        compiler_params=SMALL,
+        name="mix",
+    )(parts)
+    return pl.pallas_call(
+        analysis_kernel,
         out_shape=jax.ShapeDtypeStruct(shape, jnp.bfloat16),
         in_specs=[VMEM] * (1 + len(fields)),
         out_specs=VMEM,
         scratch_shapes=[pltpu.VMEM((count * columns, layers), jnp.float32)],
         compiler_params=SMALL,
         name="analysis",
-    )(parts, *fields)
+    )(mix, *fields)
 
 
 def swapped(block, code):
@@ -330,7 +332,11 @@
     mems, cols, rows = (lax.axis_size(a) for a in ("mem", "col", "row"))
     low, high = neighbours(background_fields, ("row", "col"))
     fields, hx, edges = inner_forecast(
-        background_fields, wind_courant, spreading_number, obs_col, obs_lev
+        background_fields,
+        spreading_number + wind_courant * 0.5,
+        spreading_number - wind_courant * 0.5,
+        obs_col,
+        obs_lev,
     )
     fields, copies = edge_forecast(
         columns, edges, low, high, hx, obs_col, obs_lev, fields, mems

time: 72.5 us -> 72.5 us (level)
  local copies, waits for them, and re-layouts: 3.56 us -> 2.55 us
  other arithmetic: 0 us -> 0.89 us
    unnamed x15 -> x11, local copies, waits for them, and re-layouts: 2.76 us -> 1.75 us
    sub x0 -> x1, other arithmetic: none -> 0.89 us  [on_device(): spreading_number - wind_courant * 0.5]
    pallas_call x1 -> x2, Pallas kernels: 4.66 us -> 4.65 us  [the longest x1 3.4 us: analysis(): pl.pallas_call(functools.partial(mix_kernel, members, NSITER, count), out...]
  transfers between devices with their start and end apart: 11 -> 11, of which waited for: 4 -> 4; matrix products, arithmetic and copies ran while one was open for 0% -> 1% of each run, Pallas kernels for 4% -> 9%
where the time goes in v6:
time: 72.5 us; the launch traced here: 71.7 us
  starting transfers between devices  46.7 us (64%)
  waiting for transfers between devices  13.1 us (18%)
  Pallas kernels  8.24 us (11%)
  local copies, waits for them, and re-layouts  2.55 us (4%)
  other arithmetic  0.89 us (1%)
    ppermute x6, starting transfers between devices, swapped(): lax.ppermute(block, 'mem', [(i, i ^ code) for i in range(lax.axis_size('m...  14.1 us
    all_to_all x1, starting transfers between devices, on_device(): parts = lax.all_to_all(parts, 'col', 0, 0)  10.4 us
    all_to_all x1, starting transfers between devices, on_device(): readings = lax.all_to_all(copies, 'mem', 0, 0)  9.47 us
    all_to_all x1, starting transfers between devices, on_device(): parts = lax.all_to_all(parts, 'row', 0, 0)  7.1 us
    all_to_all x1, waiting for transfers between devices, on_device(): parts = lax.all_to_all(parts, 'row', 0, 0)  5.07 us
    all_to_all x1, waiting for transfers between devices, on_device(): parts = lax.all_to_all(parts, 'col', 0, 0)  4.87 us
    ppermute x1, starting transfers between devices, neighbours(): low = lax.ppermute(block[:, last:, :], axis, forward)  4.26 us
    pallas_call x1, Pallas kernels, analysis(): pl.pallas_call(functools.partial(mix_kernel, members, NSITER, count), out...  3.4 us
  transfers between devices with their start and end apart: 11, of which 4 were waited for; matrix products, arithmetic and copies ran while one was open for 1% of the time, Pallas kernels for 9%

profile of v6, /device:TPU:2, one launch (start us, length us, event | category | flops | bytes accessed | tf_op | source)
XLA Modules:
  0.0 71.7 jit_solution(14685425420705672418)
XLA Ops:
  0.0 0.8 %fusion = (f32[8,1,128]{2,1,0:T(1,128)S(1)}, f32[8,1,128]{2,1,0:T(1,128)S(1)}) fusion(f32[8,128,128]{2,1,0:T(8,128)} %param.7), kind=kLoop, calls=%fused_computation.4 | loop fusion | bytes 16384 | tf_op jit(solution)/shard_map/slice | solution.py:30
  0.8 4.3 %collective-permute-start = (f32[8,1,128]{2,0,1:T(8,128)S(1)}, f32[8,1,128]{2,0,1:T(8,128)S(1)}, u32[]{:S(2)}, u32[]{:S(2)}) collective-permute-start(f32[8,1,128]{2,0,1:T(8,128)S(1)} %bitcast.10), channel_id=1, source_target_pairs={{0,8},{8,16},{16,24},{24,32},{32,40},{40,48},{48,56},{56,64},{64,7... | collective-permute-start | bytes 12296 | tf_op jit(solution)/shard_map/ppermute | solution.py:29
  5.1 1.3 %collective-permute-start.1 = (f32[8,1,128]{2,0,1:T(8,128)S(1)}, f32[8,1,128]{2,0,1:T(8,128)S(1)}, u32[]{:S(2)}, u32[]{:S(2)}) collective-permute-start(f32[8,1,128]{2,0,1:T(8,128)S(1)} %bitcast.9), channel_id=1, source_target_pairs={{8,0},{16,8},{24,16},{32,24},{40,32},{48,40},{56,48},{64,56},{72,6... | collective-permute-start | bytes 12296 | tf_op jit(solution)/shard_map/ppermute | solution.py:30
  6.4 0.0 copy-start.1
  6.4 0.9 %multiply_subtract_fusion = (f32[128,128]{1,0:T(8,128)S(1)}, f32[128,128]{1,0:T(8,128)S(1)}) fusion(f32[128,128]{1,0:T(8,128)} %param.9, f32[128,128]{1,0:T(8,128)} %param.8), kind=kLoop, calls=%fused_computation | loop fusion | flops 49152 | bytes 262144 | tf_op jit(solution)/shard_map/sub | solution.py:337
  7.3 0.0 copy-start
  7.3 0.7 copy-done
  7.9 1.0 %copy-done.4 = f32[8,128,128]{2,1,0:T(8,128)S(1)} copy-done((f32[8,128,128]{2,1,0:T(8,128)S(1)}, f32[8,128,128]{2,1,0:T(8,128)}, u32[]{:S(2)}) %copy-start.4) | copy-done | bytes 524312
  9.0 1.0 %inner_forecast.1 = (bf16[8,16384]{1,0:T(8,128)(2,1)S(1)}, f32[8,384]{1,0:T(8,128)S(1)}, f32[4,8,128]{2,1,0:T(8,128)S(1)}) custom-call(f32[1024,128]{1,0:T(8,128)S(1)} %bitcast.8, f32[128,128]{1,0:T(8,128)S(1)} %get-tuple-element.26.leftward, f32[128,128]{1,0:T(8,128)S(1)} %get-tuple-element.25.rightward, s32[384]{0:T(512)S(1)} %copy-done, s32[384]{0:T(512)S(1)} %copy-done.1), custom_call_target="tpu_custom_call" | custom-call | flops 301989888 | bytes 524288 | tf_op jit(solution)/shard_map/inner_forecast/pallas_call | solution.py:101
  10.0 0.0 collective-permute-done
  10.0 0.9 %collective-permute-done.1 = f32[8,1,128]{2,0,1:T(8,128)S(1)} collective-permute-done((f32[8,1,128]{2,0,1:T(8,128)S(1)}, f32[8,1,128]{2,0,1:T(8,128)S(1)}, u32[]{:S(2)}, u32[]{:S(2)}) %collective-permute-start.1) | collective-permute-done | bytes 4128 | tf_op jit(solution)/shard_map/ppermute | solution.py:30
  10.9 0.8 %edge_forecast.1 = (bf16[8,16384]{1,0:T(8,128)(2,1)S(1)}, f32[8,8,384]{2,1,0:T(8,128)}) custom-call(f32[4,8,128]{2,1,0:T(8,128)S(1)} %get-tuple-element.14.edges, f32[8,128]{1,0:T(8,128)S(1)} %bitcast.6, f32[8,128]{1,0:T(8,128)S(1)} %bitcast.7, f32[8,384]{1,0:T(8,128)S(1)} %get-tuple-element.15.readings, ...), custom_call_target="tpu_custom_call", output_to_operand_aliasing={{0}: (6, {})} | custom-call | tf_op jit(solution)/shard_map/edge_forecast/pallas_call | solution.py:140
  11.7 9.5 %all-to-all-start = ((f32[8,8,384]{2,1,0:T(8,128)}), f32[8,8,384]{2,1,0:T(8,128)S(1)}, u32[]{:S(2)}, u32[]{:S(2)}) async-start(f32[8,8,384]{2,1,0:T(8,128)} %get-tuple-element.17), calls=%async_computation | async-start | bytes 196608 | tf_op jit(solution)/shard_map/all_to_all | solution.py:344
  21.2 2.0 %collective-permute-start.2 = (bf16[8,16384]{1,0:T(8,128)(2,1)S(1)}, bf16[8,16384]{1,0:T(8,128)(2,1)S(1)}, u32[]{:S(2)}, u32[]{:S(2)}) collective-permute-start(bf16[8,16384]{1,0:T(8,128)(2,1)S(1)} %get-tuple-element.20), channel_id=1, source_target_pairs={{0,2},{1,3},{2,0},{3,1},{4,6},{5,7},{6,4},{7,5},{8,10},{9,11},{10,... | collective-permute-start | bytes 786440 | tf_op jit(solution)/shard_map/ppermute | solution.py:325
  23.2 0.0 copy-start.2
  23.3 0.0 copy-start.3
  23.3 2.3 %all-to-all-done.readings = f32[8,8,384]{2,1,0:T(8,128)S(1)} async-done(((f32[8,8,384]{2,1,0:T(8,128)}), f32[8,8,384]{2,1,0:T(8,128)S(1)}, u32[]{:S(2)}, u32[]{:S(2)}) %all-to-all-start) | async-done | bytes 98336 | tf_op jit(solution)/shard_map/all_to_all | solution.py:344
  25.6 1.1 %gram.1 = f32[12,24,128]{2,1,0:T(8,128)} custom-call(s32[1]{0:T(128)} %bitcast.me, f32[8,8,384]{2,1,0:T(8,128)S(1)} %all-to-all-done.readings, f32[384]{0:T(512)S(1)} %copy-done.2, f32[384]{0:T(512)S(1)} %copy-done.3), custom_call_target="tpu_custom_call" | custom-call | tf_op jit(solution)/shard_map/gram/pallas_call | solution.py:214
  26.7 10.4 %all-to-all-start.1 = ((f32[12,24,128]{2,1,0:T(8,128)}), f32[12,24,128]{2,1,0:T(8,128)S(1)}, u32[]{:S(2)}, u32[]{:S(2)}) async-start(f32[12,24,128]{2,1,0:T(8,128)} %gram.1), calls=%async_computation.1 | async-start | bytes 294912 | tf_op jit(solution)/shard_map/all_to_all | solution.py:353
  37.1 2.8 %collective-permute-start.3 = (bf16[8,16384]{1,0:T(8,128)(2,1)S(1)}, bf16[8,16384]{1,0:T(8,128)(2,1)S(1)}, u32[]{:S(2)}, u32[]{:S(2)}) collective-permute-start(bf16[8,16384]{1,0:T(8,128)(2,1)S(1)} %get-tuple-element.20), channel_id=1, source_target_pairs={{0,6},{1,7},{2,4},{3,5},{4,2},{5,3},{6,0},{7,1},{8,14},{9,15},{10,... | collective-permute-start | bytes 786440 | tf_op jit(solution)/shard_map/ppermute | solution.py:325
  39.9 3.0 %collective-permute-start.4 = (bf16[8,16384]{1,0:T(8,128)(2,1)S(1)}, bf16[8,16384]{1,0:T(8,128)(2,1)S(1)}, u32[]{:S(2)}, u32[]{:S(2)}) collective-permute-start(bf16[8,16384]{1,0:T(8,128)(2,1)S(1)} %collective-permute-done.2), channel_id=1, source_target_pairs={{0,6},{1,7},{2,4},{3,5},{4,2},{5,3},{6,0},{7,1},{8,14},{9,15},{10,... | collective-permute-start | bytes 786440 | tf_op jit(solution)/shard_map/ppermute | solution.py:325
  43.0 1.9 %collective-permute-start.5 = (bf16[16,16384]{1,0:T(8,128)(2,1)S(1)}, bf16[16,16384]{1,0:T(8,128)(2,1)S(1)}, u32[]{:S(2)}, u32[]{:S(2)}) collective-permute-start(bf16[16,16384]{1,0:T(8,128)(2,1)S(1)} %constant_dynamic-update-slice_fusion.refs_0_), channel_id=1, source_target_pairs={{0,1},{1,0},{2,3},{3,2},{4,5},{5,4},{6,7},{7,6},{8,9},{9,8},{10,11... | collective-permute-start | bytes 1572872 | tf_op jit(solution)/shard_map/ppermute | solution.py:325
  44.9 4.9 %all-to-all-done.1.parts = f32[12,24,128]{2,1,0:T(8,128)S(1)} async-done(((f32[12,24,128]{2,1,0:T(8,128)}), f32[12,24,128]{2,1,0:T(8,128)S(1)}, u32[]{:S(2)}, u32[]{:S(2)}) %all-to-all-start.1) | async-done | bytes 147488 | tf_op jit(solution)/shard_map/all_to_all | solution.py:353
  49.8 0.7 row_sum.1
  50.5 7.1 %all-to-all-start.2 = ((f32[8,40,128]{2,1,0:T(8,128)}), f32[8,40,128]{2,1,0:T(8,128)S(1)}, u32[]{:S(2)}, u32[]{:S(2)}) async-start(f32[8,40,128]{2,1,0:T(8,128)} %row_sum.1), calls=%async_computation.2 | async-start | bytes 327680 | tf_op jit(solution)/shard_map/all_to_all | solution.py:357
  57.6 0.0 collective-permute-done.4.refs_2_
  57.6 1.9 %collective-permute-start.6 = (bf16[8,16384]{1,0:T(8,128)(2,1)S(1)}, bf16[8,16384]{1,0:T(8,128)(2,1)S(1)}, u32[]{:S(2)}, u32[]{:S(2)}) collective-permute-start(bf16[8,16384]{1,0:T(8,128)(2,1)S(1)} %collective-permute-done.3.refs_1_), channel_id=1, source_target_pairs={{0,1},{1,0},{2,3},{3,2},{4,5},{5,4},{6,7},{7,6},{8,9},{9,8},{10,11... | collective-permute-start | bytes 786440 | tf_op jit(solution)/shard_map/ppermute | solution.py:325
  59.5 2.4 %collective-permute-start.7 = (bf16[8,16384]{1,0:T(8,128)(2,1)S(1)}, bf16[8,16384]{1,0:T(8,128)(2,1)S(1)}, u32[]{:S(2)}, u32[]{:S(2)}) collective-permute-start(bf16[8,16384]{1,0:T(8,128)(2,1)S(1)} %collective-permute-done.4.refs_2_), channel_id=1, source_target_pairs={{0,1},{1,0},{2,3},{3,2},{4,5},{5,4},{6,7},{7,6},{8,9},{9,8},{10,11... | collective-permute-start | bytes 786440 | tf_op jit(solution)/shard_map/ppermute | solution.py:325
  62.0 5.1 %all-to-all-done.2.parts = f32[8,40,128]{2,1,0:T(8,128)S(1)} async-done(((f32[8,40,128]{2,1,0:T(8,128)}), f32[8,40,128]{2,1,0:T(8,128)S(1)}, u32[]{:S(2)}, u32[]{:S(2)}) %all-to-all-start.2) | async-done | bytes 163872 | tf_op jit(solution)/shard_map/all_to_all | solution.py:357
  67.0 3.4 %mix.1 = bf16[8,64]{1,0:T(8,128)(2,1)S(1)} custom-call(f32[8,40,128]{2,1,0:T(8,128)S(1)} %all-to-all-done.2.parts), custom_call_target="tpu_custom_call" | custom-call | tf_op jit(solution)/shard_map/mix/pallas_call | solution.py:305
  70.4 0.0 collective-permute-done.5.refs_3_
  70.5 1.3 %analysis.1 = bf16[8,128,128]{2,1,0:T(8,128)(2,1)} custom-call(bf16[8,64]{1,0:T(8,128)(2,1)S(1)} %mix.1, bf16[16,16384]{1,0:T(8,128)(2,1)S(1)} %constant_dynamic-update-slice_fusion.refs_0_, bf16[8,16384]{1,0:T(8,128)(2,1)S(1)} %collective-permute-done.3.refs_1_, bf16[8,16384]{1,0:T(8,128)(2,1)S(1)} %collective-permute-done.4.refs_2_, ...), custom_call_target="tpu_custom_call" | custom-call | tf_op jit(solution)/shard_map/analysis/pallas_call | solution.py:313
  (10 shorter events, 0.1 us)
Async XLA Ops:
  0.8 9.2 %collective-permute-start = (f32[8,1,128]{2,0,1:T(8,128)S(1)}, f32[8,1,128]{2,0,1:T(8,128)S(1)}, u32[]{:S(2)}, u32[]{:S(2)}) collective-permute-start(f32[8,1,128]{2,0,1:T(8,128)S(1)} %bitcast.10), channel_id=1, source_target_pairs={{0,8},{8,16},{16,24},{24,32},{32,40},{40,48},{48,56},{56,64},{64,7... | collective-permute-start | bytes 12296 | tf_op jit(solution)/shard_map/ppermute | solution.py:29
  5.1 5.9 %collective-permute-start.1 = (f32[8,1,128]{2,0,1:T(8,128)S(1)}, f32[8,1,128]{2,0,1:T(8,128)S(1)}, u32[]{:S(2)}, u32[]{:S(2)}) collective-permute-start(f32[8,1,128]{2,0,1:T(8,128)S(1)} %bitcast.9), channel_id=1, source_target_pairs={{8,0},{16,8},{24,16},{32,24},{40,32},{48,40},{56,48},{64,56},{72,6... | collective-permute-start | bytes 12296 | tf_op jit(solution)/shard_map/ppermute | solution.py:30
  6.4 0.9 %copy-start.1 = (s32[384]{0:T(512)S(1)}, s32[384]{0:T(512)}, u32[]{:S(2)}) copy-start(s32[384]{0:T(512)} %lev.3) | copy-start | bytes 4612
  7.3 0.7 copy-start
  7.9 1.0 %copy-start.4 = (f32[8,128,128]{2,1,0:T(8,128)S(1)}, f32[8,128,128]{2,1,0:T(8,128)}, u32[]{:S(2)}) copy-start(f32[8,128,128]{2,1,0:T(8,128)} %param.7) | copy-start | bytes 1572868
  11.7 13.8 %all-to-all-start = ((f32[8,8,384]{2,1,0:T(8,128)}), f32[8,8,384]{2,1,0:T(8,128)S(1)}, u32[]{:S(2)}, u32[]{:S(2)}) async-start(f32[8,8,384]{2,1,0:T(8,128)} %get-tuple-element.17), calls=%async_computation | async-start | bytes 196608 | tf_op jit(solution)/shard_map/all_to_all | solution.py:344
  21.2 18.7 %collective-permute-start.2 = (bf16[8,16384]{1,0:T(8,128)(2,1)S(1)}, bf16[8,16384]{1,0:T(8,128)(2,1)S(1)}, u32[]{:S(2)}, u32[]{:S(2)}) collective-permute-start(bf16[8,16384]{1,0:T(8,128)(2,1)S(1)} %get-tuple-element.20), channel_id=1, source_target_pairs={{0,2},{1,3},{2,0},{3,1},{4,6},{5,7},{6,4},{7,5},{8,10},{9,11},{10,... | collective-permute-start | bytes 786440 | tf_op jit(solution)/shard_map/ppermute | solution.py:325
  23.2 2.3 %copy-start.2 = (f32[384]{0:T(512)S(1)}, f32[384]{0:T(512)}, u32[]{:S(2)}) copy-start(f32[384]{0:T(512)} %value.1) | copy-start | bytes 4612
  23.3 2.3 %copy-start.3 = (f32[384]{0:T(512)S(1)}, f32[384]{0:T(512)}, u32[]{:S(2)}) copy-start(f32[384]{0:T(512)} %var.1) | copy-start | bytes 4612
  26.7 23.2 %all-to-all-start.1 = ((f32[12,24,128]{2,1,0:T(8,128)}), f32[12,24,128]{2,1,0:T(8,128)S(1)}, u32[]{:S(2)}, u32[]{:S(2)}) async-start(f32[12,24,128]{2,1,0:T(8,128)} %gram.1), calls=%async_computation.1 | async-start | bytes 294912 | tf_op jit(solution)/shard_map/all_to_all | solution.py:353
  37.1 20.5 %collective-permute-start.3 = (bf16[8,16384]{1,0:T(8,128)(2,1)S(1)}, bf16[8,16384]{1,0:T(8,128)(2,1)S(1)}, u32[]{:S(2)}, u32[]{:S(2)}) collective-permute-start(bf16[8,16384]{1,0:T(8,128)(2,1)S(1)} %get-tuple-element.20), channel_id=1, source_target_pairs={{0,6},{1,7},{2,4},{3,5},{4,2},{5,3},{6,0},{7,1},{8,14},{9,15},{10,... | collective-permute-start | bytes 786440 | tf_op jit(solution)/shard_map/ppermute | solution.py:325
  39.9 17.7 %collective-permute-start.4 = (bf16[8,16384]{1,0:T(8,128)(2,1)S(1)}, bf16[8,16384]{1,0:T(8,128)(2,1)S(1)}, u32[]{:S(2)}, u32[]{:S(2)}) collective-permute-start(bf16[8,16384]{1,0:T(8,128)(2,1)S(1)} %collective-permute-done.2), channel_id=1, source_target_pairs={{0,6},{1,7},{2,4},{3,5},{4,2},{5,3},{6,0},{7,1},{8,14},{9,15},{10,... | collective-permute-start | bytes 786440 | tf_op jit(solution)/shard_map/ppermute | solution.py:325
  43.0 27.4 %collective-permute-start.5 = (bf16[16,16384]{1,0:T(8,128)(2,1)S(1)}, bf16[16,16384]{1,0:T(8,128)(2,1)S(1)}, u32[]{:S(2)}, u32[]{:S(2)}) collective-permute-start(bf16[16,16384]{1,0:T(8,128)(2,1)S(1)} %constant_dynamic-update-slice_fusion.refs_0_), channel_id=1, source_target_pairs={{0,1},{1,0},{2,3},{3,2},{4,5},{5,4},{6,7},{7,6},{8,9},{9,8},{10,11... | collective-permute-start | bytes 1572872 | tf_op jit(solution)/shard_map/ppermute | solution.py:325
  50.5 16.5 %all-to-all-start.2 = ((f32[8,40,128]{2,1,0:T(8,128)}), f32[8,40,128]{2,1,0:T(8,128)S(1)}, u32[]{:S(2)}, u32[]{:S(2)}) async-start(f32[8,40,128]{2,1,0:T(8,128)} %row_sum.1), calls=%async_computation.2 | async-start | bytes 327680 | tf_op jit(solution)/shard_map/all_to_all | solution.py:357
  57.6 12.8 %collective-permute-start.6 = (bf16[8,16384]{1,0:T(8,128)(2,1)S(1)}, bf16[8,16384]{1,0:T(8,128)(2,1)S(1)}, u32[]{:S(2)}, u32[]{:S(2)}) collective-permute-start(bf16[8,16384]{1,0:T(8,128)(2,1)S(1)} %collective-permute-done.3.refs_1_), channel_id=1, source_target_pairs={{0,1},{1,0},{2,3},{3,2},{4,5},{5,4},{6,7},{7,6},{8,9},{9,8},{10,11... | collective-permute-start | bytes 786440 | tf_op jit(solution)/shard_map/ppermute | solution.py:325
  59.5 10.9 %collective-permute-start.7 = (bf16[8,16384]{1,0:T(8,128)(2,1)S(1)}, bf16[8,16384]{1,0:T(8,128)(2,1)S(1)}, u32[]{:S(2)}, u32[]{:S(2)}) collective-permute-start(bf16[8,16384]{1,0:T(8,128)(2,1)S(1)} %collective-permute-done.4.refs_2_), channel_id=1, source_target_pairs={{0,1},{1,0},{2,3},{3,2},{4,5},{5,4},{6,7},{7,6},{8,9},{9,8},{10,11... | collective-permute-start | bytes 786440 | tf_op jit(solution)/shard_map/ppermute | solution.py:325

commit v7 on v6

--- a/solution.py
+++ b/solution.py
@@ -8,6 +8,7 @@
 from jax.sharding import Mesh, PartitionSpec as P
 
 NSITER = 8
+PIECES = 4
 ROWS = 8
 LANES = 128
 GROUP = 8
@@ -283,20 +284,33 @@
 
 
 def analysis_kernel(mix, *refs):
-    *fields, out, cells = refs
+    *fields, out, cells, stage, sems = refs
     count, columns, layers = out.shape
     mine = mix[...]
     step = 16
-    for base in range(0, columns, step):
-        held = [part[:, base * layers : (base + step) * layers] for part in fields]
-        block = jnp.dot(
-            mine, jnp.concatenate(held, axis=0), preferred_element_type=jnp.float32
+    width = columns // PIECES
+    writes = []
+    for piece in range(PIECES):
+        first = piece * width
+        for base in range(first, first + width, step):
+            held = [part[:, base * layers : (base + step) * layers] for part in fields]
+            block = jnp.dot(
+                mine, jnp.concatenate(held, axis=0), preferred_element_type=jnp.float32
+            )
+            for i in range(step):
+                cells[pl.ds(base + i, count, stride=columns), :] = block[
+                    :, i * layers : (i + 1) * layers
+                ]
+        for m in range(count):
+            low = m * columns + first
+            stage[m, first : first + width, :] = cells[low : low + width, :].astype(jnp.bfloat16)
+        window = pl.ds(first, width)
+        writes.append(
+            pltpu.make_async_copy(stage.at[:, window, :], out.at[:, window, :], sems.at[piece])
         )
-        for i in range(step):
-            cells[pl.ds(base + i, count, stride=columns), :] = block[
-                :, i * layers : (i + 1) * layers
-            ]
-    out[...] = cells[...].astype(jnp.bfloat16).reshape(out.shape)
+        writes[-1].start()
+    for write in writes:
+        write.wait()
 
 
 def analysis(parts, fields, shape):
@@ -314,8 +328,12 @@
         analysis_kernel,
         out_shape=jax.ShapeDtypeStruct(shape, jnp.bfloat16),
         in_specs=[VMEM] * (1 + len(fields)),
-        out_specs=VMEM,
-        scratch_shapes=[pltpu.VMEM((count * columns, layers), jnp.float32)],
+        out_specs=pl.BlockSpec(memory_space=pl.ANY),
+        scratch_shapes=[
+            pltpu.VMEM((count * columns, layers), jnp.float32),
+            pltpu.VMEM(shape, jnp.bfloat16),
+            pltpu.SemaphoreType.DMA((PIECES,)),
+        ],
         compiler_params=SMALL,
         name="analysis",
     )(mix, *fields)

time: 72.5 us -> 72.4 us (level)
  no operation moved by 1% of the time
where the time goes in v7:
time: 72.4 us; the launch traced here: 71.7 us
  starting transfers between devices  46.7 us (65%)
  waiting for transfers between devices  13.1 us (18%)
  Pallas kernels  8.2 us (11%)
  local copies, waits for them, and re-layouts  2.55 us (4%)
  other arithmetic  0.89 us (1%)
    ppermute x6, starting transfers between devices, swapped(): lax.ppermute(block, 'mem', [(i, i ^ code) for i in range(lax.axis_size('m...  14.1 us
    all_to_all x1, starting transfers between devices, on_device(): parts = lax.all_to_all(parts, 'col', 0, 0)  10.4 us
    all_to_all x1, starting transfers between devices, on_device(): readings = lax.all_to_all(copies, 'mem', 0, 0)  9.47 us
    all_to_all x1, starting transfers between devices, on_device(): parts = lax.all_to_all(parts, 'row', 0, 0)  7.1 us
    all_to_all x1, waiting for transfers between devices, on_device(): parts = lax.all_to_all(parts, 'row', 0, 0)  5.07 us
    all_to_all x1, waiting for transfers between devices, on_device(): parts = lax.all_to_all(parts, 'col', 0, 0)  4.87 us
    ppermute x1, starting transfers between devices, neighbours(): low = lax.ppermute(block[:, last:, :], axis, forward)  4.26 us
    pallas_call x1, Pallas kernels, analysis(): pl.pallas_call(functools.partial(mix_kernel, members, NSITER, count), out...  3.4 us
  transfers between devices with their start and end apart: 11, of which 4 were waited for; matrix products, arithmetic and copies ran while one was open for 1% of the time, Pallas kernels for 9%

profile of v7, /device:TPU:2, one launch (start us, length us, event | category | flops | bytes accessed | tf_op | source)
XLA Modules:
  0.0 71.7 jit_solution(4768905176009792791)
XLA Ops:
  0.0 0.8 %fusion = (f32[8,1,128]{2,1,0:T(1,128)S(1)}, f32[8,1,128]{2,1,0:T(1,128)S(1)}) fusion(f32[8,128,128]{2,1,0:T(8,128)} %param.7), kind=kLoop, calls=%fused_computation.4 | loop fusion | bytes 16384 | tf_op jit(solution)/shard_map/slice | solution.py:31
  0.8 4.3 %collective-permute-start = (f32[8,1,128]{2,0,1:T(8,128)S(1)}, f32[8,1,128]{2,0,1:T(8,128)S(1)}, u32[]{:S(2)}, u32[]{:S(2)}) collective-permute-start(f32[8,1,128]{2,0,1:T(8,128)S(1)} %bitcast.10), channel_id=1, source_target_pairs={{0,8},{8,16},{16,24},{24,32},{32,40},{40,48},{48,56},{56,64},{64,7... | collective-permute-start | bytes 12296 | tf_op jit(solution)/shard_map/ppermute | solution.py:30
  5.1 1.3 %collective-permute-start.1 = (f32[8,1,128]{2,0,1:T(8,128)S(1)}, f32[8,1,128]{2,0,1:T(8,128)S(1)}, u32[]{:S(2)}, u32[]{:S(2)}) collective-permute-start(f32[8,1,128]{2,0,1:T(8,128)S(1)} %bitcast.9), channel_id=1, source_target_pairs={{8,0},{16,8},{24,16},{32,24},{40,32},{48,40},{56,48},{64,56},{72,6... | collective-permute-start | bytes 12296 | tf_op jit(solution)/shard_map/ppermute | solution.py:31
  6.4 0.0 copy-start.1
  6.4 0.9 %multiply_subtract_fusion = (f32[128,128]{1,0:T(8,128)S(1)}, f32[128,128]{1,0:T(8,128)S(1)}) fusion(f32[128,128]{1,0:T(8,128)} %param.9, f32[128,128]{1,0:T(8,128)} %param.8), kind=kLoop, calls=%fused_computation | loop fusion | flops 49152 | bytes 262144 | tf_op jit(solution)/shard_map/sub | solution.py:355
  7.3 0.0 copy-start
  7.3 0.7 copy-done
  7.9 1.0 %copy-done.4 = f32[8,128,128]{2,1,0:T(8,128)S(1)} copy-done((f32[8,128,128]{2,1,0:T(8,128)S(1)}, f32[8,128,128]{2,1,0:T(8,128)}, u32[]{:S(2)}) %copy-start.4) | copy-done | bytes 524312
  9.0 1.0 %inner_forecast.1 = (bf16[8,16384]{1,0:T(8,128)(2,1)S(1)}, f32[8,384]{1,0:T(8,128)S(1)}, f32[4,8,128]{2,1,0:T(8,128)S(1)}) custom-call(f32[1024,128]{1,0:T(8,128)S(1)} %bitcast.8, f32[128,128]{1,0:T(8,128)S(1)} %get-tuple-element.26.leftward, f32[128,128]{1,0:T(8,128)S(1)} %get-tuple-element.25.rightward, s32[384]{0:T(512)S(1)} %copy-done, s32[384]{0:T(512)S(1)} %copy-done.1), custom_call_target="tpu_custom_call" | custom-call | flops 301989888 | bytes 524288 | tf_op jit(solution)/shard_map/inner_forecast/pallas_call | solution.py:102
  10.0 0.9 %collective-permute-done.1 = f32[8,1,128]{2,0,1:T(8,128)S(1)} collective-permute-done((f32[8,1,128]{2,0,1:T(8,128)S(1)}, f32[8,1,128]{2,0,1:T(8,128)S(1)}, u32[]{:S(2)}, u32[]{:S(2)}) %collective-permute-start.1) | collective-permute-done | bytes 4128 | tf_op jit(solution)/shard_map/ppermute | solution.py:31
  10.9 0.8 %edge_forecast.1 = (bf16[8,16384]{1,0:T(8,128)(2,1)S(1)}, f32[8,8,384]{2,1,0:T(8,128)}) custom-call(f32[4,8,128]{2,1,0:T(8,128)S(1)} %get-tuple-element.14.edges, f32[8,128]{1,0:T(8,128)S(1)} %bitcast.6, f32[8,128]{1,0:T(8,128)S(1)} %bitcast.7, f32[8,384]{1,0:T(8,128)S(1)} %get-tuple-element.15.readings, ...), custom_call_target="tpu_custom_call", output_to_operand_aliasing={{0}: (6, {})} | custom-call | tf_op jit(solution)/shard_map/edge_forecast/pallas_call | solution.py:141
  11.7 9.5 %all-to-all-start = ((f32[8,8,384]{2,1,0:T(8,128)}), f32[8,8,384]{2,1,0:T(8,128)S(1)}, u32[]{:S(2)}, u32[]{:S(2)}) async-start(f32[8,8,384]{2,1,0:T(8,128)} %get-tuple-element.17), calls=%async_computation | async-start | bytes 196608 | tf_op jit(solution)/shard_map/all_to_all | solution.py:362
  21.2 2.0 %collective-permute-start.2 = (bf16[8,16384]{1,0:T(8,128)(2,1)S(1)}, bf16[8,16384]{1,0:T(8,128)(2,1)S(1)}, u32[]{:S(2)}, u32[]{:S(2)}) collective-permute-start(bf16[8,16384]{1,0:T(8,128)(2,1)S(1)} %get-tuple-element.20), channel_id=1, source_target_pairs={{0,2},{1,3},{2,0},{3,1},{4,6},{5,7},{6,4},{7,5},{8,10},{9,11},{10,... | collective-permute-start | bytes 786440 | tf_op jit(solution)/shard_map/ppermute | solution.py:343
  23.2 0.0 copy-start.2
  23.3 0.0 copy-start.3
  23.3 2.3 %all-to-all-done.readings = f32[8,8,384]{2,1,0:T(8,128)S(1)} async-done(((f32[8,8,384]{2,1,0:T(8,128)}), f32[8,8,384]{2,1,0:T(8,128)S(1)}, u32[]{:S(2)}, u32[]{:S(2)}) %all-to-all-start) | async-done | bytes 98336 | tf_op jit(solution)/shard_map/all_to_all | solution.py:362
  25.6 1.1 %gram.1 = f32[12,24,128]{2,1,0:T(8,128)} custom-call(s32[1]{0:T(128)} %bitcast.me, f32[8,8,384]{2,1,0:T(8,128)S(1)} %all-to-all-done.readings, f32[384]{0:T(512)S(1)} %copy-done.2, f32[384]{0:T(512)S(1)} %copy-done.3), custom_call_target="tpu_custom_call" | custom-call | tf_op jit(solution)/shard_map/gram/pallas_call | solution.py:215
  26.7 10.4 %all-to-all-start.1 = ((f32[12,24,128]{2,1,0:T(8,128)}), f32[12,24,128]{2,1,0:T(8,128)S(1)}, u32[]{:S(2)}, u32[]{:S(2)}) async-start(f32[12,24,128]{2,1,0:T(8,128)} %gram.1), calls=%async_computation.1 | async-start | bytes 294912 | tf_op jit(solution)/shard_map/all_to_all | solution.py:371
  37.1 2.8 %collective-permute-start.3 = (bf16[8,16384]{1,0:T(8,128)(2,1)S(1)}, bf16[8,16384]{1,0:T(8,128)(2,1)S(1)}, u32[]{:S(2)}, u32[]{:S(2)}) collective-permute-start(bf16[8,16384]{1,0:T(8,128)(2,1)S(1)} %get-tuple-element.20), channel_id=1, source_target_pairs={{0,6},{1,7},{2,4},{3,5},{4,2},{5,3},{6,0},{7,1},{8,14},{9,15},{10,... | collective-permute-start | bytes 786440 | tf_op jit(solution)/shard_map/ppermute | solution.py:343
  39.9 0.0 collective-permute-done.2
  39.9 3.0 %collective-permute-start.4 = (bf16[8,16384]{1,0:T(8,128)(2,1)S(1)}, bf16[8,16384]{1,0:T(8,128)(2,1)S(1)}, u32[]{:S(2)}, u32[]{:S(2)}) collective-permute-start(bf16[8,16384]{1,0:T(8,128)(2,1)S(1)} %collective-permute-done.2), channel_id=1, source_target_pairs={{0,6},{1,7},{2,4},{3,5},{4,2},{5,3},{6,0},{7,1},{8,14},{9,15},{10,... | collective-permute-start | bytes 786440 | tf_op jit(solution)/shard_map/ppermute | solution.py:343
  43.0 1.9 %collective-permute-start.5 = (bf16[16,16384]{1,0:T(8,128)(2,1)S(1)}, bf16[16,16384]{1,0:T(8,128)(2,1)S(1)}, u32[]{:S(2)}, u32[]{:S(2)}) collective-permute-start(bf16[16,16384]{1,0:T(8,128)(2,1)S(1)} %constant_dynamic-update-slice_fusion.refs_0_), channel_id=1, source_target_pairs={{0,1},{1,0},{2,3},{3,2},{4,5},{5,4},{6,7},{7,6},{8,9},{9,8},{10,11... | collective-permute-start | bytes 1572872 | tf_op jit(solution)/shard_map/ppermute | solution.py:343
  44.9 4.9 %all-to-all-done.1.parts = f32[12,24,128]{2,1,0:T(8,128)S(1)} async-done(((f32[12,24,128]{2,1,0:T(8,128)}), f32[12,24,128]{2,1,0:T(8,128)S(1)}, u32[]{:S(2)}, u32[]{:S(2)}) %all-to-all-start.1) | async-done | bytes 147488 | tf_op jit(solution)/shard_map/all_to_all | solution.py:371
  49.8 0.7 row_sum.1
  50.5 7.1 %all-to-all-start.2 = ((f32[8,40,128]{2,1,0:T(8,128)}), f32[8,40,128]{2,1,0:T(8,128)S(1)}, u32[]{:S(2)}, u32[]{:S(2)}) async-start(f32[8,40,128]{2,1,0:T(8,128)} %row_sum.1), calls=%async_computation.2 | async-start | bytes 327680 | tf_op jit(solution)/shard_map/all_to_all | solution.py:375
  57.6 0.0 collective-permute-done.3.refs_1_
  57.6 1.9 %collective-permute-start.6 = (bf16[8,16384]{1,0:T(8,128)(2,1)S(1)}, bf16[8,16384]{1,0:T(8,128)(2,1)S(1)}, u32[]{:S(2)}, u32[]{:S(2)}) collective-permute-start(bf16[8,16384]{1,0:T(8,128)(2,1)S(1)} %collective-permute-done.3.refs_1_), channel_id=1, source_target_pairs={{0,1},{1,0},{2,3},{3,2},{4,5},{5,4},{6,7},{7,6},{8,9},{9,8},{10,11... | collective-permute-start | bytes 786440 | tf_op jit(solution)/shard_map/ppermute | solution.py:343
  59.5 2.4 %collective-permute-start.7 = (bf16[8,16384]{1,0:T(8,128)(2,1)S(1)}, bf16[8,16384]{1,0:T(8,128)(2,1)S(1)}, u32[]{:S(2)}, u32[]{:S(2)}) collective-permute-start(bf16[8,16384]{1,0:T(8,128)(2,1)S(1)} %collective-permute-done.4.refs_2_), channel_id=1, source_target_pairs={{0,1},{1,0},{2,3},{3,2},{4,5},{5,4},{6,7},{7,6},{8,9},{9,8},{10,11... | collective-permute-start | bytes 786440 | tf_op jit(solution)/shard_map/ppermute | solution.py:343
  62.0 5.1 %all-to-all-done.2.parts = f32[8,40,128]{2,1,0:T(8,128)S(1)} async-done(((f32[8,40,128]{2,1,0:T(8,128)}), f32[8,40,128]{2,1,0:T(8,128)S(1)}, u32[]{:S(2)}, u32[]{:S(2)}) %all-to-all-start.2) | async-done | bytes 163872 | tf_op jit(solution)/shard_map/all_to_all | solution.py:375
  67.0 3.4 %mix.1 = bf16[8,64]{1,0:T(8,128)(2,1)S(1)} custom-call(f32[8,40,128]{2,1,0:T(8,128)S(1)} %all-to-all-done.2.parts), custom_call_target="tpu_custom_call" | custom-call | tf_op jit(solution)/shard_map/mix/pallas_call | solution.py:319
  70.4 0.0 collective-permute-done.5.refs_3_
  70.5 1.2 %analysis.1 = bf16[8,128,128]{2,1,0:T(8,128)(2,1)} custom-call(bf16[8,64]{1,0:T(8,128)(2,1)S(1)} %mix.1, bf16[16,16384]{1,0:T(8,128)(2,1)S(1)} %constant_dynamic-update-slice_fusion.refs_0_, bf16[8,16384]{1,0:T(8,128)(2,1)S(1)} %collective-permute-done.3.refs_1_, bf16[8,16384]{1,0:T(8,128)(2,1)S(1)} %collective-permute-done.4.refs_2_, ...), custom_call_target="tpu_custom_call" | custom-call | tf_op jit(solution)/shard_map/analysis/pallas_call | solution.py:327
  (10 shorter events, 0.1 us)
Async XLA Ops:
  0.8 9.2 %collective-permute-start = (f32[8,1,128]{2,0,1:T(8,128)S(1)}, f32[8,1,128]{2,0,1:T(8,128)S(1)}, u32[]{:S(2)}, u32[]{:S(2)}) collective-permute-start(f32[8,1,128]{2,0,1:T(8,128)S(1)} %bitcast.10), channel_id=1, source_target_pairs={{0,8},{8,16},{16,24},{24,32},{32,40},{40,48},{48,56},{56,64},{64,7... | collective-permute-start | bytes 12296 | tf_op jit(solution)/shard_map/ppermute | solution.py:30
  5.1 5.9 %collective-permute-start.1 = (f32[8,1,128]{2,0,1:T(8,128)S(1)}, f32[8,1,128]{2,0,1:T(8,128)S(1)}, u32[]{:S(2)}, u32[]{:S(2)}) collective-permute-start(f32[8,1,128]{2,0,1:T(8,128)S(1)} %bitcast.9), channel_id=1, source_target_pairs={{8,0},{16,8},{24,16},{32,24},{40,32},{48,40},{56,48},{64,56},{72,6... | collective-permute-start | bytes 12296 | tf_op jit(solution)/shard_map/ppermute | solution.py:31
  6.4 0.9 %copy-start.1 = (s32[384]{0:T(512)S(1)}, s32[384]{0:T(512)}, u32[]{:S(2)}) copy-start(s32[384]{0:T(512)} %lev.3) | copy-start | bytes 4612
  7.3 0.7 copy-start
  7.9 1.0 %copy-start.4 = (f32[8,128,128]{2,1,0:T(8,128)S(1)}, f32[8,128,128]{2,1,0:T(8,128)}, u32[]{:S(2)}) copy-start(f32[8,128,128]{2,1,0:T(8,128)} %param.7) | copy-start | bytes 1572868
  11.7 13.8 %all-to-all-start = ((f32[8,8,384]{2,1,0:T(8,128)}), f32[8,8,384]{2,1,0:T(8,128)S(1)}, u32[]{:S(2)}, u32[]{:S(2)}) async-start(f32[8,8,384]{2,1,0:T(8,128)} %get-tuple-element.17), calls=%async_computation | async-start | bytes 196608 | tf_op jit(solution)/shard_map/all_to_all | solution.py:362
  21.2 18.7 %collective-permute-start.2 = (bf16[8,16384]{1,0:T(8,128)(2,1)S(1)}, bf16[8,16384]{1,0:T(8,128)(2,1)S(1)}, u32[]{:S(2)}, u32[]{:S(2)}) collective-permute-start(bf16[8,16384]{1,0:T(8,128)(2,1)S(1)} %get-tuple-element.20), channel_id=1, source_target_pairs={{0,2},{1,3},{2,0},{3,1},{4,6},{5,7},{6,4},{7,5},{8,10},{9,11},{10,... | collective-permute-start | bytes 786440 | tf_op jit(solution)/shard_map/ppermute | solution.py:343
  23.2 2.3 %copy-start.2 = (f32[384]{0:T(512)S(1)}, f32[384]{0:T(512)}, u32[]{:S(2)}) copy-start(f32[384]{0:T(512)} %value.1) | copy-start | bytes 4612
  23.3 2.3 %copy-start.3 = (f32[384]{0:T(512)S(1)}, f32[384]{0:T(512)}, u32[]{:S(2)}) copy-start(f32[384]{0:T(512)} %var.1) | copy-start | bytes 4612
  26.7 23.2 %all-to-all-start.1 = ((f32[12,24,128]{2,1,0:T(8,128)}), f32[12,24,128]{2,1,0:T(8,128)S(1)}, u32[]{:S(2)}, u32[]{:S(2)}) async-start(f32[12,24,128]{2,1,0:T(8,128)} %gram.1), calls=%async_computation.1 | async-start | bytes 294912 | tf_op jit(solution)/shard_map/all_to_all | solution.py:371
  37.1 20.5 %collective-permute-start.3 = (bf16[8,16384]{1,0:T(8,128)(2,1)S(1)}, bf16[8,16384]{1,0:T(8,128)(2,1)S(1)}, u32[]{:S(2)}, u32[]{:S(2)}) collective-permute-start(bf16[8,16384]{1,0:T(8,128)(2,1)S(1)} %get-tuple-element.20), channel_id=1, source_target_pairs={{0,6},{1,7},{2,4},{3,5},{4,2},{5,3},{6,0},{7,1},{8,14},{9,15},{10,... | collective-permute-start | bytes 786440 | tf_op jit(solution)/shard_map/ppermute | solution.py:343
  39.9 17.7 %collective-permute-start.4 = (bf16[8,16384]{1,0:T(8,128)(2,1)S(1)}, bf16[8,16384]{1,0:T(8,128)(2,1)S(1)}, u32[]{:S(2)}, u32[]{:S(2)}) collective-permute-start(bf16[8,16384]{1,0:T(8,128)(2,1)S(1)} %collective-permute-done.2), channel_id=1, source_target_pairs={{0,6},{1,7},{2,4},{3,5},{4,2},{5,3},{6,0},{7,1},{8,14},{9,15},{10,... | collective-permute-start | bytes 786440 | tf_op jit(solution)/shard_map/ppermute | solution.py:343
  43.0 27.4 %collective-permute-start.5 = (bf16[16,16384]{1,0:T(8,128)(2,1)S(1)}, bf16[16,16384]{1,0:T(8,128)(2,1)S(1)}, u32[]{:S(2)}, u32[]{:S(2)}) collective-permute-start(bf16[16,16384]{1,0:T(8,128)(2,1)S(1)} %constant_dynamic-update-slice_fusion.refs_0_), channel_id=1, source_target_pairs={{0,1},{1,0},{2,3},{3,2},{4,5},{5,4},{6,7},{7,6},{8,9},{9,8},{10,11... | collective-permute-start | bytes 1572872 | tf_op jit(solution)/shard_map/ppermute | solution.py:343
  50.5 16.5 %all-to-all-start.2 = ((f32[8,40,128]{2,1,0:T(8,128)}), f32[8,40,128]{2,1,0:T(8,128)S(1)}, u32[]{:S(2)}, u32[]{:S(2)}) async-start(f32[8,40,128]{2,1,0:T(8,128)} %row_sum.1), calls=%async_computation.2 | async-start | bytes 327680 | tf_op jit(solution)/shard_map/all_to_all | solution.py:375
  57.6 12.8 %collective-permute-start.6 = (bf16[8,16384]{1,0:T(8,128)(2,1)S(1)}, bf16[8,16384]{1,0:T(8,128)(2,1)S(1)}, u32[]{:S(2)}, u32[]{:S(2)}) collective-permute-start(bf16[8,16384]{1,0:T(8,128)(2,1)S(1)} %collective-permute-done.3.refs_1_), channel_id=1, source_target_pairs={{0,1},{1,0},{2,3},{3,2},{4,5},{5,4},{6,7},{7,6},{8,9},{9,8},{10,11... | collective-permute-start | bytes 786440 | tf_op jit(solution)/shard_map/ppermute | solution.py:343
  59.5 10.9 %collective-permute-start.7 = (bf16[8,16384]{1,0:T(8,128)(2,1)S(1)}, bf16[8,16384]{1,0:T(8,128)(2,1)S(1)}, u32[]{:S(2)}, u32[]{:S(2)}) collective-permute-start(bf16[8,16384]{1,0:T(8,128)(2,1)S(1)} %collective-permute-done.4.refs_2_), channel_id=1, source_target_pairs={{0,1},{1,0},{2,3},{3,2},{4,5},{5,4},{6,7},{7,6},{8,9},{9,8},{10,11... | collective-permute-start | bytes 786440 | tf_op jit(solution)/shard_map/ppermute | solution.py:343

commit v8 on v6

--- a/solution.py
+++ b/solution.py
@@ -26,8 +26,8 @@
     forward = [(i, i + 1) for i in range(count - 1)]
     backward = [(target, source) for source, target in forward]
     last = block.shape[1] - 1
+    high = lax.ppermute(block[:, :1, :], axis, backward)
     low = lax.ppermute(block[:, last:, :], axis, forward)
-    high = lax.ppermute(block[:, :1, :], axis, backward)
     return low[:, 0], high[:, 0]
 
 

time: 72.5 us -> 72.5 us (level)
  no operation moved by 1% of the time
where the time goes in v8:
time: 72.5 us; the launch traced here: 71.7 us
  starting transfers between devices  46.7 us (64%)
  waiting for transfers between devices  13.1 us (18%)
  Pallas kernels  8.24 us (11%)
  local copies, waits for them, and re-layouts  2.55 us (4%)
  other arithmetic  0.89 us (1%)
    ppermute x6, starting transfers between devices, swapped(): lax.ppermute(block, 'mem', [(i, i ^ code) for i in range(lax.axis_size('m...  14.1 us
    all_to_all x1, starting transfers between devices, on_device(): parts = lax.all_to_all(parts, 'col', 0, 0)  10.4 us
    all_to_all x1, starting transfers between devices, on_device(): readings = lax.all_to_all(copies, 'mem', 0, 0)  9.47 us
    all_to_all x1, starting transfers between devices, on_device(): parts = lax.all_to_all(parts, 'row', 0, 0)  7.1 us
    all_to_all x1, waiting for transfers between devices, on_device(): parts = lax.all_to_all(parts, 'row', 0, 0)  5.07 us
    all_to_all x1, waiting for transfers between devices, on_device(): parts = lax.all_to_all(parts, 'col', 0, 0)  4.87 us
    ppermute x1, starting transfers between devices, neighbours(): low = lax.ppermute(block[:, last:, :], axis, forward)  4.26 us
    pallas_call x1, Pallas kernels, analysis(): pl.pallas_call(functools.partial(mix_kernel, members, NSITER, count), out...  3.4 us
  transfers between devices with their start and end apart: 11, of which 4 were waited for; matrix products, arithmetic and copies ran while one was open for 1% of the time, Pallas kernels for 9%

profile of v8, /device:TPU:2, one launch (start us, length us, event | category | flops | bytes accessed | tf_op | source)
XLA Modules:
  0.0 71.7 jit_solution(14685425420705672418)
XLA Ops:
  0.0 0.8 %fusion = (f32[8,1,128]{2,1,0:T(1,128)S(1)}, f32[8,1,128]{2,1,0:T(1,128)S(1)}) fusion(f32[8,128,128]{2,1,0:T(8,128)} %param.7), kind=kLoop, calls=%fused_computation.4 | loop fusion | bytes 16384 | tf_op jit(solution)/shard_map/slice | solution.py:29
  0.8 4.3 %collective-permute-start = (f32[8,1,128]{2,0,1:T(8,128)S(1)}, f32[8,1,128]{2,0,1:T(8,128)S(1)}, u32[]{:S(2)}, u32[]{:S(2)}) collective-permute-start(f32[8,1,128]{2,0,1:T(8,128)S(1)} %bitcast.10), channel_id=1, source_target_pairs={{0,8},{8,16},{16,24},{24,32},{32,40},{40,48},{48,56},{56,64},{64,7... | collective-permute-start | bytes 12296 | tf_op jit(solution)/shard_map/ppermute | solution.py:30
  5.1 1.3 %collective-permute-start.1 = (f32[8,1,128]{2,0,1:T(8,128)S(1)}, f32[8,1,128]{2,0,1:T(8,128)S(1)}, u32[]{:S(2)}, u32[]{:S(2)}) collective-permute-start(f32[8,1,128]{2,0,1:T(8,128)S(1)} %bitcast.9), channel_id=1, source_target_pairs={{8,0},{16,8},{24,16},{32,24},{40,32},{48,40},{56,48},{64,56},{72,6... | collective-permute-start | bytes 12296 | tf_op jit(solution)/shard_map/ppermute | solution.py:29
  6.4 0.0 copy-start.1
  6.4 0.9 %multiply_subtract_fusion = (f32[128,128]{1,0:T(8,128)S(1)}, f32[128,128]{1,0:T(8,128)S(1)}) fusion(f32[128,128]{1,0:T(8,128)} %param.9, f32[128,128]{1,0:T(8,128)} %param.8), kind=kLoop, calls=%fused_computation | loop fusion | flops 49152 | bytes 262144 | tf_op jit(solution)/shard_map/sub | solution.py:337
  7.3 0.0 copy-start
  7.3 0.7 copy-done
  7.9 1.0 %copy-done.4 = f32[8,128,128]{2,1,0:T(8,128)S(1)} copy-done((f32[8,128,128]{2,1,0:T(8,128)S(1)}, f32[8,128,128]{2,1,0:T(8,128)}, u32[]{:S(2)}) %copy-start.4) | copy-done | bytes 524312
  9.0 1.0 %inner_forecast.1 = (bf16[8,16384]{1,0:T(8,128)(2,1)S(1)}, f32[8,384]{1,0:T(8,128)S(1)}, f32[4,8,128]{2,1,0:T(8,128)S(1)}) custom-call(f32[1024,128]{1,0:T(8,128)S(1)} %bitcast.8, f32[128,128]{1,0:T(8,128)S(1)} %get-tuple-element.26.leftward, f32[128,128]{1,0:T(8,128)S(1)} %get-tuple-element.25.rightward, s32[384]{0:T(512)S(1)} %copy-done, s32[384]{0:T(512)S(1)} %copy-done.1), custom_call_target="tpu_custom_call" | custom-call | flops 301989888 | bytes 524288 | tf_op jit(solution)/shard_map/inner_forecast/pallas_call | solution.py:101
  10.0 0.0 collective-permute-done
  10.0 0.9 %collective-permute-done.1 = f32[8,1,128]{2,0,1:T(8,128)S(1)} collective-permute-done((f32[8,1,128]{2,0,1:T(8,128)S(1)}, f32[8,1,128]{2,0,1:T(8,128)S(1)}, u32[]{:S(2)}, u32[]{:S(2)}) %collective-permute-start.1) | collective-permute-done | bytes 4128 | tf_op jit(solution)/shard_map/ppermute | solution.py:29
  10.9 0.8 %edge_forecast.1 = (bf16[8,16384]{1,0:T(8,128)(2,1)S(1)}, f32[8,8,384]{2,1,0:T(8,128)}) custom-call(f32[4,8,128]{2,1,0:T(8,128)S(1)} %get-tuple-element.14.edges, f32[8,128]{1,0:T(8,128)S(1)} %bitcast.6, f32[8,128]{1,0:T(8,128)S(1)} %bitcast.7, f32[8,384]{1,0:T(8,128)S(1)} %get-tuple-element.15.readings, ...), custom_call_target="tpu_custom_call", output_to_operand_aliasing={{0}: (6, {})} | custom-call | tf_op jit(solution)/shard_map/edge_forecast/pallas_call | solution.py:140
  11.7 9.5 %all-to-all-start = ((f32[8,8,384]{2,1,0:T(8,128)}), f32[8,8,384]{2,1,0:T(8,128)S(1)}, u32[]{:S(2)}, u32[]{:S(2)}) async-start(f32[8,8,384]{2,1,0:T(8,128)} %get-tuple-element.17), calls=%async_computation | async-start | bytes 196608 | tf_op jit(solution)/shard_map/all_to_all | solution.py:344
  21.2 2.0 %collective-permute-start.2 = (bf16[8,16384]{1,0:T(8,128)(2,1)S(1)}, bf16[8,16384]{1,0:T(8,128)(2,1)S(1)}, u32[]{:S(2)}, u32[]{:S(2)}) collective-permute-start(bf16[8,16384]{1,0:T(8,128)(2,1)S(1)} %get-tuple-element.20), channel_id=1, source_target_pairs={{0,2},{1,3},{2,0},{3,1},{4,6},{5,7},{6,4},{7,5},{8,10},{9,11},{10,... | collective-permute-start | bytes 786440 | tf_op jit(solution)/shard_map/ppermute | solution.py:325
  23.2 0.0 copy-start.2
  23.3 0.0 copy-start.3
  23.3 2.3 %all-to-all-done.readings = f32[8,8,384]{2,1,0:T(8,128)S(1)} async-done(((f32[8,8,384]{2,1,0:T(8,128)}), f32[8,8,384]{2,1,0:T(8,128)S(1)}, u32[]{:S(2)}, u32[]{:S(2)}) %all-to-all-start) | async-done | bytes 98336 | tf_op jit(solution)/shard_map/all_to_all | solution.py:344
  25.6 1.1 %gram.1 = f32[12,24,128]{2,1,0:T(8,128)} custom-call(s32[1]{0:T(128)} %bitcast.me, f32[8,8,384]{2,1,0:T(8,128)S(1)} %all-to-all-done.readings, f32[384]{0:T(512)S(1)} %copy-done.2, f32[384]{0:T(512)S(1)} %copy-done.3), custom_call_target="tpu_custom_call" | custom-call | tf_op jit(solution)/shard_map/gram/pallas_call | solution.py:214
  26.7 10.4 %all-to-all-start.1 = ((f32[12,24,128]{2,1,0:T(8,128)}), f32[12,24,128]{2,1,0:T(8,128)S(1)}, u32[]{:S(2)}, u32[]{:S(2)}) async-start(f32[12,24,128]{2,1,0:T(8,128)} %gram.1), calls=%async_computation.1 | async-start | bytes 294912 | tf_op jit(solution)/shard_map/all_to_all | solution.py:353
  37.1 2.8 %collective-permute-start.3 = (bf16[8,16384]{1,0:T(8,128)(2,1)S(1)}, bf16[8,16384]{1,0:T(8,128)(2,1)S(1)}, u32[]{:S(2)}, u32[]{:S(2)}) collective-permute-start(bf16[8,16384]{1,0:T(8,128)(2,1)S(1)} %get-tuple-element.20), channel_id=1, source_target_pairs={{0,6},{1,7},{2,4},{3,5},{4,2},{5,3},{6,0},{7,1},{8,14},{9,15},{10,... | collective-permute-start | bytes 786440 | tf_op jit(solution)/shard_map/ppermute | solution.py:325
  39.9 3.0 %collective-permute-start.4 = (bf16[8,16384]{1,0:T(8,128)(2,1)S(1)}, bf16[8,16384]{1,0:T(8,128)(2,1)S(1)}, u32[]{:S(2)}, u32[]{:S(2)}) collective-permute-start(bf16[8,16384]{1,0:T(8,128)(2,1)S(1)} %collective-permute-done.2), channel_id=1, source_target_pairs={{0,6},{1,7},{2,4},{3,5},{4,2},{5,3},{6,0},{7,1},{8,14},{9,15},{10,... | collective-permute-start | bytes 786440 | tf_op jit(solution)/shard_map/ppermute | solution.py:325
  43.0 1.9 %collective-permute-start.5 = (bf16[16,16384]{1,0:T(8,128)(2,1)S(1)}, bf16[16,16384]{1,0:T(8,128)(2,1)S(1)}, u32[]{:S(2)}, u32[]{:S(2)}) collective-permute-start(bf16[16,16384]{1,0:T(8,128)(2,1)S(1)} %constant_dynamic-update-slice_fusion.refs_0_), channel_id=1, source_target_pairs={{0,1},{1,0},{2,3},{3,2},{4,5},{5,4},{6,7},{7,6},{8,9},{9,8},{10,11... | collective-permute-start | bytes 1572872 | tf_op jit(solution)/shard_map/ppermute | solution.py:325
  44.9 4.9 %all-to-all-done.1.parts = f32[12,24,128]{2,1,0:T(8,128)S(1)} async-done(((f32[12,24,128]{2,1,0:T(8,128)}), f32[12,24,128]{2,1,0:T(8,128)S(1)}, u32[]{:S(2)}, u32[]{:S(2)}) %all-to-all-start.1) | async-done | bytes 147488 | tf_op jit(solution)/shard_map/all_to_all | solution.py:353
  49.8 0.7 row_sum.1
  50.5 7.1 %all-to-all-start.2 = ((f32[8,40,128]{2,1,0:T(8,128)}), f32[8,40,128]{2,1,0:T(8,128)S(1)}, u32[]{:S(2)}, u32[]{:S(2)}) async-start(f32[8,40,128]{2,1,0:T(8,128)} %row_sum.1), calls=%async_computation.2 | async-start | bytes 327680 | tf_op jit(solution)/shard_map/all_to_all | solution.py:357
  57.6 0.0 collective-permute-done.4.refs_2_
  57.6 1.9 %collective-permute-start.6 = (bf16[8,16384]{1,0:T(8,128)(2,1)S(1)}, bf16[8,16384]{1,0:T(8,128)(2,1)S(1)}, u32[]{:S(2)}, u32[]{:S(2)}) collective-permute-start(bf16[8,16384]{1,0:T(8,128)(2,1)S(1)} %collective-permute-done.3.refs_1_), channel_id=1, source_target_pairs={{0,1},{1,0},{2,3},{3,2},{4,5},{5,4},{6,7},{7,6},{8,9},{9,8},{10,11... | collective-permute-start | bytes 786440 | tf_op jit(solution)/shard_map/ppermute | solution.py:325
  59.5 2.4 %collective-permute-start.7 = (bf16[8,16384]{1,0:T(8,128)(2,1)S(1)}, bf16[8,16384]{1,0:T(8,128)(2,1)S(1)}, u32[]{:S(2)}, u32[]{:S(2)}) collective-permute-start(bf16[8,16384]{1,0:T(8,128)(2,1)S(1)} %collective-permute-done.4.refs_2_), channel_id=1, source_target_pairs={{0,1},{1,0},{2,3},{3,2},{4,5},{5,4},{6,7},{7,6},{8,9},{9,8},{10,11... | collective-permute-start | bytes 786440 | tf_op jit(solution)/shard_map/ppermute | solution.py:325
  62.0 5.1 %all-to-all-done.2.parts = f32[8,40,128]{2,1,0:T(8,128)S(1)} async-done(((f32[8,40,128]{2,1,0:T(8,128)}), f32[8,40,128]{2,1,0:T(8,128)S(1)}, u32[]{:S(2)}, u32[]{:S(2)}) %all-to-all-start.2) | async-done | bytes 163872 | tf_op jit(solution)/shard_map/all_to_all | solution.py:357
  67.0 3.4 %mix.1 = bf16[8,64]{1,0:T(8,128)(2,1)S(1)} custom-call(f32[8,40,128]{2,1,0:T(8,128)S(1)} %all-to-all-done.2.parts), custom_call_target="tpu_custom_call" | custom-call | tf_op jit(solution)/shard_map/mix/pallas_call | solution.py:305
  70.4 0.0 collective-permute-done.5.refs_3_
  70.5 1.3 %analysis.1 = bf16[8,128,128]{2,1,0:T(8,128)(2,1)} custom-call(bf16[8,64]{1,0:T(8,128)(2,1)S(1)} %mix.1, bf16[16,16384]{1,0:T(8,128)(2,1)S(1)} %constant_dynamic-update-slice_fusion.refs_0_, bf16[8,16384]{1,0:T(8,128)(2,1)S(1)} %collective-permute-done.3.refs_1_, bf16[8,16384]{1,0:T(8,128)(2,1)S(1)} %collective-permute-done.4.refs_2_, ...), custom_call_target="tpu_custom_call" | custom-call | tf_op jit(solution)/shard_map/analysis/pallas_call | solution.py:313
  (10 shorter events, 0.1 us)
Async XLA Ops:
  0.8 9.2 %collective-permute-start = (f32[8,1,128]{2,0,1:T(8,128)S(1)}, f32[8,1,128]{2,0,1:T(8,128)S(1)}, u32[]{:S(2)}, u32[]{:S(2)}) collective-permute-start(f32[8,1,128]{2,0,1:T(8,128)S(1)} %bitcast.10), channel_id=1, source_target_pairs={{0,8},{8,16},{16,24},{24,32},{32,40},{40,48},{48,56},{56,64},{64,7... | collective-permute-start | bytes 12296 | tf_op jit(solution)/shard_map/ppermute | solution.py:30
  5.1 5.9 %collective-permute-start.1 = (f32[8,1,128]{2,0,1:T(8,128)S(1)}, f32[8,1,128]{2,0,1:T(8,128)S(1)}, u32[]{:S(2)}, u32[]{:S(2)}) collective-permute-start(f32[8,1,128]{2,0,1:T(8,128)S(1)} %bitcast.9), channel_id=1, source_target_pairs={{8,0},{16,8},{24,16},{32,24},{40,32},{48,40},{56,48},{64,56},{72,6... | collective-permute-start | bytes 12296 | tf_op jit(solution)/shard_map/ppermute | solution.py:29
  6.4 0.9 %copy-start.1 = (s32[384]{0:T(512)S(1)}, s32[384]{0:T(512)}, u32[]{:S(2)}) copy-start(s32[384]{0:T(512)} %lev.3) | copy-start | bytes 4612
  7.3 0.7 copy-start
  7.9 1.0 %copy-start.4 = (f32[8,128,128]{2,1,0:T(8,128)S(1)}, f32[8,128,128]{2,1,0:T(8,128)}, u32[]{:S(2)}) copy-start(f32[8,128,128]{2,1,0:T(8,128)} %param.7) | copy-start | bytes 1572868
  11.7 13.8 %all-to-all-start = ((f32[8,8,384]{2,1,0:T(8,128)}), f32[8,8,384]{2,1,0:T(8,128)S(1)}, u32[]{:S(2)}, u32[]{:S(2)}) async-start(f32[8,8,384]{2,1,0:T(8,128)} %get-tuple-element.17), calls=%async_computation | async-start | bytes 196608 | tf_op jit(solution)/shard_map/all_to_all | solution.py:344
  21.2 18.7 %collective-permute-start.2 = (bf16[8,16384]{1,0:T(8,128)(2,1)S(1)}, bf16[8,16384]{1,0:T(8,128)(2,1)S(1)}, u32[]{:S(2)}, u32[]{:S(2)}) collective-permute-start(bf16[8,16384]{1,0:T(8,128)(2,1)S(1)} %get-tuple-element.20), channel_id=1, source_target_pairs={{0,2},{1,3},{2,0},{3,1},{4,6},{5,7},{6,4},{7,5},{8,10},{9,11},{10,... | collective-permute-start | bytes 786440 | tf_op jit(solution)/shard_map/ppermute | solution.py:325
  23.2 2.3 %copy-start.2 = (f32[384]{0:T(512)S(1)}, f32[384]{0:T(512)}, u32[]{:S(2)}) copy-start(f32[384]{0:T(512)} %value.1) | copy-start | bytes 4612
  23.3 2.3 %copy-start.3 = (f32[384]{0:T(512)S(1)}, f32[384]{0:T(512)}, u32[]{:S(2)}) copy-start(f32[384]{0:T(512)} %var.1) | copy-start | bytes 4612
  26.7 23.2 %all-to-all-start.1 = ((f32[12,24,128]{2,1,0:T(8,128)}), f32[12,24,128]{2,1,0:T(8,128)S(1)}, u32[]{:S(2)}, u32[]{:S(2)}) async-start(f32[12,24,128]{2,1,0:T(8,128)} %gram.1), calls=%async_computation.1 | async-start | bytes 294912 | tf_op jit(solution)/shard_map/all_to_all | solution.py:353
  37.1 20.5 %collective-permute-start.3 = (bf16[8,16384]{1,0:T(8,128)(2,1)S(1)}, bf16[8,16384]{1,0:T(8,128)(2,1)S(1)}, u32[]{:S(2)}, u32[]{:S(2)}) collective-permute-start(bf16[8,16384]{1,0:T(8,128)(2,1)S(1)} %get-tuple-element.20), channel_id=1, source_target_pairs={{0,6},{1,7},{2,4},{3,5},{4,2},{5,3},{6,0},{7,1},{8,14},{9,15},{10,... | collective-permute-start | bytes 786440 | tf_op jit(solution)/shard_map/ppermute | solution.py:325
  39.9 17.7 %collective-permute-start.4 = (bf16[8,16384]{1,0:T(8,128)(2,1)S(1)}, bf16[8,16384]{1,0:T(8,128)(2,1)S(1)}, u32[]{:S(2)}, u32[]{:S(2)}) collective-permute-start(bf16[8,16384]{1,0:T(8,128)(2,1)S(1)} %collective-permute-done.2), channel_id=1, source_target_pairs={{0,6},{1,7},{2,4},{3,5},{4,2},{5,3},{6,0},{7,1},{8,14},{9,15},{10,... | collective-permute-start | bytes 786440 | tf_op jit(solution)/shard_map/ppermute | solution.py:325
  43.0 27.4 %collective-permute-start.5 = (bf16[16,16384]{1,0:T(8,128)(2,1)S(1)}, bf16[16,16384]{1,0:T(8,128)(2,1)S(1)}, u32[]{:S(2)}, u32[]{:S(2)}) collective-permute-start(bf16[16,16384]{1,0:T(8,128)(2,1)S(1)} %constant_dynamic-update-slice_fusion.refs_0_), channel_id=1, source_target_pairs={{0,1},{1,0},{2,3},{3,2},{4,5},{5,4},{6,7},{7,6},{8,9},{9,8},{10,11... | collective-permute-start | bytes 1572872 | tf_op jit(solution)/shard_map/ppermute | solution.py:325
  50.5 16.5 %all-to-all-start.2 = ((f32[8,40,128]{2,1,0:T(8,128)}), f32[8,40,128]{2,1,0:T(8,128)S(1)}, u32[]{:S(2)}, u32[]{:S(2)}) async-start(f32[8,40,128]{2,1,0:T(8,128)} %row_sum.1), calls=%async_computation.2 | async-start | bytes 327680 | tf_op jit(solution)/shard_map/all_to_all | solution.py:357
  57.6 12.8 %collective-permute-start.6 = (bf16[8,16384]{1,0:T(8,128)(2,1)S(1)}, bf16[8,16384]{1,0:T(8,128)(2,1)S(1)}, u32[]{:S(2)}, u32[]{:S(2)}) collective-permute-start(bf16[8,16384]{1,0:T(8,128)(2,1)S(1)} %collective-permute-done.3.refs_1_), channel_id=1, source_target_pairs={{0,1},{1,0},{2,3},{3,2},{4,5},{5,4},{6,7},{7,6},{8,9},{9,8},{10,11... | collective-permute-start | bytes 786440 | tf_op jit(solution)/shard_map/ppermute | solution.py:325
  59.5 10.9 %collective-permute-start.7 = (bf16[8,16384]{1,0:T(8,128)(2,1)S(1)}, bf16[8,16384]{1,0:T(8,128)(2,1)S(1)}, u32[]{:S(2)}, u32[]{:S(2)}) collective-permute-start(bf16[8,16384]{1,0:T(8,128)(2,1)S(1)} %collective-permute-done.4.refs_2_), channel_id=1, source_target_pairs={{0,1},{1,0},{2,3},{3,2},{4,5},{5,4},{6,7},{7,6},{8,9},{9,8},{10,11... | collective-permute-start | bytes 786440 | tf_op jit(solution)/shard_map/ppermute | solution.py:325
